TPU v7x, 32 devices: a whole 2x2x4 slice. The times are simulated.
32 devices in a mesh: segment: 4 (over z), row: 2 (over x), col: 4 (over y, core).
Axes of the slice: x: 2, y: 2, z: 4, core: 2. Of those that a mesh axis runs over, the one named last changes fastest.
Arguments:
- saved_inputs: bfloat16 [4, 1, 32, 64, 256], P('segment', None, 'row', 'col'), may hold values from -6 to 6
- out_grad: bfloat16 [1, 32, 64, 256], P(None, 'row', 'col'), may hold values from -6 to 6
- tissue: int32 [1, 2, 4], P(None, 'row', 'col'), may hold values 0 or 1
- conv_taps: float32 [4, 7, 7, 256], P('segment'), may hold values from -0.875 to 0.875
- conv_bias: float32 [4, 256], P('segment'), may hold values from -3 to 3
- norm_gain: float32 [4, 256], P('segment'), may hold values from 0.1 to 1.9
- norm_bias: float32 [4, 256], P('segment'), may hold values from -3 to 3
- w_in: bfloat16 [4, 256, 1024], P('segment'), may hold values from -0.375 to 0.375
- b_in: float32 [4, 1024], P('segment'), may hold values from -3 to 3
- w_out: bfloat16 [4, 1024, 256], P('segment'), may hold values from -0.1875 to 0.1875
- layer_scale: float32 [4, 256], P('segment'), may hold values from 0.3 to 1.5
Outputs:
- section_grads: bfloat16 [4, 1, 32, 64, 256], P('segment', None, 'row', 'col')
- grad_w_in: float32 [4, 256, 1024], P('segment', 'col')
- grad_w_out: float32 [4, 1024, 256], P('segment', 'col')
- grad_taps: float32 [4, 7, 7, 256], P('segment')
Inputs may be any that keep to these rules, and one draw needn't show every extreme that they name: 1 marks a tile that holds tissue, 0 an empty one.
All inputs are finite; a program needn't handle non-finite values. No bound on the sum of `tissue` on one device may be relied on, other than what follows from the above.
Results may differ from a plain program's by a relative error of at most 0.013.
Values may be sent and summed in bfloat16 or wider, within the bound.
No kernel may reach another device: no remote copies, remote signals or barrier semaphores. Data moves between devices by JAX's collectives and lax.ppermute only.
A program may use at most 128 MiB of HBM per device.

v0:
```python
import math

import jax
import jax.numpy as jnp
from jax import lax
from jax.sharding import PartitionSpec as P

epsilon = 1e-06


def with_halo(block, sides, width):
    for axis, dim in sides:
        count = lax.axis_size(axis)
        forward = [(i, i + 1) for i in range(count - 1)]
        backward = [(target, source) for source, target in forward]
        low = lax.ppermute(
            lax.slice_in_dim(block, block.shape[dim] - width, None, axis=dim), axis, forward
        )
        high = lax.ppermute(lax.slice_in_dim(block, 0, width, axis=dim), axis, backward)
        block = jnp.concatenate([low, block, high], axis=dim)
    return block


def shifted(block, axis, distance):
    devices = range(lax.axis_size(axis))
    route = [(i - distance, i) for i in devices if i - distance in devices]
    return lax.ppermute(block, axis, route)


def depthwise(padded, conv_taps, height, across):
    side = conv_taps.shape[0]
    total = jnp.zeros((height, across, padded.shape[-1]), jnp.float32)
    for shift_r in range(side):
        for shift_c in range(side):
            total = total + conv_taps[shift_r, shift_c] * padded[
                shift_r : shift_r + height, shift_c : shift_c + across
            ].astype(jnp.float32)
    return total


def transposed(padded_grad, conv_taps, height, across):
    side = conv_taps.shape[0]
    margin = side // 2
    total = jnp.zeros((height, across, padded_grad.shape[-1]), jnp.float32)
    for shift_r in range(side):
        for shift_c in range(side):
            start_r = 2 * margin - shift_r
            start_c = 2 * margin - shift_c
            total = total + conv_taps[shift_r, shift_c] * padded_grad[
                start_r : start_r + height, start_c : start_c + across
            ].astype(jnp.float32)
    return total


def kernel_grad(padded, grad, side, height, across):
    grad_wide = grad.astype(jnp.float32)
    pieces = []
    for shift_r in range(side):
        for shift_c in range(side):
            window = padded[shift_r : shift_r + height, shift_c : shift_c + across].astype(
                jnp.float32
            )
            pieces.append(jnp.sum(window * grad_wide, axis=(0, 1)))
    return jnp.stack(pieces).reshape(side, side, -1)


def normalize(conv_out, norm_gain, norm_bias):
    average = jnp.mean(conv_out, axis=-1, keepdims=True)
    centred = conv_out - average
    spread = jnp.mean(centred * centred, axis=-1, keepdims=True)
    inv_std = lax.rsqrt(spread + epsilon)
    standard = centred * inv_std
    normed = (standard * norm_gain + norm_bias).astype(jnp.bfloat16)
    return (standard, inv_std, normed)


def mlp_back(normed, branch_grad, norm_gain, w_in, b_in, w_out):
    pre_gate = jnp.dot(normed, w_in, preferred_element_type=jnp.float32) + b_in
    gated, gelu_back = jax.vjp(jax.nn.gelu, pre_gate)
    hidden = gated.astype(jnp.bfloat16)
    grad_out = jnp.dot(hidden.T, branch_grad, preferred_element_type=jnp.float32)
    hidden_grad = jnp.dot(branch_grad, w_out.T, preferred_element_type=jnp.float32)
    pre_grad = gelu_back(hidden_grad)[0].astype(jnp.bfloat16)
    grad_in = jnp.dot(normed.T, pre_grad, preferred_element_type=jnp.float32)
    norm_grad = jnp.dot(pre_grad, w_in.T, preferred_element_type=jnp.float32) * norm_gain
    return (norm_grad, grad_in, grad_out)


def finish_norm(norm_grad, standard, inv_std):
    conv_grad = inv_std * (
        norm_grad
        - jnp.mean(norm_grad, axis=-1, keepdims=True)
        - standard * jnp.mean(norm_grad * standard, axis=-1, keepdims=True)
    )
    return conv_grad.astype(jnp.bfloat16)


def pixel_grad(conv_out, upstream, gate, norm_gain, norm_bias, w_in, b_in, w_out, layer_scale):
    standard, inv_std, normed = normalize(conv_out, norm_gain, norm_bias)
    branch_grad = (gate * layer_scale * upstream.astype(jnp.float32)).astype(jnp.bfloat16)
    norm_grad, grad_in, grad_out = mlp_back(normed, branch_grad, norm_gain, w_in, b_in, w_out)
    return (finish_norm(norm_grad, standard, inv_std), grad_in, grad_out)


def per_device(
    saved_inputs,
    out_grad,
    tissue,
    conv_taps,
    conv_bias,
    norm_gain,
    norm_bias,
    w_in,
    b_in,
    w_out,
    layer_scale,
):
    segments = lax.axis_size("segment")
    section = lax.axis_index("segment")
    col_count = lax.axis_size("col")
    crop_count, height, across, channels = out_grad.shape
    tiles_r = tissue.shape[1]
    tiles_c = tissue.shape[2]
    tile_side = height // tiles_r
    hidden_units = w_in.shape[2]
    taps = conv_taps[0]
    side = taps.shape[0]
    margin = side // 2
    bias_conv = conv_bias[0]
    gain_norm = norm_gain[0]
    bias_norm = norm_bias[0]
    weight_in = w_in[0]
    bias_in = b_in[0]
    weight_out = w_out[0]
    scale_layer = layer_scale[0]
    pixel_total = crop_count * height * across * lax.axis_size("row") * col_count
    norm_scale = 1.0 / math.sqrt(pixel_total)
    saved_pad = with_halo(saved_inputs[0], (("row", 1), ("col", 2)), margin)

    def zero_grads(pixels):
        return (
            jnp.zeros((pixels, channels), jnp.bfloat16),
            jnp.zeros((channels, hidden_units), jnp.float32),
            jnp.zeros((hidden_units, channels), jnp.float32),
        )

    def advance(step_index, loop_state):
        incoming, collected, sum_in, sum_out, sum_taps = loop_state
        crop_index = step_index - (segments - 1 - section)
        active = jnp.logical_and(crop_index >= 0, crop_index < crop_count)
        crop_index = jnp.clip(crop_index, 0, crop_count - 1)
        own_grad = lax.dynamic_index_in_dim(out_grad, crop_index, 0, keepdims=False)
        upstream = jnp.where(section == segments - 1, own_grad, incoming)
        saved_tile = lax.dynamic_index_in_dim(saved_pad, crop_index, 0, keepdims=False)
        conv_out = depthwise(saved_tile, taps, height, across) + bias_conv
        tile_marks = lax.dynamic_index_in_dim(tissue, crop_index, 0, keepdims=False)
        pixel_mask = jnp.broadcast_to(
            tile_marks.astype(jnp.float32)[:, None, :, None],
            (tiles_r, tile_side, tiles_c, tile_side),
        ).reshape(height * across, 1)

        def worked():
            return pixel_grad(
                conv_out.reshape(-1, channels),
                upstream.reshape(-1, channels),
                pixel_mask,
                gain_norm,
                bias_norm,
                weight_in,
                bias_in,
                weight_out,
                scale_layer,
            )

        def skipped():
            return zero_grads(height * across)

        grad_rows, add_in, add_out = lax.cond(active, worked, skipped)
        conv_grad = grad_rows.reshape(height, across, channels)
        sum_in = sum_in + add_in
        sum_out = sum_out + add_out
        sum_taps = sum_taps + kernel_grad(saved_tile, conv_grad, side, height, across)
        padded_grad = with_halo(conv_grad, (("row", 0), ("col", 1)), margin)
        input_grad = (
            upstream.astype(jnp.float32) + transposed(padded_grad, taps, height, across)
        ).astype(jnp.bfloat16)
        updated = lax.dynamic_update_index_in_dim(collected, input_grad, crop_index, 0)
        collected = jnp.where(active, updated, collected)
        passed = shifted(input_grad, "segment", -1)
        return (passed, collected, sum_in, sum_out, sum_taps)

    initial = (
        jnp.zeros((height, across, channels), jnp.bfloat16),
        jnp.zeros((crop_count, height, across, channels), jnp.bfloat16),
        jnp.zeros((channels, hidden_units), jnp.float32),
        jnp.zeros((hidden_units, channels), jnp.float32),
        jnp.zeros((side, side, channels), jnp.float32),
    )
    final_state = lax.fori_loop(0, crop_count + segments - 1, advance, initial)
    collected = final_state[1]
    sum_in = final_state[2]
    sum_out = final_state[3]
    sum_taps = final_state[4]
    summed_in, summed_out, summed_taps = lax.psum((sum_in, sum_out, sum_taps), ("row", "col"))
    column = lax.axis_index("col")
    share_in = lax.dynamic_slice_in_dim(
        summed_in, column * (channels // col_count), channels // col_count, 0
    )
    share_out = lax.dynamic_slice_in_dim(
        summed_out, column * (hidden_units // col_count), hidden_units // col_count, 0
    )
    return (
        collected[None],
        (share_in * norm_scale)[None],
        (share_out * norm_scale)[None],
        (summed_taps * norm_scale)[None],
    )


def solution(mesh):
    return jax.shard_map(
        per_device,
        mesh=mesh,
        in_specs=(
            P("segment", None, "row", "col", None),
            P(None, "row", "col", None),
            P(None, "row", "col"),
            P("segment", None, None, None),
            P("segment", None),
            P("segment", None),
            P("segment", None),
            P("segment", None, None),
            P("segment", None),
            P("segment", None, None),
            P("segment", None),
        ),
        out_specs=(
            P("segment", None, "row", "col", None),
            P("segment", "col", None),
            P("segment", "col", None),
            P("segment", None, None, None),
        ),
        check_vma=False,
    )
```

profile of v0, /device:TPU:18, one launch (start us, length us, event | category | flops | bytes accessed | tf_op | source)
XLA Modules:
  0.0 497.5 jit_solution(773248885445245206)
XLA Ops:
  9.3 4.5 collective-permute-start.6
  20.3 2.2 collective-permute-done.8
  23.6 384.1 %while.24 = (s32[]{:T(128)}, bf16[16,16,256]{2,1,0:T(8,128)(2,1)S(1)}, bf16[1,16,16,256]{3,2,1,0:T(8,128)(2,1)}, f32[256,1024]{1,0:T(8,128)S(1)}, f32[1024,256]{...) while((s32[]{:T(128)}, ...), condition=%wide.region_56.57_spmd.clone, body=%wide.region_0.56_spmd.clone.sunk | while | flops 713714432 | bytes 112942032 | solution.py:199
  23.6 2.3 slice_convert_fusion.53
  25.9 2.3 slice_convert_fusion.54
  30.6 1.7 fusion.118
  32.3 1.7 slice_convert_fusion.52
  78.1 4.8 collective-permute-start
  91.7 4.5 collective-permute-start.3
  99.7 3.1 bitcast_select_fusion.3
  102.9 2.5 collective-permute-start.4
  105.4 16.8 %collective-permute-done.4 = bf16[16,16,256]{2,1,0:T(8,128)(2,1)S(1)} collective-permute-done((bf16[16,16,256]{2,1,0:T(8,128)(2,1)S(1)}, bf16[16,16,256]{2,1,0:T(8,128)(2,1)S(1)}, u32[]{:S(2)}, u32[]{:S(2)}) %collective-permute-start.4) | collective-permute-done | bytes 131104 | tf_op jit(solution)/shard_map/while/body/eval_jaxpr/ppermute | solution.py:27
  122.2 2.3 slice_convert_fusion.53
  124.5 2.3 slice_convert_fusion.54
  129.2 1.7 fusion.118
  130.9 1.7 slice_convert_fusion.52
  174.2 13.9 %conditional.3 = (bf16[256,256]{0,1:T(8,128)(2,1)}, f32[256,1024]{1,0:T(8,128)S(1)}, f32[1024,256]{1,0:T(8,128)S(1)}) conditional(s32[]{:T(128)} %convert_element_type.1669, () %tuple.232, (f32[16,16,256]{2,1,0:T(8,128)}, f32[16,16,256]{2,1,0:T(8,128)}, f32[256]{0:T(256)S(1)}, f32[16,16,256]{2,1,0:T(8,128)}, f32[16,16,256]{2,1,0:T(8,128)}, ...), branch_computations={%region_1.1_spmd, %region_2.6_spmd} | conditional | flops 687342080 | bytes 42378324 | solution.py:178
  174.2 8.7 %fusion.97 = (f32[16,16]{1,0:T(8,128)S(1)}, f32[16,16,256]{2,1,0:T(8,128)S(1)}) fusion(f32[256]{0:T(256)S(1)} %bitcast.550, f32[16,16,256]{2,1,0:T(8,128)} %get-tuple-element.800, f32[16,16,256]{2,1,0:T(8,128)} %get-tuple-element.801, f32[16,16,256]{2,1,0:T(8,128)} %get-tuple-element.798, f32[16,16,256]{2,1,0:T(8,128)} %get-tuple-element.799, ...), kind=kLoop, calls=%fused_computation.242 | loop fusion | flops 6487808 | bytes 25693184 | tf_op jit(solution)/shard_map/while/body/eval_jaxpr/cond/branch_1_fun/reduce_sum | solution.py:68
  189.8 5.5 %collective-permute-start = (bf16[3,16,256]{2,1,0:T(8,128)(2,1)}, bf16[3,16,256]{2,1,0:T(8,128)(2,1)}, u32[]{:S(2)}, u32[]{:S(2)}) collective-permute-start(bf16[3,16,256]{2,1,0:T(8,128)(2,1)} %bitcast.412), channel_id=1, source_target_pairs={{4,0},{5,1},{6,2},{7,3},{12,8},{13,9},{14,10},{15,11},{20,16},{21,... | collective-permute-start | bytes 73736 | tf_op jit(solution)/shard_map/while/body/eval_jaxpr/ppermute | solution.py:19
  199.7 2.5 select_add_fusion.7
  204.8 3.1 collective-permute-start.3
  211.4 3.1 bitcast_select_fusion.3
  214.6 2.1 collective-permute-start.4
  216.7 4.9 collective-permute-done.4
  221.6 2.3 slice_convert_fusion.53
  223.9 2.3 slice_convert_fusion.54
  228.6 1.7 fusion.118
  230.3 1.7 slice_convert_fusion.52
  276.1 5.6 %collective-permute-start = (bf16[3,16,256]{2,1,0:T(8,128)(2,1)}, bf16[3,16,256]{2,1,0:T(8,128)(2,1)}, u32[]{:S(2)}, u32[]{:S(2)}) collective-permute-start(bf16[3,16,256]{2,1,0:T(8,128)(2,1)} %bitcast.412), channel_id=1, source_target_pairs={{4,0},{5,1},{6,2},{7,3},{12,8},{13,9},{14,10},{15,11},{20,16},{21,... | collective-permute-start | bytes 73736 | tf_op jit(solution)/shard_map/while/body/eval_jaxpr/ppermute | solution.py:19
  286.2 2.5 select_add_fusion.7
  291.3 3.9 collective-permute-start.3
  298.7 3.1 bitcast_select_fusion.3
  301.8 15.4 %collective-permute-start.4 = (bf16[16,16,256]{2,1,0:T(8,128)(2,1)S(1)}, bf16[16,16,256]{2,1,0:T(8,128)(2,1)S(1)}, u32[]{:S(2)}, u32[]{:S(2)}) collective-permute-start(bf16[16,16,256]{2,1,0:T(8,128)(2,1)S(1)} %get-tuple-element.1605), channel_id=1, source_target_pairs={{8,0},{16,8},{24,16},{9,1},{17,9},{25,17},{10,2},{18,10},{26,18},{... | collective-permute-start | bytes 393224 | tf_op jit(solution)/shard_map/while/body/eval_jaxpr/ppermute | solution.py:27
  317.3 2.5 collective-permute-done.4
  319.8 2.3 slice_convert_fusion.53
  322.0 2.3 slice_convert_fusion.54
  326.7 1.7 fusion.118
  328.4 1.7 slice_convert_fusion.52
  374.2 5.5 %collective-permute-start = (bf16[3,16,256]{2,1,0:T(8,128)(2,1)}, bf16[3,16,256]{2,1,0:T(8,128)(2,1)}, u32[]{:S(2)}, u32[]{:S(2)}) collective-permute-start(bf16[3,16,256]{2,1,0:T(8,128)(2,1)} %bitcast.412), channel_id=1, source_target_pairs={{4,0},{5,1},{6,2},{7,3},{12,8},{13,9},{14,10},{15,11},{20,16},{21,... | collective-permute-start | bytes 73736 | tf_op jit(solution)/shard_map/while/body/eval_jaxpr/ppermute | solution.py:19
  384.1 2.5 select_add_fusion.7
  389.3 4.8 collective-permute-start.3
  397.5 3.1 bitcast_select_fusion.3
  400.7 4.2 collective-permute-start.4
  404.9 2.7 collective-permute-done.4
  408.7 27.9 %psum.23 = f32[7,7,256]{2,1,0:T(8,128)S(1)} all-reduce(f32[7,7,256]{2,1,0:T(8,128)S(1)} %copy-done.23), channel_id=1, replica_groups=mesh['segment'=4,'row'=2,'col'=4] {'row','col'}, use_global_device_ids=true, to_apply=%region_59.60 | all-reduce | flops 12544 | bytes 100352 | tf_op jit(solution)/shard_map/psum | solution.py:204
  437.3 50.0 %all-reduce.3.cloned.1.call-done = (f32[256,1024]{1,0:T(8,128)}, f32[1024,256]{1,0:T(8,128)}) async-done(((f32[256,1024]{1,0:T(8,128)}, f32[1024,256]{1,0:T(8,128)}), (f32[256,1024]{1,0:T(8,128)}, f32[1024,256]{1,0:T(8,128)})) %all-reduce.3.cloned.1.call-update) | async-done | bytes 2097168 | tf_op jit(solution)/shard_map/psum | solution.py:204
  487.3 1.7 multiply_bitcast_fusion
  489.0 1.7 multiply_bitcast_fusion.1
  (1281 shorter events, 242.4 us)
Async XLA Ops:
  7.2 480.1 %all-reduce.3.cloned.1.call-start = ((), (), s32[]{:S(2)}) async-start(), calls=%async_computation | async-start | bytes 4194304 | tf_op jit(solution)/shard_map/psum | solution.py:204
  8.0 5.8 %collective-permute-start.5 = (bf16[1,3,16,256]{3,2,1,0:T(8,128)(2,1)S(1)}, bf16[1,3,16,256]{3,2,1,0:T(8,128)(2,1)S(1)}, u32[]{:S(2)}, u32[]{:S(2)}) collective-permute-start(bf16[1,3,16,256]{3,2,1,0:T(8,128)(2,1)S(1)} %get-tuple-element.1223), channel_id=1, source_target_pairs={{0,4},{1,5},{2,6},{3,7},{8,12},{9,13},{10,14},{11,15},{16,20},{17,... | collective-permute-start | bytes 73736 | tf_op jit(solution)/shard_map/ppermute | solution.py:16
  9.3 6.1 %collective-permute-start.6 = (bf16[1,3,16,256]{3,2,1,0:T(8,128)(2,1)S(1)}, bf16[1,3,16,256]{3,2,1,0:T(8,128)(2,1)S(1)}, u32[]{:S(2)}, u32[]{:S(2)}) collective-permute-start(bf16[1,3,16,256]{3,2,1,0:T(8,128)(2,1)S(1)} %get-tuple-element.1224), channel_id=1, source_target_pairs={{4,0},{5,1},{6,2},{7,3},{12,8},{13,9},{14,10},{15,11},{20,16},{21,... | collective-permute-start | bytes 73736 | tf_op jit(solution)/shard_map/ppermute | solution.py:19
  16.2 4.1 collective-permute-start.7
  17.7 4.9 collective-permute-start.8
  30.6 29.2 %copy-start.63 = (f32[1,1,256]{2,1,0:T(1,128)}, f32[1,1,256]{2,1,0:T(1,128)S(1)}, u32[]{:S(2)}) copy-start(f32[1,1,256]{2,1,0:T(1,128)S(1)} %get-tuple-element.1591) | copy-start | bytes 3076 | tf_op jit(solution)/shard_map/while
  30.6 29.9 %copy-start.61 = (f32[1,1,256]{2,1,0:T(1,128)}, f32[1,1,256]{2,1,0:T(1,128)S(1)}, u32[]{:S(2)}) copy-start(f32[1,1,256]{2,1,0:T(1,128)S(1)} %get-tuple-element.1593) | copy-start | bytes 3076 | tf_op jit(solution)/shard_map/while
  30.6 30.7 %copy-start.59 = (f32[1,1,256]{2,1,0:T(1,128)}, f32[1,1,256]{2,1,0:T(1,128)S(1)}, u32[]{:S(2)}) copy-start(f32[1,1,256]{2,1,0:T(1,128)S(1)} %get-tuple-element.1595) | copy-start | bytes 3076 | tf_op jit(solution)/shard_map/while
  32.2 41.1 %copy-start.99 = (f32[1,1,256]{2,1,0:T(1,128)}, f32[1,1,256]{2,1,0:T(1,128)S(1)}, u32[]{:S(2)}) copy-start(f32[1,1,256]{2,1,0:T(1,128)S(1)} %get-tuple-element.1517) | copy-start | bytes 3076 | tf_op jit(solution)/shard_map/while
  32.3 41.9 %copy-start.97 = (f32[1,1,256]{2,1,0:T(1,128)}, f32[1,1,256]{2,1,0:T(1,128)S(1)}, u32[]{:S(2)}) copy-start(f32[1,1,256]{2,1,0:T(1,128)S(1)} %get-tuple-element.1519) | copy-start | bytes 3076 | tf_op jit(solution)/shard_map/while
  34.0 41.6 %copy-start.1 = (bf16[16,16,256]{2,1,0:T(8,128)(2,1)}, bf16[16,16,256]{2,1,0:T(8,128)(2,1)S(1)}, u32[]{:S(2)}) copy-start(bf16[16,16,256]{2,1,0:T(8,128)(2,1)S(1)} %get-tuple-element.1597) | copy-start | bytes 393220 | tf_op jit(solution)/shard_map/while
  78.1 11.0 %collective-permute-start = (bf16[3,16,256]{2,1,0:T(8,128)(2,1)}, bf16[3,16,256]{2,1,0:T(8,128)(2,1)}, u32[]{:S(2)}, u32[]{:S(2)}) collective-permute-start(bf16[3,16,256]{2,1,0:T(8,128)(2,1)} %bitcast.412), channel_id=1, source_target_pairs={{4,0},{5,1},{6,2},{7,3},{12,8},{13,9},{14,10},{15,11},{20,16},{21,... | collective-permute-start | bytes 73736 | tf_op jit(solution)/shard_map/while/body/eval_jaxpr/ppermute | solution.py:19
  83.6 6.0 %collective-permute-start.1 = (bf16[3,16,256]{2,1,0:T(8,128)(2,1)}, bf16[3,16,256]{2,1,0:T(8,128)(2,1)}, u32[]{:S(2)}, u32[]{:S(2)}) collective-permute-start(bf16[3,16,256]{2,1,0:T(8,128)(2,1)} %bitcast.346), channel_id=1, source_target_pairs={{0,4},{1,5},{2,6},{3,7},{8,12},{9,13},{10,14},{11,15},{16,20},{17,... | collective-permute-start | bytes 73736 | tf_op jit(solution)/shard_map/while/body/eval_jaxpr/ppermute | solution.py:16
  90.4 7.3 %collective-permute-start.2 = (bf16[22,3,256]{2,1,0:T(4,128)(2,1)S(1)}, bf16[22,3,256]{2,1,0:T(4,128)(2,1)S(1)}, u32[]{:S(2)}, u32[]{:S(2)}) collective-permute-start(bf16[22,3,256]{2,1,0:T(4,128)(2,1)S(1)} %get-tuple-element.1601), channel_id=1, source_target_pairs={{1,0},{2,1},{3,2},{5,4},{6,5},{7,6},{9,8},{10,9},{11,10},{13,12},{... | collective-permute-start | bytes 101384 | tf_op jit(solution)/shard_map/while/body/eval_jaxpr/ppermute | solution.py:19
  91.7 6.0 %collective-permute-start.3 = (bf16[22,3,256]{2,1,0:T(4,128)(2,1)S(1)}, bf16[22,3,256]{2,1,0:T(4,128)(2,1)S(1)}, u32[]{:S(2)}, u32[]{:S(2)}) collective-permute-start(bf16[22,3,256]{2,1,0:T(4,128)(2,1)S(1)} %get-tuple-element.1602), channel_id=1, source_target_pairs={{0,1},{1,2},{2,3},{4,5},{5,6},{6,7},{8,9},{9,10},{10,11},{12,13},{... | collective-permute-start | bytes 101384 | tf_op jit(solution)/shard_map/while/body/eval_jaxpr/ppermute | solution.py:16
  102.9 19.4 %collective-permute-start.4 = (bf16[16,16,256]{2,1,0:T(8,128)(2,1)S(1)}, bf16[16,16,256]{2,1,0:T(8,128)(2,1)S(1)}, u32[]{:S(2)}, u32[]{:S(2)}) collective-permute-start(bf16[16,16,256]{2,1,0:T(8,128)(2,1)S(1)} %get-tuple-element.1605), channel_id=1, source_target_pairs={{8,0},{16,8},{24,16},{9,1},{17,9},{25,17},{10,2},{18,10},{26,18},{... | collective-permute-start | bytes 393224 | tf_op jit(solution)/shard_map/while/body/eval_jaxpr/ppermute | solution.py:27
  129.2 29.2 %copy-start.63 = (f32[1,1,256]{2,1,0:T(1,128)}, f32[1,1,256]{2,1,0:T(1,128)S(1)}, u32[]{:S(2)}) copy-start(f32[1,1,256]{2,1,0:T(1,128)S(1)} %get-tuple-element.1591) | copy-start | bytes 3076 | tf_op jit(solution)/shard_map/while
  129.2 29.9 %copy-start.61 = (f32[1,1,256]{2,1,0:T(1,128)}, f32[1,1,256]{2,1,0:T(1,128)S(1)}, u32[]{:S(2)}) copy-start(f32[1,1,256]{2,1,0:T(1,128)S(1)} %get-tuple-element.1593) | copy-start | bytes 3076 | tf_op jit(solution)/shard_map/while
  129.2 30.7 %copy-start.59 = (f32[1,1,256]{2,1,0:T(1,128)}, f32[1,1,256]{2,1,0:T(1,128)S(1)}, u32[]{:S(2)}) copy-start(f32[1,1,256]{2,1,0:T(1,128)S(1)} %get-tuple-element.1595) | copy-start | bytes 3076 | tf_op jit(solution)/shard_map/while
  130.9 41.1 %copy-start.99 = (f32[1,1,256]{2,1,0:T(1,128)}, f32[1,1,256]{2,1,0:T(1,128)S(1)}, u32[]{:S(2)}) copy-start(f32[1,1,256]{2,1,0:T(1,128)S(1)} %get-tuple-element.1517) | copy-start | bytes 3076 | tf_op jit(solution)/shard_map/while
  130.9 41.9 %copy-start.97 = (f32[1,1,256]{2,1,0:T(1,128)}, f32[1,1,256]{2,1,0:T(1,128)S(1)}, u32[]{:S(2)}) copy-start(f32[1,1,256]{2,1,0:T(1,128)S(1)} %get-tuple-element.1519) | copy-start | bytes 3076 | tf_op jit(solution)/shard_map/while
  132.6 41.6 %copy-start.1 = (bf16[16,16,256]{2,1,0:T(8,128)(2,1)}, bf16[16,16,256]{2,1,0:T(8,128)(2,1)S(1)}, u32[]{:S(2)}) copy-start(bf16[16,16,256]{2,1,0:T(8,128)(2,1)S(1)} %get-tuple-element.1597) | copy-start | bytes 393220 | tf_op jit(solution)/shard_map/while
  189.8 12.9 %collective-permute-start = (bf16[3,16,256]{2,1,0:T(8,128)(2,1)}, bf16[3,16,256]{2,1,0:T(8,128)(2,1)}, u32[]{:S(2)}, u32[]{:S(2)}) collective-permute-start(bf16[3,16,256]{2,1,0:T(8,128)(2,1)} %bitcast.412), channel_id=1, source_target_pairs={{4,0},{5,1},{6,2},{7,3},{12,8},{13,9},{14,10},{15,11},{20,16},{21,... | collective-permute-start | bytes 73736 | tf_op jit(solution)/shard_map/while/body/eval_jaxpr/ppermute | solution.py:19
  195.9 6.8 %collective-permute-start.1 = (bf16[3,16,256]{2,1,0:T(8,128)(2,1)}, bf16[3,16,256]{2,1,0:T(8,128)(2,1)}, u32[]{:S(2)}, u32[]{:S(2)}) collective-permute-start(bf16[3,16,256]{2,1,0:T(8,128)(2,1)} %bitcast.346), channel_id=1, source_target_pairs={{0,4},{1,5},{2,6},{3,7},{8,12},{9,13},{10,14},{11,15},{16,20},{17,... | collective-permute-start | bytes 73736 | tf_op jit(solution)/shard_map/while/body/eval_jaxpr/ppermute | solution.py:16
  203.5 5.9 %collective-permute-start.2 = (bf16[22,3,256]{2,1,0:T(4,128)(2,1)S(1)}, bf16[22,3,256]{2,1,0:T(4,128)(2,1)S(1)}, u32[]{:S(2)}, u32[]{:S(2)}) collective-permute-start(bf16[22,3,256]{2,1,0:T(4,128)(2,1)S(1)} %get-tuple-element.1601), channel_id=1, source_target_pairs={{1,0},{2,1},{3,2},{5,4},{6,5},{7,6},{9,8},{10,9},{11,10},{13,12},{... | collective-permute-start | bytes 101384 | tf_op jit(solution)/shard_map/while/body/eval_jaxpr/ppermute | solution.py:19
  204.8 4.6 collective-permute-start.3
  214.6 7.0 %collective-permute-start.4 = (bf16[16,16,256]{2,1,0:T(8,128)(2,1)S(1)}, bf16[16,16,256]{2,1,0:T(8,128)(2,1)S(1)}, u32[]{:S(2)}, u32[]{:S(2)}) collective-permute-start(bf16[16,16,256]{2,1,0:T(8,128)(2,1)S(1)} %get-tuple-element.1605), channel_id=1, source_target_pairs={{8,0},{16,8},{24,16},{9,1},{17,9},{25,17},{10,2},{18,10},{26,18},{... | collective-permute-start | bytes 393224 | tf_op jit(solution)/shard_map/while/body/eval_jaxpr/ppermute | solution.py:27
  228.5 29.2 %copy-start.63 = (f32[1,1,256]{2,1,0:T(1,128)}, f32[1,1,256]{2,1,0:T(1,128)S(1)}, u32[]{:S(2)}) copy-start(f32[1,1,256]{2,1,0:T(1,128)S(1)} %get-tuple-element.1591) | copy-start | bytes 3076 | tf_op jit(solution)/shard_map/while
  228.5 29.9 %copy-start.61 = (f32[1,1,256]{2,1,0:T(1,128)}, f32[1,1,256]{2,1,0:T(1,128)S(1)}, u32[]{:S(2)}) copy-start(f32[1,1,256]{2,1,0:T(1,128)S(1)} %get-tuple-element.1593) | copy-start | bytes 3076 | tf_op jit(solution)/shard_map/while
  228.6 30.7 %copy-start.59 = (f32[1,1,256]{2,1,0:T(1,128)}, f32[1,1,256]{2,1,0:T(1,128)S(1)}, u32[]{:S(2)}) copy-start(f32[1,1,256]{2,1,0:T(1,128)S(1)} %get-tuple-element.1595) | copy-start | bytes 3076 | tf_op jit(solution)/shard_map/while
  230.2 41.1 %copy-start.99 = (f32[1,1,256]{2,1,0:T(1,128)}, f32[1,1,256]{2,1,0:T(1,128)S(1)}, u32[]{:S(2)}) copy-start(f32[1,1,256]{2,1,0:T(1,128)S(1)} %get-tuple-element.1517) | copy-start | bytes 3076 | tf_op jit(solution)/shard_map/while
  230.2 41.9 %copy-start.97 = (f32[1,1,256]{2,1,0:T(1,128)}, f32[1,1,256]{2,1,0:T(1,128)S(1)}, u32[]{:S(2)}) copy-start(f32[1,1,256]{2,1,0:T(1,128)S(1)} %get-tuple-element.1519) | copy-start | bytes 3076 | tf_op jit(solution)/shard_map/while
  232.0 41.6 %copy-start.1 = (bf16[16,16,256]{2,1,0:T(8,128)(2,1)}, bf16[16,16,256]{2,1,0:T(8,128)(2,1)S(1)}, u32[]{:S(2)}) copy-start(bf16[16,16,256]{2,1,0:T(8,128)(2,1)S(1)} %get-tuple-element.1597) | copy-start | bytes 393220 | tf_op jit(solution)/shard_map/while
  276.1 13.1 %collective-permute-start = (bf16[3,16,256]{2,1,0:T(8,128)(2,1)}, bf16[3,16,256]{2,1,0:T(8,128)(2,1)}, u32[]{:S(2)}, u32[]{:S(2)}) collective-permute-start(bf16[3,16,256]{2,1,0:T(8,128)(2,1)} %bitcast.412), channel_id=1, source_target_pairs={{4,0},{5,1},{6,2},{7,3},{12,8},{13,9},{14,10},{15,11},{20,16},{21,... | collective-permute-start | bytes 73736 | tf_op jit(solution)/shard_map/while/body/eval_jaxpr/ppermute | solution.py:19
  282.4 6.8 %collective-permute-start.1 = (bf16[3,16,256]{2,1,0:T(8,128)(2,1)}, bf16[3,16,256]{2,1,0:T(8,128)(2,1)}, u32[]{:S(2)}, u32[]{:S(2)}) collective-permute-start(bf16[3,16,256]{2,1,0:T(8,128)(2,1)} %bitcast.346), channel_id=1, source_target_pairs={{0,4},{1,5},{2,6},{3,7},{8,12},{9,13},{10,14},{11,15},{16,20},{17,... | collective-permute-start | bytes 73736 | tf_op jit(solution)/shard_map/while/body/eval_jaxpr/ppermute | solution.py:16
  290.0 6.7 %collective-permute-start.2 = (bf16[22,3,256]{2,1,0:T(4,128)(2,1)S(1)}, bf16[22,3,256]{2,1,0:T(4,128)(2,1)S(1)}, u32[]{:S(2)}, u32[]{:S(2)}) collective-permute-start(bf16[22,3,256]{2,1,0:T(4,128)(2,1)S(1)} %get-tuple-element.1601), channel_id=1, source_target_pairs={{1,0},{2,1},{3,2},{5,4},{6,5},{7,6},{9,8},{10,9},{11,10},{13,12},{... | collective-permute-start | bytes 101384 | tf_op jit(solution)/shard_map/while/body/eval_jaxpr/ppermute | solution.py:19
  291.3 5.4 %collective-permute-start.3 = (bf16[22,3,256]{2,1,0:T(4,128)(2,1)S(1)}, bf16[22,3,256]{2,1,0:T(4,128)(2,1)S(1)}, u32[]{:S(2)}, u32[]{:S(2)}) collective-permute-start(bf16[22,3,256]{2,1,0:T(4,128)(2,1)S(1)} %get-tuple-element.1602), channel_id=1, source_target_pairs={{0,1},{1,2},{2,3},{4,5},{5,6},{6,7},{8,9},{9,10},{10,11},{12,13},{... | collective-permute-start | bytes 101384 | tf_op jit(solution)/shard_map/while/body/eval_jaxpr/ppermute | solution.py:16
  301.8 17.9 %collective-permute-start.4 = (bf16[16,16,256]{2,1,0:T(8,128)(2,1)S(1)}, bf16[16,16,256]{2,1,0:T(8,128)(2,1)S(1)}, u32[]{:S(2)}, u32[]{:S(2)}) collective-permute-start(bf16[16,16,256]{2,1,0:T(8,128)(2,1)S(1)} %get-tuple-element.1605), channel_id=1, source_target_pairs={{8,0},{16,8},{24,16},{9,1},{17,9},{25,17},{10,2},{18,10},{26,18},{... | collective-permute-start | bytes 393224 | tf_op jit(solution)/shard_map/while/body/eval_jaxpr/ppermute | solution.py:27
  326.7 29.9 %copy-start.61 = (f32[1,1,256]{2,1,0:T(1,128)}, f32[1,1,256]{2,1,0:T(1,128)S(1)}, u32[]{:S(2)}) copy-start(f32[1,1,256]{2,1,0:T(1,128)S(1)} %get-tuple-element.1593) | copy-start | bytes 3076 | tf_op jit(solution)/shard_map/while
  326.7 30.7 %copy-start.59 = (f32[1,1,256]{2,1,0:T(1,128)}, f32[1,1,256]{2,1,0:T(1,128)S(1)}, u32[]{:S(2)}) copy-start(f32[1,1,256]{2,1,0:T(1,128)S(1)} %get-tuple-element.1595) | copy-start | bytes 3076 | tf_op jit(solution)/shard_map/while
  328.4 41.1 %copy-start.99 = (f32[1,1,256]{2,1,0:T(1,128)}, f32[1,1,256]{2,1,0:T(1,128)S(1)}, u32[]{:S(2)}) copy-start(f32[1,1,256]{2,1,0:T(1,128)S(1)} %get-tuple-element.1517) | copy-start | bytes 3076 | tf_op jit(solution)/shard_map/while
  328.4 41.9 %copy-start.97 = (f32[1,1,256]{2,1,0:T(1,128)}, f32[1,1,256]{2,1,0:T(1,128)S(1)}, u32[]{:S(2)}) copy-start(f32[1,1,256]{2,1,0:T(1,128)S(1)} %get-tuple-element.1519) | copy-start | bytes 3076 | tf_op jit(solution)/shard_map/while
  330.1 41.6 %copy-start.1 = (bf16[16,16,256]{2,1,0:T(8,128)(2,1)}, bf16[16,16,256]{2,1,0:T(8,128)(2,1)S(1)}, u32[]{:S(2)}) copy-start(bf16[16,16,256]{2,1,0:T(8,128)(2,1)S(1)} %get-tuple-element.1597) | copy-start | bytes 393220 | tf_op jit(solution)/shard_map/while
  374.2 12.9 %collective-permute-start = (bf16[3,16,256]{2,1,0:T(8,128)(2,1)}, bf16[3,16,256]{2,1,0:T(8,128)(2,1)}, u32[]{:S(2)}, u32[]{:S(2)}) collective-permute-start(bf16[3,16,256]{2,1,0:T(8,128)(2,1)} %bitcast.412), channel_id=1, source_target_pairs={{4,0},{5,1},{6,2},{7,3},{12,8},{13,9},{14,10},{15,11},{20,16},{21,... | collective-permute-start | bytes 73736 | tf_op jit(solution)/shard_map/while/body/eval_jaxpr/ppermute | solution.py:19
  380.4 6.8 %collective-permute-start.1 = (bf16[3,16,256]{2,1,0:T(8,128)(2,1)}, bf16[3,16,256]{2,1,0:T(8,128)(2,1)}, u32[]{:S(2)}, u32[]{:S(2)}) collective-permute-start(bf16[3,16,256]{2,1,0:T(8,128)(2,1)} %bitcast.346), channel_id=1, source_target_pairs={{0,4},{1,5},{2,6},{3,7},{8,12},{9,13},{10,14},{11,15},{16,20},{17,... | collective-permute-start | bytes 73736 | tf_op jit(solution)/shard_map/while/body/eval_jaxpr/ppermute | solution.py:16
  388.0 7.5 %collective-permute-start.2 = (bf16[22,3,256]{2,1,0:T(4,128)(2,1)S(1)}, bf16[22,3,256]{2,1,0:T(4,128)(2,1)S(1)}, u32[]{:S(2)}, u32[]{:S(2)}) collective-permute-start(bf16[22,3,256]{2,1,0:T(4,128)(2,1)S(1)} %get-tuple-element.1601), channel_id=1, source_target_pairs={{1,0},{2,1},{3,2},{5,4},{6,5},{7,6},{9,8},{10,9},{11,10},{13,12},{... | collective-permute-start | bytes 101384 | tf_op jit(solution)/shard_map/while/body/eval_jaxpr/ppermute | solution.py:19
  389.3 6.3 %collective-permute-start.3 = (bf16[22,3,256]{2,1,0:T(4,128)(2,1)S(1)}, bf16[22,3,256]{2,1,0:T(4,128)(2,1)S(1)}, u32[]{:S(2)}, u32[]{:S(2)}) collective-permute-start(bf16[22,3,256]{2,1,0:T(4,128)(2,1)S(1)} %get-tuple-element.1602), channel_id=1, source_target_pairs={{0,1},{1,2},{2,3},{4,5},{5,6},{6,7},{8,9},{9,10},{10,11},{12,13},{... | collective-permute-start | bytes 101384 | tf_op jit(solution)/shard_map/while/body/eval_jaxpr/ppermute | solution.py:16
  400.7 7.0 %collective-permute-start.4 = (bf16[16,16,256]{2,1,0:T(8,128)(2,1)S(1)}, bf16[16,16,256]{2,1,0:T(8,128)(2,1)S(1)}, u32[]{:S(2)}, u32[]{:S(2)}) collective-permute-start(bf16[16,16,256]{2,1,0:T(8,128)(2,1)S(1)} %get-tuple-element.1605), channel_id=1, source_target_pairs={{8,0},{16,8},{24,16},{9,1},{17,9},{25,17},{10,2},{18,10},{26,18},{... | collective-permute-start | bytes 393224 | tf_op jit(solution)/shard_map/while/body/eval_jaxpr/ppermute | solution.py:27
  (456 other events, 3078.1 us)
Sparse Core Ops, SparseCore 0:
  408.8 78.4 all-reduce.2
where the time goes:
time: 504 us; the launch traced here: 497 us
  local copies, waits for them, and re-layouts  207 us (41%)
  waiting for transfers between devices  81.1 us (16%)
  starting transfers between devices  80.8 us (16%)
  other arithmetic  76.9 us (15%)
  blocking collectives  27.9 us (6%)
  between operations  14.8 us (3%)
  loops' own time  5.84 us (1%)
    mul x188, local copies, waits for them, and re-layouts, depthwise(): conv_taps[shift_r, shift_c]  157 us
    psum x1, waiting for transfers between devices, per_device(): lax.psum((sum_in, sum_out, sum_taps), ('row', 'col'))  50 us
    ppermute x10, starting transfers between devices, with_halo(): lax.ppermute(lax.slice_in_dim(block, 0, width, axis=dim), axis, backward)  32.3 us
    psum x1, blocking collectives, per_device(): lax.psum((sum_in, sum_out, sum_taps), ('row', 'col'))  27.9 us
    ppermute x4, waiting for transfers between devices, shifted(): return lax.ppermute(block, axis, route)  26.9 us
    convert_element_type x12, other arithmetic, depthwise(): total = total + conv_taps[shift_r, shift_c] * padded[shift_r:shift_r + he...  25 us
    ppermute x10, starting transfers between devices, with_halo(): lax.ppermute(lax.slice_in_dim(block, block.shape[dim] - width, None, axis...  24.2 us
    ppermute x4, starting transfers between devices, shifted(): return lax.ppermute(block, axis, route)  24.2 us
  transfers between devices with their start and end apart: 25, of which 8 were waited for; matrix products, arithmetic and copies ran while one was open for 5% of the time, Pallas kernels for 0%

commit v1 on v0

v1 whole, which is shorter than its diff:
```python
import functools
import math

import jax
import jax.numpy as jnp
from jax import lax
from jax.experimental import pallas as pl
from jax.experimental.pallas import tpu as pltpu
from jax.sharding import PartitionSpec as P

epsilon = 1e-06
PAD = 8
LANES = 128
VMEM_BYTES = 48 * 1024 * 1024
LINE = ("segment", "row", "col")

f32 = jnp.float32
bf16 = jnp.bfloat16


class Plan:
    def __init__(self, segments, rows, cols, height, across, channels, hidden, side):
        self.segments, self.rows, self.cols = segments, rows, cols
        self.height, self.across = height, across
        self.channels, self.hidden, self.side = channels, hidden, side
        self.margin = side // 2
        self.width = across // rows
        self.full = height * rows
        self.padded = self.width + 2 * self.margin
        self.cells = self.width * self.full
        self.part = min(256, hidden)

    def main_size(self):
        sizes = []
        for r in range(self.rows):
            low = max(0, r * self.width - self.margin)
            high = min(self.across, (r + 1) * self.width + self.margin)
            sizes.append(high - low)
        return max(sizes)

    def main_start(self, r):
        return jnp.clip(r * self.width - self.margin, 0, self.across - self.main_size())

    def needs_left(self, r):
        return r * self.width < self.margin

    def needs_right(self, r):
        return (r + 1) * self.width + self.margin > self.across

    def sides(self):
        left = [r for r in range(self.rows) if self.needs_left(r)]
        right = [r for r in range(self.rows) if self.needs_right(r)]
        if set(left) & set(right):
            return [(left, []), ([], right)]
        return [(left, right)]

    def distances(self):
        out = []
        distance = 1
        while (distance - 1) * self.width < self.margin:
            out.append((distance, min(self.width, self.margin - (distance - 1) * self.width)))
            distance += 1
        return out

    def index(self, s, r, c):
        return (s * self.rows + r) * self.cols + c

    def strip(self, s, t):
        return self.index(s, t % self.rows, t // self.rows)

    def own(self, column):
        return self.margin <= column < self.margin + self.width


def vmem():
    return pl.BlockSpec(memory_space=pltpu.VMEM)


def smem():
    return pl.BlockSpec(memory_space=pltpu.SMEM)


def shape(dims, dtype):
    return jax.ShapeDtypeStruct(tuple(dims), dtype)


def call(kernel, name, operands, outs, scratch, flops):
    moved = sum(math.prod(o.shape) * o.dtype.itemsize for o in list(operands) + list(outs))
    return pl.pallas_call(
        kernel,
        out_shape=outs,
        in_specs=[vmem()] * len(operands),
        out_specs=[vmem()] * len(outs),
        scratch_shapes=scratch,
        compiler_params=pltpu.CompilerParams(vmem_limit_bytes=VMEM_BYTES),
        cost_estimate=pl.CostEstimate(flops=flops, bytes_accessed=moved, transcendentals=0),
        name=name,
    )(*operands)


def pack_kernel(plan, params, tissue_ref, x_hbm, g_hbm, *refs):
    rows, across, height = plan.rows, plan.across, plan.height
    count = rows * (1 + len(plan.sides()))
    sources, refs = refs[:params], refs[params:]
    outs, refs = refs[:count], refs[count:]
    targets, (x_ref, g_ref, xt, gt, sems) = refs[:params], refs[params:]
    moves = [
        pltpu.make_async_copy(source, target, sems.at[k])
        for k, (source, target) in enumerate(zip((x_hbm, g_hbm, *sources), (x_ref, g_ref, *targets)))
    ]
    for move in moves:
        move.start()
    tiles_r, tiles_c = tissue_ref.shape
    side_r, side_c = height // tiles_r, across // tiles_c
    me = lax.axis_index("row")
    row_at = lax.broadcasted_iota(jnp.int32, (height, plan.channels), 0)
    lane_at = lax.broadcasted_iota(jnp.int32, (height, plan.channels), 1)

    def slot(start):
        col_at = lane_at + start
        total = jnp.zeros((height, plan.channels), f32)
        for a in range(tiles_r):
            in_row = (row_at >= a * side_r) & (row_at < (a + 1) * side_r)
            for b in range(tiles_c):
                inside = in_row & (col_at >= b * side_c) & (col_at < (b + 1) * side_c)
                total = jnp.where(inside, tissue_ref[a, b].astype(f32), total)
        return total.astype(bf16)

    moves[0].wait()
    xt[...] = jnp.swapaxes(x_ref[...].astype(f32), 0, 1).astype(bf16)
    moves[1].wait()
    gt[...] = jnp.swapaxes(g_ref[...].astype(f32), 0, 1).astype(bf16)
    nx, m, w = plan.main_size(), plan.margin, plan.width
    for dr in range(rows):
        target = lax.rem(me - dr + rows, rows)
        out = outs[dr]
        out[0:nx] = xt[pl.ds(plan.main_start(target), nx)]
        out[nx : nx + w] = gt[pl.ds(target * w, w)]
        out[nx + w] = slot(target * w)
    for k, (left, right) in enumerate(plan.sides()):
        for dr in range(rows):
            target = lax.rem(me - dr + rows, rows)
            is_left = functools.reduce(jnp.logical_or, [target == r for r in left], jnp.bool_(False))
            outs[rows * (1 + k) + dr][...] = xt[pl.ds(jnp.where(is_left, across - m, 0), m)]
    for move in moves[2:]:
        move.wait()


def pack(plan, tissue, x, g, params):
    rows, h, c = plan.rows, plan.height, plan.channels
    outs = [shape((plan.main_size() + plan.width + 1, h, c), bf16)] * rows
    outs += [shape((plan.margin, h, c), bf16)] * (rows * len(plan.sides()))
    outs += [shape(a.shape, a.dtype) for a in params]
    tile = pltpu.VMEM((h, plan.across, c), bf16)
    turned = pltpu.VMEM((plan.across, h, c), bf16)
    count = len(params)
    out = pl.pallas_call(
        functools.partial(pack_kernel, plan, count),
        out_shape=outs,
        in_specs=[smem()] + [pl.BlockSpec(memory_space=pltpu.HBM)] * (2 + count),
        out_specs=[vmem()] * len(outs),
        scratch_shapes=[tile, tile, turned, turned, pltpu.SemaphoreType.DMA((2 + count,))],
        compiler_params=pltpu.CompilerParams(vmem_limit_bytes=VMEM_BYTES),
        cost_estimate=pl.CostEstimate(flops=1000, bytes_accessed=4 << 20, transcendentals=0),
        name="pack",
    )(tissue, x, g, *params)
    return out[:-count], out[-count:]


def exchange(plan, pieces):
    rows, cols = plan.rows, plan.cols
    mains, sides = [pieces[0]], []
    for k, (left, right) in enumerate(plan.sides()):
        for dr in range(rows):
            pairs = []
            for s in range(plan.segments):
                for r in range(rows):
                    for c in range(cols):
                        step = (-1 if r in left else 0) + (1 if r in right else 0)
                        if step != 0 and 0 <= c + step < cols:
                            source = plan.index(s, (r + dr) % rows, c + step)
                            pairs.append((source, plan.index(s, r, c)))
            sides.append(lax.ppermute(pieces[rows * (1 + k) + dr], LINE, pairs))
    for dr in range(1, rows):
        pairs = []
        for s in range(plan.segments):
            for r in range(rows):
                for c in range(cols):
                    pairs.append((plan.index(s, (r + dr) % rows, c), plan.index(s, r, c)))
        mains.append(lax.ppermute(pieces[dr], LINE, pairs))
    return mains + sides


def conv_block(plan, load, row_start, half, taps_ref, flip, keep):
    side = plan.side
    lanes = pl.ds(half * LANES, LANES)
    totals = [None] * plan.width
    for i in range(side):
        rows_at = pl.ds(row_start + (side - 1 - i if flip else i), 8)
        window = [load(k, rows_at, lanes) if keep(k) else None for k in range(plan.padded)]
        for j in range(side):
            tap = taps_ref[i, pl.ds(j, 1), lanes]
            move = side - 1 - j if flip else j
            for q in range(plan.width):
                if window[q + move] is not None:
                    term = tap * window[q + move]
                    totals[q] = term if totals[q] is None else totals[q] + term
    return [jnp.zeros((8, LANES), f32) if t is None else t for t in totals]


def clear_rims(ref, full):
    zeros = jnp.zeros((ref.shape[0], PAD, ref.shape[2]), ref.dtype)
    ref[:, 0:PAD, :] = zeros
    ref[:, PAD + full : PAD + full + PAD, :] = zeros


def blocks(plan):
    return [(half, block) for half in range(plan.channels // LANES) for block in range(plan.full // 8)]


def forward_kernel(plan, *refs):
    rows, full, h = plan.rows, plan.full, plan.height
    pieces = refs[: rows * (1 + len(plan.sides()))]
    refs = refs[len(pieces) :]
    (taps_ref, conv_bias_ref, gain_ref, bias_ref, w_in_ref, b_in_ref) = refs[:6]
    (og_ref, xw_ref, mask_ref, standard_ref, inv_ref, gate_ref, hidden_ref, normed_ref) = refs[6:14]
    wide_x, conv_ref, pre_ref = refs[14:]
    me = lax.axis_index("row")
    m, w, nx = plan.margin, plan.width, plan.main_size()

    clear_rims(wide_x, full)
    for dr in range(rows):
        piece = pieces[dr]
        top = pl.multiple_of(lax.rem(me + dr, rows) * h, h)
        wide_x[pl.ds(m + plan.main_start(me), nx), pl.ds(PAD + top, h), :] = piece[0:nx].astype(f32)
        og_ref[:, pl.ds(top, h), :] = piece[nx : nx + w]
        marks = piece[nx + w].astype(f32)
        for l in range(w):
            at = pl.ds(pl.multiple_of(l * full + top, h), h)
            mask_ref[at, :] = jnp.broadcast_to(marks[:, l : l + 1], (h, LANES))
    for k, (left, right) in enumerate(plan.sides()):
        is_left = functools.reduce(jnp.logical_or, [me == r for r in left], jnp.bool_(False))
        for dr in range(rows):
            top = pl.multiple_of(lax.rem(me + dr, rows) * h, h)
            start = jnp.where(is_left, 0, m + plan.across)
            piece = pieces[rows * (1 + k) + dr]
            wide_x[pl.ds(start, m), pl.ds(PAD + top, h), :] = piece[...].astype(f32)

    base = me * w
    xw_ref[...] = wide_x[pl.ds(base, plan.padded)]

    def load(column, rows_at, lanes):
        return wide_x[base + column, rows_at, lanes]

    for half, block in blocks(plan):
        lanes = pl.ds(half * LANES, LANES)
        sums = conv_block(plan, load, PAD - m + 8 * block, half, taps_ref, False, lambda k: True)
        for q in range(w):
            conv_ref[pl.ds(q * full + 8 * block, 8), lanes] = sums[q] + conv_bias_ref[:, lanes]

    for col in range(w):
        rows_at = pl.ds(col * full, full)
        conv_out = conv_ref[rows_at, :]
        average = jnp.mean(conv_out, axis=-1, keepdims=True)
        centred = conv_out - average
        spread = jnp.mean(centred * centred, axis=-1, keepdims=True)
        inv_std = lax.rsqrt(spread + epsilon)
        standard = centred * inv_std
        standard_ref[rows_at, :] = standard
        inv_ref[rows_at, :] = jnp.broadcast_to(inv_std, (full, LANES))
        normed_ref[rows_at, :] = (standard * gain_ref[...] + bias_ref[...]).astype(bf16)

    c1 = math.sqrt(2.0 / math.pi)
    c2 = c1 * 0.044715
    for n in range(plan.hidden // plan.part):
        at = pl.ds(n * plan.part, plan.part)
        pre_ref[n % 2] = (
            jnp.dot(normed_ref[...], w_in_ref[:, at], preferred_element_type=f32) + b_in_ref[:, at]
        )
        for col in range(w):
            rows_at = pl.ds(col * full, full)
            pre = pre_ref[n % 2, rows_at, :]
            square = pre * pre
            half_one = 0.5 + 0.5 * jnp.tanh(pre * (c1 + c2 * square))
            gated = pre * half_one
            slope = half_one + gated * (1.0 - half_one) * (2.0 * c1 + 6.0 * c2 * square)
            gate_ref[rows_at, at] = slope.astype(bf16)
            hidden_ref[rows_at, at] = gated.astype(bf16)


def forward(plan, pieces, taps, conv_bias, gain, bias, w_in, b_in):
    c, full, cells = plan.channels, plan.full, plan.cells
    outs = [
        shape((plan.width, full, c), bf16),
        shape((plan.padded, full + 2 * PAD, c), f32),
        shape((cells, LANES), f32),
        shape((cells, c), f32),
        shape((cells, LANES), f32),
        shape((cells, plan.hidden), bf16),
        shape((cells, plan.hidden), bf16),
        shape((cells, c), bf16),
    ]
    scratch = [
        pltpu.VMEM((plan.across + 2 * plan.margin, full + 2 * PAD, c), f32),
        pltpu.VMEM((cells, c), f32),
        pltpu.VMEM((2, cells, plan.part), f32),
    ]
    return call(
        functools.partial(forward_kernel, plan),
        "forward",
        [*pieces, taps, conv_bias, gain, bias, w_in, b_in],
        outs,
        scratch,
        2 * cells * c * plan.hidden,
    )


def across_lanes(value, channels):
    return jnp.concatenate([value] * (channels // LANES), axis=-1)


def fill_edges(plan, edge_ref, edges):
    clear_rims(edge_ref, plan.full)
    m, w = plan.margin, plan.width
    for k, (distance, count) in enumerate(plan.distances()):
        for start, piece in (
            (m - (distance - 1) * w - count, edges[2 * k]),
            (m + distance * w, edges[2 * k + 1]),
        ):
            edge_ref[pl.ds(start, count), PAD : PAD + plan.full, :] = piece[...].astype(f32)


def edge_sums(plan, edge_ref, taps_ref, half, block):
    def load(column, rows_at, lanes):
        return edge_ref[column, rows_at, lanes]

    start = PAD - plan.margin + 8 * block
    return conv_block(plan, load, start, half, taps_ref, True, lambda k: not plan.own(k))


def own_sums(plan, cg_ref, taps_ref, half, block):
    def load(column, rows_at, lanes):
        return cg_ref[column - plan.margin, rows_at, lanes]

    start = PAD - plan.margin + 8 * block
    return conv_block(plan, load, start, half, taps_ref, True, plan.own)


def load_upstream(plan, g_ref, og_ref, received, edge_ref):
    if received is None:
        g_ref[...] = og_ref[...]
        return
    taps_ref, main_ref, edges = received[0], received[1], received[2:]
    last = lax.axis_index("segment") == plan.segments - 1
    fill_edges(plan, edge_ref, edges)
    for half, block in blocks(plan):
        if block % 2:
            continue
        lanes = pl.ds(half * LANES, LANES)
        rows_at = pl.ds(8 * block, 16)
        parts = [edge_sums(plan, edge_ref, taps_ref, half, block + k) for k in range(2)]
        for q in range(plan.width):
            rest = jnp.concatenate([part[q] for part in parts], axis=0)
            value = (main_ref[q, rows_at, lanes].astype(f32) + rest).astype(bf16)
            g_ref[q, rows_at, lanes] = jnp.where(last, og_ref[q, rows_at, lanes], value)


def norm_back(plan, norm_grad_ref, gain_ref, standard_ref, inv_ref, cg_ref):
    full = plan.full
    clear_rims(cg_ref, full)
    for col in range(plan.width):
        rows_at = pl.ds(col * full, full)
        norm_grad = norm_grad_ref[rows_at, :] * gain_ref[...]
        standard = standard_ref[rows_at, :]
        inv_std = across_lanes(inv_ref[rows_at, :], plan.channels)
        grad = inv_std * (
            norm_grad
            - jnp.mean(norm_grad, axis=-1, keepdims=True)
            - standard * jnp.mean(norm_grad * standard, axis=-1, keepdims=True)
        )
        cg_ref[col, PAD : PAD + full, :] = grad.astype(bf16).astype(f32)


def contract_last(a, b):
    return lax.dot_general(a, b, (((1,), (1,)), ((), ())), preferred_element_type=f32)


def branch(plan, g_ref, scale_ref, mask_ref, bg_ref):
    full = plan.full
    for col in range(plan.width):
        rows_at = pl.ds(col * full, full)
        mask = across_lanes(mask_ref[rows_at, :], plan.channels)
        bg_ref[rows_at, :] = (mask * scale_ref[...] * g_ref[col].astype(f32)).astype(bf16)


def put_edges(plan, cg_ref, outs):
    rows_at = pl.ds(PAD, plan.full)
    for k, (distance, count) in enumerate(plan.distances()):
        outs[2 * k][...] = cg_ref[pl.ds(plan.width - count, count), rows_at, :].astype(bf16)
        outs[2 * k + 1][...] = cg_ref[pl.ds(0, count), rows_at, :].astype(bf16)


def edge_shapes(plan):
    return [
        shape((count, plan.full, plan.channels), bf16) for _, count in plan.distances() for _ in range(2)
    ]


def send_edges(plan, edges, step):
    strips = plan.rows * plan.cols
    received = []
    for k, (distance, _) in enumerate(plan.distances()):
        for way, piece in ((distance, edges[2 * k]), (-distance, edges[2 * k + 1])):
            pairs = [
                (plan.strip(s, t), plan.strip(s + step, t + way))
                for s in range(plan.segments)
                for t in range(strips)
                if 0 <= t + way < strips and 0 <= s + step < plan.segments
            ]
            received.append(lax.ppermute(piece, LINE, pairs))
    return received


def to_segment_below(plan, value):
    return lax.ppermute(value, "segment", [(s, s - 1) for s in range(1, plan.segments)])


def step_kernel(plan, n_received, og_ref, *refs):
    received = refs[:n_received] or None
    refs = refs[n_received:]
    (scale_ref, gain_ref, w_in_ref, w_out_ref, gate_ref, mask_ref, standard_ref, inv_ref, taps_ref) = refs[:9]
    count = 2 * len(plan.distances())
    new_ref, edges = refs[9], refs[10 : 10 + count]
    g_ref, bg_ref, ng_ref, cg_ref, edge_ref = refs[10 + count :]
    load_upstream(plan, g_ref, og_ref, received, edge_ref)
    branch(plan, g_ref, scale_ref, mask_ref, bg_ref)
    for n in range(plan.hidden // plan.part):
        at = pl.ds(n * plan.part, plan.part)
        hidden_grad = contract_last(bg_ref[...], w_out_ref[at, :])
        pre_grad = (hidden_grad * gate_ref[:, at].astype(f32)).astype(bf16)
        term = contract_last(pre_grad, w_in_ref[:, at])
        ng_ref[...] = term if n == 0 else ng_ref[...] + term
    norm_back(plan, ng_ref, gain_ref, standard_ref, inv_ref, cg_ref)
    put_edges(plan, cg_ref, edges)
    for half, block in blocks(plan):
        if block % 2:
            continue
        lanes = pl.ds(half * LANES, LANES)
        rows_at = pl.ds(8 * block, 16)
        parts = [own_sums(plan, cg_ref, taps_ref, half, block + k) for k in range(2)]
        for q in range(plan.width):
            moved = jnp.concatenate([part[q] for part in parts], axis=0)
            new_ref[q, rows_at, lanes] = (g_ref[q, rows_at, lanes].astype(f32) + moved).astype(bf16)


def backward_step(plan, og, received, params, saved):
    scale, gain, w_in, w_out, taps = params
    standard, inv, gate, mask = saved
    c, full, cells = plan.channels, plan.full, plan.cells
    outs = [shape((plan.width, full, c), bf16), *edge_shapes(plan)]
    scratch = [
        pltpu.VMEM((plan.width, full, c), bf16),
        pltpu.VMEM((cells, c), bf16),
        pltpu.VMEM((cells, c), f32),
        pltpu.VMEM((plan.width, full + 2 * PAD, c), f32),
        pltpu.VMEM((plan.padded, full + 2 * PAD, c), f32),
    ]
    return call(
        functools.partial(step_kernel, plan, len(received)),
        "backward",
        [og, *received, scale, gain, w_in, w_out, gate, mask, standard, inv, taps],
        outs,
        scratch,
        4 * cells * c * plan.hidden,
    )


def turn_kernel(hidden_ref, normed_ref, hidden_t_ref, normed_t_ref):
    hidden_t_ref[...] = hidden_ref[...].astype(f32).T.astype(bf16)
    normed_t_ref[...] = normed_ref[...].astype(f32).T.astype(bf16)


def turn(hidden, normed):
    outs = [shape(hidden.shape[::-1], bf16), shape(normed.shape[::-1], bf16)]
    return call(turn_kernel, "turn", [hidden, normed], outs, [], 1000)


def out_share(plan):
    return plan.hidden // plan.cols


def in_share(plan):
    rows = plan.channels // plan.cols
    return rows, plan.hidden // plan.part * rows


def taps_rows(plan):
    return -(-(plan.side**2) // 16) * 16


def put(halves_ref, bit, share, row, value):
    half = bit if share % 2 == 0 else 1 - bit
    halves_ref[half, share // 2, pl.ds(row, value.shape[0]), :] = value


def out_kernel(plan, n_received, og_ref, *refs):
    received = refs[:n_received] or None
    scale_ref, mask_ref, hidden_t_ref, g_ref, bg_ref, halves_ref, send_ref, edge_ref = refs[n_received:]
    load_upstream(plan, g_ref, og_ref, received, edge_ref)
    branch(plan, g_ref, scale_ref, mask_ref, bg_ref)
    bit = lax.rem(lax.axis_index("col"), 2)
    rows = out_share(plan)
    piece = min(plan.part, rows)
    for n in range(plan.hidden // plan.part):
        at = pl.ds(n * plan.part, plan.part)
        grad_out = jnp.dot(hidden_t_ref[at, :], bg_ref[...], preferred_element_type=f32)
        for start in range(0, plan.part, piece):
            unit = n * plan.part + start
            put(halves_ref, bit, unit // rows, unit % rows, grad_out[start : start + piece])
    for u in range(plan.cols // 2):
        send_ref[pl.ds(u * rows, rows), :] = halves_ref[1, u].astype(bf16)


def out_step(plan, og, received, scale, mask, hidden_t):
    c, full, cells, half = plan.channels, plan.full, plan.cells, plan.cols // 2
    rows = out_share(plan)
    outs = [
        shape((plan.width, full, c), bf16),
        shape((cells, c), bf16),
        shape((2, half, rows, c), f32),
        shape((half * rows, c), bf16),
    ]
    return call(
        functools.partial(out_kernel, plan, len(received)),
        "grad_out",
        [og, *received, scale, mask, hidden_t],
        outs,
        [pltpu.VMEM((plan.padded, full + 2 * PAD, c), f32)],
        2 * cells * c * plan.hidden,
    )


def in_kernel(plan, bg_ref, w_in_ref, w_out_ref, gate_ref, normed_t_ref, ng_ref, halves_ref):
    bit = lax.rem(lax.axis_index("col"), 2)
    rows, _ = in_share(plan)
    for n in range(plan.hidden // plan.part):
        at = pl.ds(n * plan.part, plan.part)
        hidden_grad = contract_last(bg_ref[...], w_out_ref[at, :])
        pre_grad = (hidden_grad * gate_ref[:, at].astype(f32)).astype(bf16)
        term = contract_last(pre_grad, w_in_ref[:, at])
        ng_ref[...] = term if n == 0 else ng_ref[...] + term
        grad_in = jnp.dot(normed_t_ref[...], pre_grad, preferred_element_type=f32)
        for share in range(plan.cols):
            put(halves_ref, bit, share, n * rows, grad_in[share * rows : (share + 1) * rows])


def in_step(plan, bg, w_in, w_out, gate, normed_t):
    c, cells = plan.channels, plan.cells
    outs = [shape((cells, c), f32), shape((2, plan.cols // 2, in_share(plan)[1], c), f32)]
    return call(
        functools.partial(in_kernel, plan),
        "grad_in",
        [bg, w_in, w_out, gate, normed_t],
        outs,
        [],
        6 * cells * c * plan.hidden,
    )


def taps_kernel(plan, ng_ref, halves_ref, gain_ref, standard_ref, inv_ref, xw_ref, cg_ref, send_ref, *edges):
    full, width, side = plan.full, plan.width, plan.side
    _, share_rows = in_share(plan)
    norm_back(plan, ng_ref, gain_ref, standard_ref, inv_ref, cg_ref)
    put_edges(plan, cg_ref, edges)
    count = plan.cols // 2
    for u in range(count):
        send_ref[pl.ds(u * share_rows, share_rows), :] = halves_ref[1, u].astype(bf16)
    rows = []
    for i in range(side):
        pieces = [[] for _ in range(side)]
        for half in range(plan.channels // LANES):
            lanes = pl.ds(half * LANES, LANES)
            totals = [jnp.zeros((8, LANES), f32) for _ in range(side)]
            for block in range(full // 8):
                window = xw_ref[:, pl.ds(PAD - plan.margin + i + 8 * block, 8), lanes]
                grad = cg_ref[:, pl.ds(PAD + 8 * block, 8), lanes]
                for j in range(side):
                    totals[j] = totals[j] + jnp.sum(window[j : j + width] * grad, axis=0)
            for j in range(side):
                pieces[j].append(jnp.sum(totals[j], axis=0, keepdims=True))
        rows += [jnp.concatenate(p, axis=-1) for p in pieces]
    rows.append(jnp.zeros((taps_rows(plan) - side**2, plan.channels), f32))
    at = pl.ds(count * share_rows, taps_rows(plan))
    send_ref[at, :] = jnp.concatenate(rows, axis=0).astype(bf16)


def taps_step(plan, norm_grad, halves, gain, standard, inv, xw):
    c, full = plan.channels, plan.full
    outs = [
        shape((plan.width, full + 2 * PAD, c), f32),
        shape((plan.cols // 2 * in_share(plan)[1] + taps_rows(plan), c), bf16),
        *edge_shapes(plan),
    ]
    return call(
        functools.partial(taps_kernel, plan),
        "grad_taps",
        [norm_grad, halves, gain, standard, inv, xw],
        outs,
        [],
        2 * plan.cells * c * plan.side**2,
    )


def finish_kernel(plan, g_ref, cg_ref, taps_ref, *refs):
    edges, (new_ref, edge_ref) = refs[:-2], refs[-2:]
    fill_edges(plan, edge_ref, edges)
    for half, block in blocks(plan):
        if block % 2:
            continue
        lanes = pl.ds(half * LANES, LANES)
        own = [own_sums(plan, cg_ref, taps_ref, half, block + k) for k in range(2)]
        rest = [edge_sums(plan, edge_ref, taps_ref, half, block + k) for k in range(2)]
        r, at = divmod(8 * block, plan.height)
        for q in range(plan.width):
            moved = jnp.concatenate([own[k][q] + rest[k][q] for k in range(2)], axis=0)
            upstream = g_ref[q, pl.ds(8 * block, 16), lanes].astype(f32)
            new_ref[r, q, pl.ds(at, 16), lanes] = (upstream + moved).astype(bf16)


def finish(plan, upstream, conv_grad, taps, edges):
    c = plan.channels
    return call(
        functools.partial(finish_kernel, plan),
        "finish",
        [upstream, conv_grad, taps, *edges],
        [shape((plan.rows, plan.width, plan.height, c), bf16)],
        [pltpu.VMEM((plan.padded, plan.full + 2 * PAD, c), f32)],
        2 * plan.cells * c * plan.side**2,
    )[0]


def swap(value, axis, bit):
    size = lax.axis_size(axis)
    return lax.ppermute(value, axis, [(i, i ^ bit) for i in range(size)])


def combine_kernel(bit, share_rows, extra, keep_ref, sent_ref, got_ref, send_ref, next_ref):
    count = keep_ref.shape[1]
    mine = lax.rem(lax.axis_index("col") // bit, 2)
    for u in range(count // 2):
        for half in range(2):
            share = 2 * u + (mine if half == 0 else 1 - mine)
            at = pl.ds(pl.multiple_of(share * share_rows, 16), share_rows)
            value = keep_ref[0, share] + got_ref[at, :].astype(f32)
            if half == 0:
                next_ref[0, u] = value
            else:
                send_ref[pl.ds(u * share_rows, share_rows), :] = value.astype(bf16)
    if extra:
        old = pl.ds(count * share_rows, extra)
        new = pl.ds(count // 2 * share_rows, extra)
        send_ref[new, :] = (sent_ref[old, :].astype(f32) + got_ref[old, :].astype(f32)).astype(bf16)


def close_kernel(share_rows, extra, keep_ref, sent_ref, got_ref, out_ref):
    at = pl.ds(0, share_rows)
    out_ref[at, :] = (keep_ref[0, 0] + got_ref[at, :].astype(f32)).astype(bf16)
    if extra:
        rest = pl.ds(share_rows, extra)
        out_ref[rest, :] = (sent_ref[rest, :].astype(f32) + got_ref[rest, :].astype(f32)).astype(bf16)


class Reduction:
    def __init__(self, plan, halves, send, share_rows, extra):
        self.plan, self.share_rows, self.extra = plan, share_rows, extra
        self.keep, self.send, self.bit = halves, send, 1
        if plan.cols > 2:
            self.next_stage()

    def next_stage(self):
        c = self.plan.channels
        got = swap(self.send, "col", self.bit)
        self.bit *= 2
        count = self.keep.shape[1] // 2
        self.send, self.keep = call(
            functools.partial(combine_kernel, self.bit, self.share_rows, self.extra),
            "combine",
            [self.keep, self.send, got],
            [
                shape((count * self.share_rows + self.extra, c), bf16),
                shape((1, count, self.share_rows, c), f32),
            ],
            [],
            1000,
        )

    def terms(self):
        plan = self.plan
        while 2 * self.bit < plan.cols:
            self.next_stage()
        got = swap(self.send, "col", self.bit)
        total = call(
            functools.partial(close_kernel, self.share_rows, self.extra),
            "close",
            [self.keep, self.send, got],
            [shape((self.share_rows + self.extra, plan.channels), bf16)],
            [],
            1000,
        )[0]
        terms = [total]
        bit = 1
        while bit < plan.rows:
            terms = [total, swap(total, "row", bit)]
            bit *= 2
            if bit < plan.rows:
                total = (terms[0].astype(f32) + terms[1].astype(f32)).astype(bf16)
        return terms


def read(refs, scale, start, count):
    return scale * sum(ref[pl.ds(start, count), :].astype(f32) for ref in refs)


def out_result_kernel(plan, scale, *refs):
    refs[-1][...] = read(refs[:-1], scale, 0, out_share(plan))


def in_result_kernel(plan, scale, *refs):
    terms, (in_ref, taps_ref) = refs[:-2], refs[-2:]
    rows, share_rows = in_share(plan)
    for n in range(plan.hidden // plan.part):
        in_ref[:, pl.ds(n * plan.part, plan.part)] = read(terms, scale, n * rows, rows)
    sums = read(terms, scale, share_rows, taps_rows(plan))
    for i in range(plan.side):
        taps_ref[i] = sums[i * plan.side : (i + 1) * plan.side]


def out_result(plan, scale, terms):
    kernel = functools.partial(out_result_kernel, plan, scale)
    return call(kernel, "out_result", terms, [shape((out_share(plan), plan.channels), f32)], [], 1000)[0]


def in_result(plan, scale, terms):
    outs = [
        shape((in_share(plan)[0], plan.hidden), f32),
        shape((plan.side, plan.side, plan.channels), f32),
    ]
    return call(functools.partial(in_result_kernel, plan, scale), "in_result", terms, outs, [], 1000)


def to_tile(plan, strips):
    rows, cols = plan.rows, plan.cols
    me = lax.axis_index("row")
    tile = jnp.zeros((rows, *strips.shape[1:]), strips.dtype)
    own = lax.dynamic_index_in_dim(strips, me, 0, keepdims=True)
    tile = lax.dynamic_update_slice_in_dim(tile, own, me, 0)
    for dr in range(1, rows):
        target = lax.rem(me + dr, rows)
        piece = lax.dynamic_index_in_dim(strips, target, 0, keepdims=True)
        got = lax.ppermute(piece, "row", [(r, (r + dr) % rows) for r in range(rows)])
        tile = lax.dynamic_update_slice_in_dim(tile, got, lax.rem(me - dr + rows, rows), 0)
    tile = tile.reshape(plan.across, plan.height, plan.channels)
    return jnp.swapaxes(tile, 0, 1)


def one_crop(plan, norm_scale, tissue, saved, out_grad, params):
    packed, params = pack(plan, tissue, saved, out_grad, params)
    taps, w_in, w_out, conv_bias, gain, bias, b_in, scale = params
    pieces = exchange(plan, packed)
    taps_above = to_segment_below(plan, taps)
    og, xw, mask, standard, inv, gate, hidden, normed = forward(
        plan, pieces, taps, conv_bias, gain, bias, w_in, b_in
    )
    step_params, kept = (scale, gain, w_in, w_out, taps), (standard, inv, gate, mask)
    received, turned = [], None
    for _ in range(plan.segments - 1):
        own, *edges = backward_step(plan, og, received, step_params, kept)
        received = [taps_above, to_segment_below(plan, own), *send_edges(plan, edges, -1)]
        if turned is None:
            hidden, normed, _ = lax.optimization_barrier((hidden, normed, own))
            turned = turn(hidden, normed)
    hidden_t, normed_t = turned if turned is not None else turn(hidden, normed)
    upstream, branch_grad, halves, send = out_step(plan, og, received, scale, mask, hidden_t)
    out_sum = Reduction(plan, halves, send, out_share(plan), 0)
    norm_grad, halves = in_step(plan, branch_grad, w_in, w_out, gate, normed_t)
    norm_grad, _ = lax.optimization_barrier((norm_grad, out_sum.send))
    conv_grad, send, *edges = taps_step(plan, norm_grad, halves, gain, standard, inv, xw)
    in_sum = Reduction(plan, halves, send, in_share(plan)[1], taps_rows(plan))
    grad_out = out_result(plan, norm_scale, out_sum.terms())
    strips = finish(plan, upstream, conv_grad, taps, send_edges(plan, edges, 0))
    grad_in, grad_taps = in_result(plan, norm_scale, in_sum.terms())
    return to_tile(plan, strips), grad_in, grad_out, grad_taps


def per_device(
    saved_inputs,
    out_grad,
    tissue,
    conv_taps,
    conv_bias,
    norm_gain,
    norm_bias,
    w_in,
    b_in,
    w_out,
    layer_scale,
):
    crop_count, height, across, channels = out_grad.shape
    plan = Plan(
        lax.axis_size("segment"),
        lax.axis_size("row"),
        lax.axis_size("col"),
        height,
        across,
        channels,
        w_in.shape[2],
        conv_taps.shape[1],
    )
    norm_scale = 1.0 / math.sqrt(crop_count * plan.full * across * plan.cols)
    params = (conv_taps[0], w_in[0], w_out[0], conv_bias, norm_gain, norm_bias, b_in, layer_scale)
    results = [
        one_crop(plan, norm_scale, tissue[crop], saved_inputs[0, crop], out_grad[crop], params)
        for crop in range(crop_count)
    ]
    grads, *weights = zip(*results)
    grad_in, grad_out, grad_taps = (sum(w[1:], w[0]) for w in weights)
    return (jnp.stack(grads)[None], grad_in[None], grad_out[None], grad_taps[None])


def solution(mesh):
    return jax.shard_map(
        per_device,
        mesh=mesh,
        in_specs=(
            P("segment", None, "row", "col", None),
            P(None, "row", "col", None),
            P(None, "row", "col"),
            P("segment", None, None, None),
            P("segment", None),
            P("segment", None),
            P("segment", None),
            P("segment", None, None),
            P("segment", None),
            P("segment", None, None),
            P("segment", None),
        ),
        out_specs=(
            P("segment", None, "row", "col", None),
            P("segment", "col", None),
            P("segment", "col", None),
            P("segment", None, None, None),
        ),
        check_vma=False,
    )
```

time: 504 us -> 100 us (0.20); the launches traced: 497 us -> 99.3 us
  local copies, waits for them, and re-layouts: 207 us -> 6.18 us
  other arithmetic: 76.9 us -> 0 us
  waiting for transfers between devices: 81.1 us -> 25.5 us
  starting transfers between devices: 80.8 us -> 41.1 us
  blocking collectives: 27.9 us -> 0 us
  Pallas kernels: 0 us -> 25 us
  between operations: 14.8 us -> 1.61 us
  loops' own time: 5.84 us -> 0 us
    mul x192 -> x0, local copies, waits for them, and re-layouts: 163 us -> none  [the longest x188 157 us: depthwise(): conv_taps[shift_r, shift_c]]
    psum x1 -> x0, waiting for transfers between devices: 50 us -> none  [per_device(): lax.psum((sum_in, sum_out, sum_taps), ('row', 'col'))]
    ppermute x24 -> x22, starting transfers between devices: 80.7 us -> 41.1 us  [the longest x8 19.5 us: send_edges(): received.append(lax.ppermute(piece, LINE, pairs))]
    psum x1 -> x0, blocking collectives: 27.9 us -> none  [per_device(): lax.psum((sum_in, sum_out, sum_taps), ('row', 'col'))]
    convert_element_type x14 -> x0, other arithmetic: 25.7 us -> none  [the longest x12 25 us: depthwise(): total = total + conv_taps[shift_r, shift_c] * padded[shift_r:shift_r + he...]
    slice x25 -> x0, local copies, waits for them, and re-layouts: 25 us -> none  [the longest x12 14.9 us: depthwise(): conv_taps[shift_r, shift_c]]
    pallas_call x0 -> x16, Pallas kernels: none -> 25 us  [the longest x15 24.2 us: call(): pl.pallas_call(kernel, out_shape=outs, in_specs=[vmem()] * len(operands),...]
    reduce_sum x14 -> x0, other arithmetic: 17 us -> none  [the longest x1 8.74 us: normalize(): average = jnp.mean(conv_out, axis=-1, keepdims=True)]
  transfers between devices with their start and end apart: 25 -> 22, of which waited for: 8 -> 11; matrix products, arithmetic and copies ran while one was open for 5% -> 0% of each run, Pallas kernels for 0% -> 5%
where the time goes in v1:
time: 100 us; the launch traced here: 99.3 us
  starting transfers between devices  41.1 us (41%)
  waiting for transfers between devices  25.5 us (26%)
  Pallas kernels  25 us (25%)
  local copies, waits for them, and re-layouts  6.18 us (6%)
  between operations  1.61 us (2%)
    pallas_call x15, Pallas kernels, call(): pl.pallas_call(kernel, out_shape=outs, in_specs=[vmem()] * len(operands),...  24.2 us
    ppermute x8, starting transfers between devices, send_edges(): received.append(lax.ppermute(piece, LINE, pairs))  19.5 us
    ppermute x8, waiting for transfers between devices, send_edges(): received.append(lax.ppermute(piece, LINE, pairs))  15.1 us
    ppermute x6, waiting for transfers between devices, swap(): return lax.ppermute(value, axis, [(i, i ^ bit) for i in range(size)])  8.91 us
    ppermute x4, starting transfers between devices, to_segment_below(): lax.ppermute(value, 'segment', [(s, s - 1) for s in range(1, plan.segment...  8.56 us
    ppermute x2, starting transfers between devices, exchange(): sides.append(lax.ppermute(pieces[rows * (1 + k) + dr], LINE, pairs))  6.54 us
    unnamed x22, local copies, waits for them, and re-layouts  6.09 us
    ppermute x6, starting transfers between devices, swap(): return lax.ppermute(value, axis, [(i, i ^ bit) for i in range(size)])  3.82 us
  transfers between devices with their start and end apart: 22, of which 11 were waited for; matrix products, arithmetic and copies ran while one was open for 0% of the time, Pallas kernels for 5%

profile of v1, /device:TPU:18, one launch (start us, length us, event | category | flops | bytes accessed | tf_op | source)
XLA Modules:
  0.0 99.3 jit_solution(6263481924246463311)
XLA Ops:
  0.6 0.8 copy.21
  2.2 0.6 copy-done.8
  2.8 1.0 %copy-done = bf16[1,256,1024]{2,1,0:T(8,128)(2,1)S(1)} copy-done((bf16[1,256,1024]{2,1,0:T(8,128)(2,1)S(1)}, bf16[1,256,1024]{2,1,0:T(8,128)(2,1)}, u32[]{:S(2)}) %copy-start) | copy-done | bytes 524312
  3.9 1.0 %copy-done.1 = bf16[1,1024,256]{2,1,0:T(8,128)(2,1)S(1)} copy-done((bf16[1,1024,256]{2,1,0:T(8,128)(2,1)S(1)}, bf16[1,1024,256]{2,1,0:T(8,128)(2,1)}, u32[]{:S(2)}) %copy-start.1) | copy-done | bytes 524312
  4.9 0.9 copy-done.2
  5.8 0.9 copy-done.3
  6.7 0.8 pack.1
  7.5 0.6 collective-permute-start
  8.1 1.3 %collective-permute-start.1 = (bf16[3,16,256]{2,1,0:T(8,128)(2,1)S(1)}, bf16[3,16,256]{2,1,0:T(8,128)(2,1)S(1)}, u32[]{:S(2)}, u32[]{:S(2)}) collective-permute-start(bf16[3,16,256]{2,1,0:T(8,128)(2,1)S(1)} %get-tuple-element.56), channel_id=1, source_target_pairs={{0,1},{1,2},{2,3},{5,4},{6,5},{7,6},{8,9},{9,10},{10,11},{13,12},{... | collective-permute-start | bytes 73736 | tf_op jit(solution)/shard_map/ppermute | solution.py:183
  9.4 5.3 %collective-permute-start.2 = (bf16[3,16,256]{2,1,0:T(8,128)(2,1)S(1)}, bf16[3,16,256]{2,1,0:T(8,128)(2,1)S(1)}, u32[]{:S(2)}, u32[]{:S(2)}) collective-permute-start(bf16[3,16,256]{2,1,0:T(8,128)(2,1)S(1)} %get-tuple-element.57), channel_id=1, source_target_pairs={{4,1},{5,2},{6,3},{1,4},{2,5},{3,6},{12,9},{13,10},{14,11},{9,12},... | collective-permute-start | bytes 73736 | tf_op jit(solution)/shard_map/ppermute | solution.py:183
  14.7 1.5 %collective-permute-done.2.refs_3_ = bf16[3,16,256]{2,1,0:T(8,128)(2,1)S(1)} collective-permute-done((bf16[3,16,256]{2,1,0:T(8,128)(2,1)S(1)}, bf16[3,16,256]{2,1,0:T(8,128)(2,1)S(1)}, u32[]{:S(2)}, u32[]{:S(2)}) %collective-permute-start.2) | collective-permute-done | bytes 24608 | tf_op jit(solution)/shard_map/ppermute | solution.py:183
  16.2 3.6 %forward.1 = (bf16[8,32,256]{2,1,0:T(8,128)(2,1)S(1)}, f32[14,48,256]{2,1,0:T(8,128)S(1)}, f32[256,128]{1,0:T(8,128)S(1)}, f32[256,256]{1,0:T(8,128)S(1)}, f32[2...) custom-call(bf16[20,16,256]{2,1,0:T(8,128)(2,1)S(1)} %get-tuple-elem, ...), custom_call_target="tpu_custom_call" | custom-call | flops 134217728 | bytes 3481600 | tf_op jit(solution)/shard_map/forward/pallas_call | solution.py:89
  19.8 3.4 %backward.3 = (bf16[8,32,256]{2,1,0:T(8,128)(2,1)S(1)}, bf16[3,32,256]{2,1,0:T(8,128)(2,1)S(1)}, bf16[3,32,256]{2,1,0:T(8,128)(2,1)S(1)}) custom-call(bf16[8,32,256]{2,1,0:T(8,128)(2,1)S(1)} %get-tuple-element.64.og_ref, f32[1,256]{1,0:T(1,128)S(1)} %get-tuple-element.65.refs_0_.refs_4_, f32[1,256]{1,0:T(1,128)S(1)} %get-tuple-element.60.refs_6_.refs_1_.refs_5_.gain_ref, ...), custom_call_target="tpu_custom_call" | custom-call | flops 268435456 | bytes 2509824 | tf_op jit(solution)/shard_map/backward/pallas_call | solution.py:89
  23.1 2.4 %collective-permute-start.4 = (bf16[8,32,256]{2,1,0:T(8,128)(2,1)S(1)}, bf16[8,32,256]{2,1,0:T(8,128)(2,1)S(1)}, u32[]{:S(2)}, u32[]{:S(2)}) collective-permute-start(bf16[8,32,256]{2,1,0:T(8,128)(2,1)S(1)} %get-tuple-element.71), channel_id=1, source_target_pairs={{8,0},{16,8},{24,16},{9,1},{17,9},{25,17},{10,2},{18,10},{26,18},{... | collective-permute-start | bytes 393224 | tf_op jit(solution)/shard_map/ppermute | solution.py:425
  25.5 2.4 %collective-permute-start.3 = (f32[7,7,256]{2,1,0:T(8,128)S(1)}, f32[7,7,256]{2,1,0:T(8,128)S(1)}, u32[]{:S(2)}, u32[]{:S(2)}) collective-permute-start(f32[7,7,256]{2,1,0:T(8,128)S(1)} %get-tuple-element.58.refs_4_.refs_8_.refs_12_.taps_ref), channel_id=1, source_target_pairs={{8,0},{16,8},{24,16},{9,1},{17,9},{25,17},{10,2},{18,10},{26,18},{... | collective-permute-start | bytes 150536 | tf_op jit(solution)/shard_map/ppermute | solution.py:425
  27.9 2.8 %collective-permute-start.5 = (bf16[3,32,256]{2,1,0:T(8,128)(2,1)S(1)}, bf16[3,32,256]{2,1,0:T(8,128)(2,1)S(1)}, u32[]{:S(2)}, u32[]{:S(2)}) collective-permute-start(bf16[3,32,256]{2,1,0:T(8,128)(2,1)S(1)} %get-tuple-element.72), channel_id=1, source_target_pairs={{8,4},{12,1},{9,5},{13,2},{10,6},{14,3},{11,7},{16,12},{20,9},{17,... | collective-permute-start | bytes 147464 | tf_op jit(solution)/shard_map/ppermute | solution.py:420
  30.7 2.1 %collective-permute-start.6 = (bf16[3,32,256]{2,1,0:T(8,128)(2,1)S(1)}, bf16[3,32,256]{2,1,0:T(8,128)(2,1)S(1)}, u32[]{:S(2)}, u32[]{:S(2)}) collective-permute-start(bf16[3,32,256]{2,1,0:T(8,128)(2,1)S(1)} %get-tuple-element.73), channel_id=1, source_target_pairs={{12,0},{9,4},{13,1},{10,5},{14,2},{11,6},{15,3},{20,8},{17,12},{21... | collective-permute-start | bytes 147464 | tf_op jit(solution)/shard_map/ppermute | solution.py:420
  32.8 1.9 %collective-permute-done.5.refs_2_ = bf16[3,32,256]{2,1,0:T(8,128)(2,1)S(1)} collective-permute-done((bf16[3,32,256]{2,1,0:T(8,128)(2,1)S(1)}, bf16[3,32,256]{2,1,0:T(8,128)(2,1)S(1)}, u32[]{:S(2)}, u32[]{:S(2)}) %collective-permute-start.5) | collective-permute-done | bytes 49184 | tf_op jit(solution)/shard_map/ppermute | solution.py:420
  34.8 2.2 %collective-permute-done.6.refs_3_ = bf16[3,32,256]{2,1,0:T(8,128)(2,1)S(1)} collective-permute-done((bf16[3,32,256]{2,1,0:T(8,128)(2,1)S(1)}, bf16[3,32,256]{2,1,0:T(8,128)(2,1)S(1)}, u32[]{:S(2)}, u32[]{:S(2)}) %collective-permute-start.6) | collective-permute-done | bytes 49184 | tf_op jit(solution)/shard_map/ppermute | solution.py:420
  37.0 4.0 %backward.4 = (bf16[8,32,256]{2,1,0:T(8,128)(2,1)S(1)}, bf16[3,32,256]{2,1,0:T(8,128)(2,1)S(1)}, bf16[3,32,256]{2,1,0:T(8,128)(2,1)S(1)}) custom-call(bf16[8,32,256]{2,1,0:T(8,128)(2,1)S(1)} %get-tuple-element.64.og_ref, f32[7,7,256]{2,1,0:T(8,128)S(1)} %collective-permute-done.3.refs_0_, bf16[8,32,256]{2,1,0:T(8,128)(2,1)S(1)} %collective-permute-done.4.refs_1_, ...), custom_call_target="tpu_custom_call" | custom-call | flops 268435456 | bytes 2789376 | tf_op jit(solution)/shard_map/backward/pallas_call | solution.py:89
  41.0 1.9 %collective-permute-start.7 = (bf16[8,32,256]{2,1,0:T(8,128)(2,1)S(1)}, bf16[8,32,256]{2,1,0:T(8,128)(2,1)S(1)}, u32[]{:S(2)}, u32[]{:S(2)}) collective-permute-start(bf16[8,32,256]{2,1,0:T(8,128)(2,1)S(1)} %get-tuple-element.74), channel_id=1, source_target_pairs={{8,0},{16,8},{24,16},{9,1},{17,9},{25,17},{10,2},{18,10},{26,18},{... | collective-permute-start | bytes 393224 | tf_op jit(solution)/shard_map/ppermute | solution.py:425
  42.9 2.4 %collective-permute-start.8 = (bf16[3,32,256]{2,1,0:T(8,128)(2,1)S(1)}, bf16[3,32,256]{2,1,0:T(8,128)(2,1)S(1)}, u32[]{:S(2)}, u32[]{:S(2)}) collective-permute-start(bf16[3,32,256]{2,1,0:T(8,128)(2,1)S(1)} %get-tuple-element.75), channel_id=1, source_target_pairs={{8,4},{12,1},{9,5},{13,2},{10,6},{14,3},{11,7},{16,12},{20,9},{17,... | collective-permute-start | bytes 147464 | tf_op jit(solution)/shard_map/ppermute | solution.py:420
  45.4 1.9 %collective-permute-start.9 = (bf16[3,32,256]{2,1,0:T(8,128)(2,1)S(1)}, bf16[3,32,256]{2,1,0:T(8,128)(2,1)S(1)}, u32[]{:S(2)}, u32[]{:S(2)}) collective-permute-start(bf16[3,32,256]{2,1,0:T(8,128)(2,1)S(1)} %get-tuple-element.76), channel_id=1, source_target_pairs={{12,0},{9,4},{13,1},{10,5},{14,2},{11,6},{15,3},{20,8},{17,12},{21... | collective-permute-start | bytes 147464 | tf_op jit(solution)/shard_map/ppermute | solution.py:420
  47.3 2.5 %collective-permute-done.8.refs_2_ = bf16[3,32,256]{2,1,0:T(8,128)(2,1)S(1)} collective-permute-done((bf16[3,32,256]{2,1,0:T(8,128)(2,1)S(1)}, bf16[3,32,256]{2,1,0:T(8,128)(2,1)S(1)}, u32[]{:S(2)}, u32[]{:S(2)}) %collective-permute-start.8) | collective-permute-done | bytes 49184 | tf_op jit(solution)/shard_map/ppermute | solution.py:420
  49.8 2.3 %collective-permute-done.9.refs_3_ = bf16[3,32,256]{2,1,0:T(8,128)(2,1)S(1)} collective-permute-done((bf16[3,32,256]{2,1,0:T(8,128)(2,1)S(1)}, bf16[3,32,256]{2,1,0:T(8,128)(2,1)S(1)}, u32[]{:S(2)}, u32[]{:S(2)}) %collective-permute-start.9) | collective-permute-done | bytes 49184 | tf_op jit(solution)/shard_map/ppermute | solution.py:420
  52.1 4.0 %backward.5 = (bf16[8,32,256]{2,1,0:T(8,128)(2,1)S(1)}, bf16[3,32,256]{2,1,0:T(8,128)(2,1)S(1)}, bf16[3,32,256]{2,1,0:T(8,128)(2,1)S(1)}) custom-call(bf16[8,32,256]{2,1,0:T(8,128)(2,1)S(1)} %get-tuple-element.64.og_ref, f32[7,7,256]{2,1,0:T(8,128)S(1)} %collective-permute-done.3.refs_0_, bf16[8,32,256]{2,1,0:T(8,128)(2,1)S(1)} %collective-permute-done.7.refs_1_, ...), custom_call_target="tpu_custom_call" | custom-call | flops 268435456 | bytes 2789376 | tf_op jit(solution)/shard_map/backward/pallas_call | solution.py:89
  56.1 1.9 %collective-permute-start.10 = (bf16[8,32,256]{2,1,0:T(8,128)(2,1)S(1)}, bf16[8,32,256]{2,1,0:T(8,128)(2,1)S(1)}, u32[]{:S(2)}, u32[]{:S(2)}) collective-permute-start(bf16[8,32,256]{2,1,0:T(8,128)(2,1)S(1)} %get-tuple-element.77), channel_id=1, source_target_pairs={{8,0},{16,8},{24,16},{9,1},{17,9},{25,17},{10,2},{18,10},{26,18},{... | collective-permute-start | bytes 393224 | tf_op jit(solution)/shard_map/ppermute | solution.py:425
  58.0 2.3 %collective-permute-start.11 = (bf16[3,32,256]{2,1,0:T(8,128)(2,1)S(1)}, bf16[3,32,256]{2,1,0:T(8,128)(2,1)S(1)}, u32[]{:S(2)}, u32[]{:S(2)}) collective-permute-start(bf16[3,32,256]{2,1,0:T(8,128)(2,1)S(1)} %get-tuple-element.78), channel_id=1, source_target_pairs={{8,4},{12,1},{9,5},{13,2},{10,6},{14,3},{11,7},{16,12},{20,9},{17,... | collective-permute-start | bytes 147464 | tf_op jit(solution)/shard_map/ppermute | solution.py:420
  60.3 2.1 %collective-permute-start.12 = (bf16[3,32,256]{2,1,0:T(8,128)(2,1)S(1)}, bf16[3,32,256]{2,1,0:T(8,128)(2,1)S(1)}, u32[]{:S(2)}, u32[]{:S(2)}) collective-permute-start(bf16[3,32,256]{2,1,0:T(8,128)(2,1)S(1)} %get-tuple-element.79), channel_id=1, source_target_pairs={{12,0},{9,4},{13,1},{10,5},{14,2},{11,6},{15,3},{20,8},{17,12},{21... | collective-permute-start | bytes 147464 | tf_op jit(solution)/shard_map/ppermute | solution.py:420
  62.7 2.2 %collective-permute-done.11.refs_2_ = bf16[3,32,256]{2,1,0:T(8,128)(2,1)S(1)} collective-permute-done((bf16[3,32,256]{2,1,0:T(8,128)(2,1)S(1)}, bf16[3,32,256]{2,1,0:T(8,128)(2,1)S(1)}, u32[]{:S(2)}, u32[]{:S(2)}) %collective-permute-start.11) | collective-permute-done | bytes 49184 | tf_op jit(solution)/shard_map/ppermute | solution.py:420
  64.9 2.3 %collective-permute-done.12.refs_3_ = bf16[3,32,256]{2,1,0:T(8,128)(2,1)S(1)} collective-permute-done((bf16[3,32,256]{2,1,0:T(8,128)(2,1)S(1)}, bf16[3,32,256]{2,1,0:T(8,128)(2,1)S(1)}, u32[]{:S(2)}, u32[]{:S(2)}) %collective-permute-start.12) | collective-permute-done | bytes 49184 | tf_op jit(solution)/shard_map/ppermute | solution.py:420
  67.1 1.1 %grad_out.1 = (bf16[8,32,256]{2,1,0:T(8,128)(2,1)S(1)}, bf16[256,256]{1,0:T(8,128)(2,1)S(1)}, f32[2,2,256,256]{3,2,1,0:T(8,128)S(1)}, bf16[512,256]{1,0:T(8,128)(2,1)S(1)}) custom-call(bf16[8,32,256]{2,1,0:T(8,128)(2,1)S(1)} %get-tuple-element.64.og_ref, f32[7,7,256]{2,1,0:T(8,128)S(1)} %collective-permute-done.3.refs_0_, ...), custom_call_target="tpu_custom_call" | custom-call | flops 134217728 | bytes 2639872 | tf_op jit(solution)/shard_map/grad_out/pallas_call | solution.py:89
  68.3 2.0 %collective-permute-start.13 = (bf16[512,256]{1,0:T(8,128)(2,1)S(1)}, bf16[512,256]{1,0:T(8,128)(2,1)S(1)}, u32[]{:S(2)}, u32[]{:S(2)}) collective-permute-start(bf16[512,256]{1,0:T(8,128)(2,1)S(1)} %get-tuple-element.90.sent_ref), channel_id=1, source_target_pairs={{0,1},{1,0},{2,3},{3,2},{4,5},{5,4},{6,7},{7,6},{8,9},{9,8},{10,11... | collective-permute-start | bytes 786440 | tf_op jit(solution)/shard_map/ppermute | solution.py:644
  70.2 1.1 %grad_in.1 = (f32[256,256]{1,0:T(8,128)S(1)}, f32[2,2,256,256]{3,2,1,0:T(8,128)S(1)}) custom-call(bf16[256,256]{1,0:T(8,128)(2,1)S(1)} %get-tuple-element.86.bg_ref, bf16[256,1024]{1,0:T(8,128)(2,1)S(1)} %get-tuple-element.62.refs_8_.refs_2_.refs_6_.w_in_ref, bf16[1024,256]{1,0:T(8,128)(2,1)S(1)} %get-tuple-element.66.refs_3_.refs_7_.w_out_ref, ...), custom_call_target="tpu_custom_call" | custom-call | flops 402653184 | bytes 3145728 | tf_op jit(solution)/shard_map/grad_in/pallas_call | solution.py:89
  71.4 2.6 %grad_taps.1 = (f32[8,48,256]{2,1,0:T(8,128)S(1)}, bf16[576,256]{1,0:T(8,128)(2,1)S(1)}, bf16[3,32,256]{2,1,0:T(8,128)(2,1)S(1)}, bf16[3,32,256]{2,1,0:T(8,128)(2,1)S(1)}) custom-call(f32[256,256]{1,0:T(8,128)S(1)} %get-tuple-element.92.ng_ref, f32[2,2,256,256]{3,2,1,0:T(8,128)S(1)} %get-tuple-element.93.halves_ref.keep_ref, ...), custom_call_target="tpu_custom_call" | custom-call | flops 6422528 | bytes 3179520 | tf_op jit(solution)/shard_map/grad_taps/pallas_call | solution.py:89
  74.0 0.4 collective-permute-start.17
  74.5 1.9 %collective-permute-start.14 = (bf16[3,32,256]{2,1,0:T(8,128)(2,1)S(1)}, bf16[3,32,256]{2,1,0:T(8,128)(2,1)S(1)}, u32[]{:S(2)}, u32[]{:S(2)}) collective-permute-start(bf16[3,32,256]{2,1,0:T(8,128)(2,1)S(1)} %get-tuple-element.96), channel_id=1, source_target_pairs={{0,4},{4,1},{1,5},{5,2},{2,6},{6,3},{3,7},{8,12},{12,9},{9,13},{13... | collective-permute-start | bytes 147464 | tf_op jit(solution)/shard_map/ppermute | solution.py:420
  76.4 3.9 %collective-permute-start.15 = (bf16[3,32,256]{2,1,0:T(8,128)(2,1)S(1)}, bf16[3,32,256]{2,1,0:T(8,128)(2,1)S(1)}, u32[]{:S(2)}, u32[]{:S(2)}) collective-permute-start(bf16[3,32,256]{2,1,0:T(8,128)(2,1)S(1)} %get-tuple-element.97), channel_id=1, source_target_pairs={{4,0},{1,4},{5,1},{2,5},{6,2},{3,6},{7,3},{12,8},{9,12},{13,9},{10... | collective-permute-start | bytes 147464 | tf_op jit(solution)/shard_map/ppermute | solution.py:420
  80.4 1.6 %collective-permute-done.15.refs_1_ = bf16[3,32,256]{2,1,0:T(8,128)(2,1)S(1)} collective-permute-done((bf16[3,32,256]{2,1,0:T(8,128)(2,1)S(1)}, bf16[3,32,256]{2,1,0:T(8,128)(2,1)S(1)}, u32[]{:S(2)}, u32[]{:S(2)}) %collective-permute-start.15) | collective-permute-done | bytes 49184 | tf_op jit(solution)/shard_map/ppermute | solution.py:420
  82.0 2.6 %finish.1 = bf16[2,8,16,256]{3,2,1,0:T(8,128)(2,1)S(1)} custom-call(bf16[8,32,256]{2,1,0:T(8,128)(2,1)S(1)} %get-tuple-element.85.g_ref, f32[8,48,256]{2,1,0:T(8,128)S(1)} %get-tuple-element.95.cg_ref, f32[7,7,256]{2,1,0:T(8,128)S(1)} %get-tuple-element.58.refs_4_.refs_8_.refs_12_.taps_ref, bf16[3,32,256]{2,1,0:T(8,128)(2,1)S(1)} %collective-permute-done.14.refs_0_, ...), custom_call_target="tpu_custom_call" | custom-call | flops 6422528 | bytes 803840 | tf_op jit(solution)/shard_map/finish/pallas_call | solution.py:89
  84.7 0.4 collective-permute-start.18
  85.2 2.0 %collective-permute-start.16 = (bf16[1,8,16,256]{3,2,1,0:T(8,128)(2,1)S(1)}, bf16[1,8,16,256]{3,2,1,0:T(8,128)(2,1)S(1)}, u32[]{:S(2)}, u32[]{:S(2)}) collective-permute-start(bf16[1,8,16,256]{3,2,1,0:T(8,128)(2,1)S(1)} %get-tuple-element.108), channel_id=1, source_target_pairs={{0,4},{4,0},{1,5},{5,1},{2,6},{6,2},{3,7},{7,3},{8,12},{12,8},{9,1... | collective-permute-start | bytes 196616 | tf_op jit(solution)/shard_map/ppermute | solution.py:760
  87.5 4.3 %collective-permute-done.18.got_ref = bf16[320,256]{1,0:T(8,128)(2,1)S(1)} collective-permute-done((bf16[320,256]{1,0:T(8,128)(2,1)S(1)}, bf16[320,256]{1,0:T(8,128)(2,1)S(1)}, u32[]{:S(2)}, u32[]{:S(2)}) %collective-permute-start.18) | collective-permute-done | bytes 163872 | tf_op jit(solution)/shard_map/ppermute | solution.py:644
  91.8 0.8 collective-permute-start.19
  92.6 0.7 out_result.1
  93.4 4.6 %collective-permute-done.19.refs_1_ = bf16[320,256]{1,0:T(8,128)(2,1)S(1)} collective-permute-done((bf16[320,256]{1,0:T(8,128)(2,1)S(1)}, bf16[320,256]{1,0:T(8,128)(2,1)S(1)}, u32[]{:S(2)}, u32[]{:S(2)}) %collective-permute-start.19) | collective-permute-done | bytes 163872 | tf_op jit(solution)/shard_map/ppermute | solution.py:644
  97.9 0.7 in_result.1
  98.7 0.7 copy.17
  (38 shorter events, 1.0 us)
Async XLA Ops:
  2.1 0.7 copy-start.8
  2.1 0.7 copy-start.4
  2.1 0.7 copy-start.6
  2.1 0.7 copy-start.7
  2.1 0.7 copy-start.5
  2.8 1.0 %copy-start = (bf16[1,256,1024]{2,1,0:T(8,128)(2,1)S(1)}, bf16[1,256,1024]{2,1,0:T(8,128)(2,1)}, u32[]{:S(2)}) copy-start(bf16[1,256,1024]{2,1,0:T(8,128)(2,1)} %param.18) | copy-start | bytes 1572868
  3.9 1.0 %copy-start.1 = (bf16[1,1024,256]{2,1,0:T(8,128)(2,1)S(1)}, bf16[1,1024,256]{2,1,0:T(8,128)(2,1)}, u32[]{:S(2)}) copy-start(bf16[1,1024,256]{2,1,0:T(8,128)(2,1)} %param.20) | copy-start | bytes 1572868
  4.9 0.9 copy-start.2
  5.8 0.9 copy-start.3
  7.5 8.7 %collective-permute-start = (bf16[20,16,256]{2,1,0:T(8,128)(2,1)S(1)}, bf16[20,16,256]{2,1,0:T(8,128)(2,1)S(1)}, u32[]{:S(2)}, u32[]{:S(2)}) collective-permute-start(bf16[20,16,256]{2,1,0:T(8,128)(2,1)S(1)} %get-tuple-element.55), channel_id=1, source_target_pairs={{4,0},{5,1},{6,2},{7,3},{0,4},{1,5},{2,6},{3,7},{12,8},{13,9},{14,... | collective-permute-start | bytes 491528 | tf_op jit(solution)/shard_map/ppermute | solution.py:190
  8.1 6.6 %collective-permute-start.1 = (bf16[3,16,256]{2,1,0:T(8,128)(2,1)S(1)}, bf16[3,16,256]{2,1,0:T(8,128)(2,1)S(1)}, u32[]{:S(2)}, u32[]{:S(2)}) collective-permute-start(bf16[3,16,256]{2,1,0:T(8,128)(2,1)S(1)} %get-tuple-element.56), channel_id=1, source_target_pairs={{0,1},{1,2},{2,3},{5,4},{6,5},{7,6},{8,9},{9,10},{10,11},{13,12},{... | collective-permute-start | bytes 73736 | tf_op jit(solution)/shard_map/ppermute | solution.py:183
  9.4 6.8 %collective-permute-start.2 = (bf16[3,16,256]{2,1,0:T(8,128)(2,1)S(1)}, bf16[3,16,256]{2,1,0:T(8,128)(2,1)S(1)}, u32[]{:S(2)}, u32[]{:S(2)}) collective-permute-start(bf16[3,16,256]{2,1,0:T(8,128)(2,1)S(1)} %get-tuple-element.57), channel_id=1, source_target_pairs={{4,1},{5,2},{6,3},{1,4},{2,5},{3,6},{12,9},{13,10},{14,11},{9,12},... | collective-permute-start | bytes 73736 | tf_op jit(solution)/shard_map/ppermute | solution.py:183
  23.1 13.9 %collective-permute-start.4 = (bf16[8,32,256]{2,1,0:T(8,128)(2,1)S(1)}, bf16[8,32,256]{2,1,0:T(8,128)(2,1)S(1)}, u32[]{:S(2)}, u32[]{:S(2)}) collective-permute-start(bf16[8,32,256]{2,1,0:T(8,128)(2,1)S(1)} %get-tuple-element.71), channel_id=1, source_target_pairs={{8,0},{16,8},{24,16},{9,1},{17,9},{25,17},{10,2},{18,10},{26,18},{... | collective-permute-start | bytes 393224 | tf_op jit(solution)/shard_map/ppermute | solution.py:425
  25.5 7.3 %collective-permute-start.3 = (f32[7,7,256]{2,1,0:T(8,128)S(1)}, f32[7,7,256]{2,1,0:T(8,128)S(1)}, u32[]{:S(2)}, u32[]{:S(2)}) collective-permute-start(f32[7,7,256]{2,1,0:T(8,128)S(1)} %get-tuple-element.58.refs_4_.refs_8_.refs_12_.taps_ref), channel_id=1, source_target_pairs={{8,0},{16,8},{24,16},{9,1},{17,9},{25,17},{10,2},{18,10},{26,18},{... | collective-permute-start | bytes 150536 | tf_op jit(solution)/shard_map/ppermute | solution.py:425
  27.9 6.9 %collective-permute-start.5 = (bf16[3,32,256]{2,1,0:T(8,128)(2,1)S(1)}, bf16[3,32,256]{2,1,0:T(8,128)(2,1)S(1)}, u32[]{:S(2)}, u32[]{:S(2)}) collective-permute-start(bf16[3,32,256]{2,1,0:T(8,128)(2,1)S(1)} %get-tuple-element.72), channel_id=1, source_target_pairs={{8,4},{12,1},{9,5},{13,2},{10,6},{14,3},{11,7},{16,12},{20,9},{17,... | collective-permute-start | bytes 147464 | tf_op jit(solution)/shard_map/ppermute | solution.py:420
  30.7 6.3 %collective-permute-start.6 = (bf16[3,32,256]{2,1,0:T(8,128)(2,1)S(1)}, bf16[3,32,256]{2,1,0:T(8,128)(2,1)S(1)}, u32[]{:S(2)}, u32[]{:S(2)}) collective-permute-start(bf16[3,32,256]{2,1,0:T(8,128)(2,1)S(1)} %get-tuple-element.73), channel_id=1, source_target_pairs={{12,0},{9,4},{13,1},{10,5},{14,2},{11,6},{15,3},{20,8},{17,12},{21... | collective-permute-start | bytes 147464 | tf_op jit(solution)/shard_map/ppermute | solution.py:420
  41.0 11.1 %collective-permute-start.7 = (bf16[8,32,256]{2,1,0:T(8,128)(2,1)S(1)}, bf16[8,32,256]{2,1,0:T(8,128)(2,1)S(1)}, u32[]{:S(2)}, u32[]{:S(2)}) collective-permute-start(bf16[8,32,256]{2,1,0:T(8,128)(2,1)S(1)} %get-tuple-element.74), channel_id=1, source_target_pairs={{8,0},{16,8},{24,16},{9,1},{17,9},{25,17},{10,2},{18,10},{26,18},{... | collective-permute-start | bytes 393224 | tf_op jit(solution)/shard_map/ppermute | solution.py:425
  42.9 6.9 %collective-permute-start.8 = (bf16[3,32,256]{2,1,0:T(8,128)(2,1)S(1)}, bf16[3,32,256]{2,1,0:T(8,128)(2,1)S(1)}, u32[]{:S(2)}, u32[]{:S(2)}) collective-permute-start(bf16[3,32,256]{2,1,0:T(8,128)(2,1)S(1)} %get-tuple-element.75), channel_id=1, source_target_pairs={{8,4},{12,1},{9,5},{13,2},{10,6},{14,3},{11,7},{16,12},{20,9},{17,... | collective-permute-start | bytes 147464 | tf_op jit(solution)/shard_map/ppermute | solution.py:420
  45.4 6.7 %collective-permute-start.9 = (bf16[3,32,256]{2,1,0:T(8,128)(2,1)S(1)}, bf16[3,32,256]{2,1,0:T(8,128)(2,1)S(1)}, u32[]{:S(2)}, u32[]{:S(2)}) collective-permute-start(bf16[3,32,256]{2,1,0:T(8,128)(2,1)S(1)} %get-tuple-element.76), channel_id=1, source_target_pairs={{12,0},{9,4},{13,1},{10,5},{14,2},{11,6},{15,3},{20,8},{17,12},{21... | collective-permute-start | bytes 147464 | tf_op jit(solution)/shard_map/ppermute | solution.py:420
  56.1 11.1 %collective-permute-start.10 = (bf16[8,32,256]{2,1,0:T(8,128)(2,1)S(1)}, bf16[8,32,256]{2,1,0:T(8,128)(2,1)S(1)}, u32[]{:S(2)}, u32[]{:S(2)}) collective-permute-start(bf16[8,32,256]{2,1,0:T(8,128)(2,1)S(1)} %get-tuple-element.77), channel_id=1, source_target_pairs={{8,0},{16,8},{24,16},{9,1},{17,9},{25,17},{10,2},{18,10},{26,18},{... | collective-permute-start | bytes 393224 | tf_op jit(solution)/shard_map/ppermute | solution.py:425
  58.0 6.9 %collective-permute-start.11 = (bf16[3,32,256]{2,1,0:T(8,128)(2,1)S(1)}, bf16[3,32,256]{2,1,0:T(8,128)(2,1)S(1)}, u32[]{:S(2)}, u32[]{:S(2)}) collective-permute-start(bf16[3,32,256]{2,1,0:T(8,128)(2,1)S(1)} %get-tuple-element.78), channel_id=1, source_target_pairs={{8,4},{12,1},{9,5},{13,2},{10,6},{14,3},{11,7},{16,12},{20,9},{17,... | collective-permute-start | bytes 147464 | tf_op jit(solution)/shard_map/ppermute | solution.py:420
  60.3 6.9 %collective-permute-start.12 = (bf16[3,32,256]{2,1,0:T(8,128)(2,1)S(1)}, bf16[3,32,256]{2,1,0:T(8,128)(2,1)S(1)}, u32[]{:S(2)}, u32[]{:S(2)}) collective-permute-start(bf16[3,32,256]{2,1,0:T(8,128)(2,1)S(1)} %get-tuple-element.79), channel_id=1, source_target_pairs={{12,0},{9,4},{13,1},{10,5},{14,2},{11,6},{15,3},{20,8},{17,12},{21... | collective-permute-start | bytes 147464 | tf_op jit(solution)/shard_map/ppermute | solution.py:420
  68.3 3.1 %collective-permute-start.13 = (bf16[512,256]{1,0:T(8,128)(2,1)S(1)}, bf16[512,256]{1,0:T(8,128)(2,1)S(1)}, u32[]{:S(2)}, u32[]{:S(2)}) collective-permute-start(bf16[512,256]{1,0:T(8,128)(2,1)S(1)} %get-tuple-element.90.sent_ref), channel_id=1, source_target_pairs={{0,1},{1,0},{2,3},{3,2},{4,5},{5,4},{6,7},{7,6},{8,9},{9,8},{10,11... | collective-permute-start | bytes 786440 | tf_op jit(solution)/shard_map/ppermute | solution.py:644
  74.0 10.6 %collective-permute-start.17 = (bf16[576,256]{1,0:T(8,128)(2,1)S(1)}, bf16[576,256]{1,0:T(8,128)(2,1)S(1)}, u32[]{:S(2)}, u32[]{:S(2)}) collective-permute-start(bf16[576,256]{1,0:T(8,128)(2,1)S(1)} %get-tuple-element.98.sent_ref), channel_id=1, source_target_pairs={{0,1},{1,0},{2,3},{3,2},{4,5},{5,4},{6,7},{7,6},{8,9},{9,8},{10,11... | collective-permute-start | bytes 884744 | tf_op jit(solution)/shard_map/ppermute | solution.py:644
  74.5 6.0 %collective-permute-start.14 = (bf16[3,32,256]{2,1,0:T(8,128)(2,1)S(1)}, bf16[3,32,256]{2,1,0:T(8,128)(2,1)S(1)}, u32[]{:S(2)}, u32[]{:S(2)}) collective-permute-start(bf16[3,32,256]{2,1,0:T(8,128)(2,1)S(1)} %get-tuple-element.96), channel_id=1, source_target_pairs={{0,4},{4,1},{1,5},{5,2},{2,6},{6,3},{3,7},{8,12},{12,9},{9,13},{13... | collective-permute-start | bytes 147464 | tf_op jit(solution)/shard_map/ppermute | solution.py:420
  76.4 5.7 %collective-permute-start.15 = (bf16[3,32,256]{2,1,0:T(8,128)(2,1)S(1)}, bf16[3,32,256]{2,1,0:T(8,128)(2,1)S(1)}, u32[]{:S(2)}, u32[]{:S(2)}) collective-permute-start(bf16[3,32,256]{2,1,0:T(8,128)(2,1)S(1)} %get-tuple-element.97), channel_id=1, source_target_pairs={{4,0},{1,4},{5,1},{2,5},{6,2},{3,6},{7,3},{12,8},{9,12},{13,9},{10... | collective-permute-start | bytes 147464 | tf_op jit(solution)/shard_map/ppermute | solution.py:420
  80.3 7.0 %collective-permute-start.20 = (bf16[256,256]{1,0:T(8,128)(2,1)S(1)}, bf16[256,256]{1,0:T(8,128)(2,1)S(1)}, u32[]{:S(2)}, u32[]{:S(2)}) collective-permute-start(bf16[256,256]{1,0:T(8,128)(2,1)S(1)} %get-tuple-element.91.sent_ref), channel_id=1, source_target_pairs={{0,2},{1,3},{2,0},{3,1},{4,6},{5,7},{6,4},{7,5},{8,10},{9,11},{10,... | collective-permute-start | bytes 393224 | tf_op jit(solution)/shard_map/ppermute | solution.py:644
  84.7 7.0 %collective-permute-start.18 = (bf16[320,256]{1,0:T(8,128)(2,1)S(1)}, bf16[320,256]{1,0:T(8,128)(2,1)S(1)}, u32[]{:S(2)}, u32[]{:S(2)}) collective-permute-start(bf16[320,256]{1,0:T(8,128)(2,1)S(1)} %get-tuple-element.100.sent_ref), channel_id=1, source_target_pairs={{0,2},{1,3},{2,0},{3,1},{4,6},{5,7},{6,4},{7,5},{8,10},{9,11},{10,... | collective-permute-start | bytes 491528 | tf_op jit(solution)/shard_map/ppermute | solution.py:644
  85.2 7.3 %collective-permute-start.16 = (bf16[1,8,16,256]{3,2,1,0:T(8,128)(2,1)S(1)}, bf16[1,8,16,256]{3,2,1,0:T(8,128)(2,1)S(1)}, u32[]{:S(2)}, u32[]{:S(2)}) collective-permute-start(bf16[1,8,16,256]{3,2,1,0:T(8,128)(2,1)S(1)} %get-tuple-element.108), channel_id=1, source_target_pairs={{0,4},{4,0},{1,5},{5,1},{2,6},{6,2},{3,7},{7,3},{8,12},{12,8},{9,1... | collective-permute-start | bytes 196616 | tf_op jit(solution)/shard_map/ppermute | solution.py:760
  87.4 5.2 %collective-permute-start.21 = (bf16[256,256]{1,0:T(8,128)(2,1)S(1)}, bf16[256,256]{1,0:T(8,128)(2,1)S(1)}, u32[]{:S(2)}, u32[]{:S(2)}) collective-permute-start(bf16[256,256]{1,0:T(8,128)(2,1)S(1)} %close.3.refs_0_), channel_id=1, source_target_pairs={{0,4},{4,0},{1,5},{5,1},{2,6},{6,2},{3,7},{7,3},{8,12},{12,8},{9,1... | collective-permute-start | bytes 393224 | tf_op jit(solution)/shard_map/ppermute | solution.py:644
  91.8 6.1 %collective-permute-start.19 = (bf16[320,256]{1,0:T(8,128)(2,1)S(1)}, bf16[320,256]{1,0:T(8,128)(2,1)S(1)}, u32[]{:S(2)}, u32[]{:S(2)}) collective-permute-start(bf16[320,256]{1,0:T(8,128)(2,1)S(1)} %close.2.refs_0_), channel_id=1, source_target_pairs={{0,4},{4,0},{1,5},{5,1},{2,6},{6,2},{3,7},{7,3},{8,12},{12,8},{9,1... | collective-permute-start | bytes 491528 | tf_op jit(solution)/shard_map/ppermute | solution.py:644
  92.6 0.8 copy-start.9

commit v2 on v1

--- a/solution.py
+++ b/solution.py
@@ -29,6 +29,10 @@
         self.padded = self.width + 2 * self.margin
         self.cells = self.width * self.full
         self.part = min(256, hidden)
+        self.halves = channels // LANES
+
+    def wide(self, columns):
+        return (self.halves, columns, self.full + 2 * PAD, LANES)
 
     def main_size(self):
         sizes = []
@@ -84,8 +88,7 @@
     return jax.ShapeDtypeStruct(tuple(dims), dtype)
 
 
-def call(kernel, name, operands, outs, scratch, flops):
-    moved = sum(math.prod(o.shape) * o.dtype.itemsize for o in list(operands) + list(outs))
+def call(kernel, name, operands, outs, scratch, flops=1000):
     return pl.pallas_call(
         kernel,
         out_shape=outs,
@@ -93,23 +96,39 @@
         out_specs=[vmem()] * len(outs),
         scratch_shapes=scratch,
         compiler_params=pltpu.CompilerParams(vmem_limit_bytes=VMEM_BYTES),
-        cost_estimate=pl.CostEstimate(flops=flops, bytes_accessed=moved, transcendentals=0),
+        cost_estimate=pl.CostEstimate(flops=flops, bytes_accessed=1000, transcendentals=0),
         name=name,
     )(*operands)
 
 
-def pack_kernel(plan, params, tissue_ref, x_hbm, g_hbm, *refs):
+def pack_kernel(plan, x_ref, *refs):
+    rows, across = plan.rows, plan.across
+    outs, xt = refs[:-1], refs[-1]
+    me = lax.axis_index("row")
+    xt[...] = jnp.swapaxes(x_ref[...].astype(f32), 0, 1).astype(bf16)
+    nx, m = plan.main_size(), plan.margin
+    for dr in range(rows):
+        target = lax.rem(me - dr + rows, rows)
+        outs[dr][...] = xt[pl.ds(plan.main_start(target), nx)]
+    for k, (left, right) in enumerate(plan.sides()):
+        for dr in range(rows):
+            target = lax.rem(me - dr + rows, rows)
+            is_left = functools.reduce(jnp.logical_or, [target == r for r in left], jnp.bool_(False))
+            outs[rows * (1 + k) + dr][...] = xt[pl.ds(jnp.where(is_left, across - m, 0), m)]
+
+
+def pack(plan, x):
+    rows, h, c = plan.rows, plan.height, plan.channels
+    outs = [shape((plan.main_size(), h, c), bf16)] * rows
+    outs += [shape((plan.margin, h, c), bf16)] * (rows * len(plan.sides()))
+    return call(
+        functools.partial(pack_kernel, plan), "pack", [x], outs, [pltpu.VMEM((plan.across, h, c), bf16)]
+    )
+
+
+def pack_upstream_kernel(plan, tissue_ref, g_ref, *refs):
     rows, across, height = plan.rows, plan.across, plan.height
-    count = rows * (1 + len(plan.sides()))
-    sources, refs = refs[:params], refs[params:]
-    outs, refs = refs[:count], refs[count:]
-    targets, (x_ref, g_ref, xt, gt, sems) = refs[:params], refs[params:]
-    moves = [
-        pltpu.make_async_copy(source, target, sems.at[k])
-        for k, (source, target) in enumerate(zip((x_hbm, g_hbm, *sources), (x_ref, g_ref, *targets)))
-    ]
-    for move in moves:
-        move.start()
+    outs, gt = refs[:-1], refs[-1]
     tiles_r, tiles_c = tissue_ref.shape
     side_r, side_c = height // tiles_r, across // tiles_c
     me = lax.axis_index("row")
@@ -126,50 +145,64 @@
                 total = jnp.where(inside, tissue_ref[a, b].astype(f32), total)
         return total.astype(bf16)
 
-    moves[0].wait()
-    xt[...] = jnp.swapaxes(x_ref[...].astype(f32), 0, 1).astype(bf16)
-    moves[1].wait()
     gt[...] = jnp.swapaxes(g_ref[...].astype(f32), 0, 1).astype(bf16)
-    nx, m, w = plan.main_size(), plan.margin, plan.width
+    w = plan.width
     for dr in range(rows):
         target = lax.rem(me - dr + rows, rows)
-        out = outs[dr]
-        out[0:nx] = xt[pl.ds(plan.main_start(target), nx)]
-        out[nx : nx + w] = gt[pl.ds(target * w, w)]
-        out[nx + w] = slot(target * w)
-    for k, (left, right) in enumerate(plan.sides()):
-        for dr in range(rows):
-            target = lax.rem(me - dr + rows, rows)
-            is_left = functools.reduce(jnp.logical_or, [target == r for r in left], jnp.bool_(False))
-            outs[rows * (1 + k) + dr][...] = xt[pl.ds(jnp.where(is_left, across - m, 0), m)]
-    for move in moves[2:]:
+        outs[dr][0:w] = gt[pl.ds(target * w, w)]
+        outs[dr][w] = slot(target * w)
+
+
+def pack_upstream(plan, tissue, g):
+    h, c = plan.height, plan.channels
+    outs = [shape((plan.width + 1, h, c), bf16)] * plan.rows
+    return pl.pallas_call(
+        functools.partial(pack_upstream_kernel, plan),
+        out_shape=outs,
+        in_specs=[smem(), vmem()],
+        out_specs=[vmem()] * len(outs),
+        scratch_shapes=[pltpu.VMEM((plan.across, h, c), bf16)],
+        compiler_params=pltpu.CompilerParams(vmem_limit_bytes=VMEM_BYTES),
+        cost_estimate=pl.CostEstimate(flops=1000, bytes_accessed=1000, transcendentals=0),
+        name="pack_upstream",
+    )(tissue, g)
+
+
+def load_kernel(count, *refs):
+    moves = [
+        pltpu.make_async_copy(refs[k], refs[count + k], refs[-1].at[k]) for k in range(count)
+    ]
+    for move in moves:
+        move.start()
+    for move in moves:
         move.wait()
 
 
-def pack(plan, tissue, x, g, params):
-    rows, h, c = plan.rows, plan.height, plan.channels
-    outs = [shape((plan.main_size() + plan.width + 1, h, c), bf16)] * rows
-    outs += [shape((plan.margin, h, c), bf16)] * (rows * len(plan.sides()))
-    outs += [shape(a.shape, a.dtype) for a in params]
-    tile = pltpu.VMEM((h, plan.across, c), bf16)
-    turned = pltpu.VMEM((plan.across, h, c), bf16)
+def load(params):
     count = len(params)
-    out = pl.pallas_call(
-        functools.partial(pack_kernel, plan, count),
-        out_shape=outs,
-        in_specs=[smem()] + [pl.BlockSpec(memory_space=pltpu.HBM)] * (2 + count),
-        out_specs=[vmem()] * len(outs),
-        scratch_shapes=[tile, tile, turned, turned, pltpu.SemaphoreType.DMA((2 + count,))],
+    return pl.pallas_call(
+        functools.partial(load_kernel, count),
+        out_shape=[shape(a.shape, a.dtype) for a in params],
+        in_specs=[pl.BlockSpec(memory_space=pltpu.HBM)] * count,
+        out_specs=[vmem()] * count,
+        scratch_shapes=[pltpu.SemaphoreType.DMA((count,))],
         compiler_params=pltpu.CompilerParams(vmem_limit_bytes=VMEM_BYTES),
-        cost_estimate=pl.CostEstimate(flops=1000, bytes_accessed=4 << 20, transcendentals=0),
-        name="pack",
-    )(tissue, x, g, *params)
-    return out[:-count], out[-count:]
-
-
-def exchange(plan, pieces):
+        cost_estimate=pl.CostEstimate(flops=1000, bytes_accessed=1000, transcendentals=0),
+        name="load",
+    )(*params)
+
+
+def exchange_mains(plan, pieces):
+    received = [pieces[0]]
+    for dr in range(1, plan.rows):
+        pairs = [((r + dr) % plan.rows, r) for r in range(plan.rows)]
+        received.append(lax.ppermute(pieces[dr], "row", pairs))
+    return received
+
+
+def exchange_sides(plan, pieces):
     rows, cols = plan.rows, plan.cols
-    mains, sides = [pieces[0]], []
+    received = []
     for k, (left, right) in enumerate(plan.sides()):
         for dr in range(rows):
             pairs = []
@@ -180,15 +213,8 @@
                         if step != 0 and 0 <= c + step < cols:
                             source = plan.index(s, (r + dr) % rows, c + step)
                             pairs.append((source, plan.index(s, r, c)))
-            sides.append(lax.ppermute(pieces[rows * (1 + k) + dr], LINE, pairs))
-    for dr in range(1, rows):
-        pairs = []
-        for s in range(plan.segments):
-            for r in range(rows):
-                for c in range(cols):
-                    pairs.append((plan.index(s, (r + dr) % rows, c), plan.index(s, r, c)))
-        mains.append(lax.ppermute(pieces[dr], LINE, pairs))
-    return mains + sides
+            received.append(lax.ppermute(pieces[rows * k + dr], LINE, pairs))
+    return received
 
 
 def conv_block(plan, load, row_start, half, taps_ref, flip, keep):
@@ -197,9 +223,9 @@
     totals = [None] * plan.width
     for i in range(side):
         rows_at = pl.ds(row_start + (side - 1 - i if flip else i), 8)
-        window = [load(k, rows_at, lanes) if keep(k) else None for k in range(plan.padded)]
+        window = [load(k, rows_at, half) if keep(k) else None for k in range(plan.padded)]
         for j in range(side):
-            tap = taps_ref[i, pl.ds(j, 1), lanes]
+            tap = taps_ref[i, j, :, lanes]
             move = side - 1 - j if flip else j
             for q in range(plan.width):
                 if window[q + move] is not None:
@@ -209,9 +235,9 @@
 
 
 def clear_rims(ref, full):
-    zeros = jnp.zeros((ref.shape[0], PAD, ref.shape[2]), ref.dtype)
-    ref[:, 0:PAD, :] = zeros
-    ref[:, PAD + full : PAD + full + PAD, :] = zeros
+    zeros = jnp.zeros((*ref.shape[:2], PAD, LANES), ref.dtype)
+    ref[:, :, 0:PAD, :] = zeros
+    ref[:, :, PAD + full : PAD + full + PAD, :] = zeros
 
 
 def blocks(plan):
@@ -223,34 +249,29 @@
     pieces = refs[: rows * (1 + len(plan.sides()))]
     refs = refs[len(pieces) :]
     (taps_ref, conv_bias_ref, gain_ref, bias_ref, w_in_ref, b_in_ref) = refs[:6]
-    (og_ref, xw_ref, mask_ref, standard_ref, inv_ref, gate_ref, hidden_ref, normed_ref) = refs[6:14]
-    wide_x, conv_ref, pre_ref = refs[14:]
+    (xw_ref, standard_ref, inv_ref, gate_ref, hidden_ref, normed_ref) = refs[6:12]
+    wide_x, conv_ref, pre_ref = refs[12:]
     me = lax.axis_index("row")
     m, w, nx = plan.margin, plan.width, plan.main_size()
 
     clear_rims(wide_x, full)
-    for dr in range(rows):
-        piece = pieces[dr]
-        top = pl.multiple_of(lax.rem(me + dr, rows) * h, h)
-        wide_x[pl.ds(m + plan.main_start(me), nx), pl.ds(PAD + top, h), :] = piece[0:nx].astype(f32)
-        og_ref[:, pl.ds(top, h), :] = piece[nx : nx + w]
-        marks = piece[nx + w].astype(f32)
-        for l in range(w):
-            at = pl.ds(pl.multiple_of(l * full + top, h), h)
-            mask_ref[at, :] = jnp.broadcast_to(marks[:, l : l + 1], (h, LANES))
+    parts = [(m + plan.main_start(me), nx, pieces[dr], dr) for dr in range(rows)]
     for k, (left, right) in enumerate(plan.sides()):
         is_left = functools.reduce(jnp.logical_or, [me == r for r in left], jnp.bool_(False))
-        for dr in range(rows):
-            top = pl.multiple_of(lax.rem(me + dr, rows) * h, h)
-            start = jnp.where(is_left, 0, m + plan.across)
-            piece = pieces[rows * (1 + k) + dr]
-            wide_x[pl.ds(start, m), pl.ds(PAD + top, h), :] = piece[...].astype(f32)
+        start = jnp.where(is_left, 0, m + plan.across)
+        parts += [(start, m, pieces[rows * (1 + k) + dr], dr) for dr in range(rows)]
+    for start, count, piece, dr in parts:
+        top = pl.multiple_of(lax.rem(me + dr, rows) * h, h)
+        for half in range(plan.halves):
+            wide_x[half, pl.ds(start, count), pl.ds(PAD + top, h), :] = piece[
+                :, :, half * LANES : (half + 1) * LANES
+            ].astype(f32)
 
     base = me * w
-    xw_ref[...] = wide_x[pl.ds(base, plan.padded)]
-
-    def load(column, rows_at, lanes):
-        return wide_x[base + column, rows_at, lanes]
+    xw_ref[...] = wide_x[:, pl.ds(base, plan.padded)]
+
+    def load(column, rows_at, half):
+        return wide_x[half, base + column, rows_at, :]
 
     for half, block in blocks(plan):
         lanes = pl.ds(half * LANES, LANES)
@@ -291,9 +312,7 @@
 def forward(plan, pieces, taps, conv_bias, gain, bias, w_in, b_in):
     c, full, cells = plan.channels, plan.full, plan.cells
     outs = [
-        shape((plan.width, full, c), bf16),
-        shape((plan.padded, full + 2 * PAD, c), f32),
-        shape((cells, LANES), f32),
+        shape(plan.wide(plan.padded), f32),
         shape((cells, c), f32),
         shape((cells, LANES), f32),
         shape((cells, plan.hidden), bf16),
@@ -301,7 +320,7 @@
         shape((cells, c), bf16),
     ]
     scratch = [
-        pltpu.VMEM((plan.across + 2 * plan.margin, full + 2 * PAD, c), f32),
+        pltpu.VMEM(plan.wide(plan.across + 2 * plan.margin), f32),
         pltpu.VMEM((cells, c), f32),
         pltpu.VMEM((2, cells, plan.part), f32),
     ]
@@ -311,8 +330,26 @@
         [*pieces, taps, conv_bias, gain, bias, w_in, b_in],
         outs,
         scratch,
-        2 * cells * c * plan.hidden,
+        36 * cells * c * plan.hidden,
     )
+
+
+def upstream_kernel(plan, *refs):
+    pieces, (og_ref, mask_ref) = refs[:-2], refs[-2:]
+    w, h, full = plan.width, plan.height, plan.full
+    me = lax.axis_index("row")
+    for dr, piece in enumerate(pieces):
+        top = pl.multiple_of(lax.rem(me + dr, plan.rows) * h, h)
+        og_ref[:, pl.ds(top, h), :] = piece[0:w]
+        marks = piece[w].astype(f32)
+        for l in range(w):
+            at = pl.ds(pl.multiple_of(l * full + top, h), h)
+            mask_ref[at, :] = jnp.broadcast_to(marks[:, l : l + 1], (h, LANES))
+
+
+def upstream_strip(plan, pieces):
+    outs = [shape((plan.width, plan.full, plan.channels), bf16), shape((plan.cells, LANES), f32)]
+    return call(functools.partial(upstream_kernel, plan), "upstream", pieces, outs, [])
 
 
 def across_lanes(value, channels):
@@ -327,20 +364,23 @@
             (m - (distance - 1) * w - count, edges[2 * k]),
             (m + distance * w, edges[2 * k + 1]),
         ):
-            edge_ref[pl.ds(start, count), PAD : PAD + plan.full, :] = piece[...].astype(f32)
+            for half in range(plan.halves):
+                edge_ref[half, pl.ds(start, count), PAD : PAD + plan.full, :] = piece[
+                    :, :, half * LANES : (half + 1) * LANES
+                ].astype(f32)
 
 
 def edge_sums(plan, edge_ref, taps_ref, half, block):
-    def load(column, rows_at, lanes):
-        return edge_ref[column, rows_at, lanes]
+    def load(column, rows_at, half):
+        return edge_ref[half, column, rows_at, :]
 
     start = PAD - plan.margin + 8 * block
     return conv_block(plan, load, start, half, taps_ref, True, lambda k: not plan.own(k))
 
 
 def own_sums(plan, cg_ref, taps_ref, half, block):
-    def load(column, rows_at, lanes):
-        return cg_ref[column - plan.margin, rows_at, lanes]
+    def load(column, rows_at, half):
+        return cg_ref[half, column - plan.margin, rows_at, :]
 
     start = PAD - plan.margin + 8 * block
     return conv_block(plan, load, start, half, taps_ref, True, plan.own)
@@ -378,7 +418,9 @@
             - jnp.mean(norm_grad, axis=-1, keepdims=True)
             - standard * jnp.mean(norm_grad * standard, axis=-1, keepdims=True)
         )
-        cg_ref[col, PAD : PAD + full, :] = grad.astype(bf16).astype(f32)
+        grad = grad.astype(bf16).astype(f32)
+        for half in range(plan.halves):
+            cg_ref[half, col, PAD : PAD + full, :] = grad[:, half * LANES : (half + 1) * LANES]
 
 
 def contract_last(a, b):
@@ -396,8 +438,11 @@
 def put_edges(plan, cg_ref, outs):
     rows_at = pl.ds(PAD, plan.full)
     for k, (distance, count) in enumerate(plan.distances()):
-        outs[2 * k][...] = cg_ref[pl.ds(plan.width - count, count), rows_at, :].astype(bf16)
-        outs[2 * k + 1][...] = cg_ref[pl.ds(0, count), rows_at, :].astype(bf16)
+        for half in range(plan.halves):
+            lanes = pl.ds(half * LANES, LANES)
+            last = cg_ref[half, pl.ds(plan.width - count, count), rows_at, :]
+            outs[2 * k][:, :, lanes] = last.astype(bf16)
+            outs[2 * k + 1][:, :, lanes] = cg_ref[half, pl.ds(0, count), rows_at, :].astype(bf16)
 
 
 def edge_shapes(plan):
@@ -462,8 +507,8 @@
         pltpu.VMEM((plan.width, full, c), bf16),
         pltpu.VMEM((cells, c), bf16),
         pltpu.VMEM((cells, c), f32),
-        pltpu.VMEM((plan.width, full + 2 * PAD, c), f32),
-        pltpu.VMEM((plan.padded, full + 2 * PAD, c), f32),
+        pltpu.VMEM(plan.wide(plan.width), f32),
+        pltpu.VMEM(plan.wide(plan.padded), f32),
     ]
     return call(
         functools.partial(step_kernel, plan, len(received)),
@@ -535,7 +580,7 @@
         "grad_out",
         [og, *received, scale, mask, hidden_t],
         outs,
-        [pltpu.VMEM((plan.padded, full + 2 * PAD, c), f32)],
+        [pltpu.VMEM(plan.wide(plan.padded), f32)],
         2 * cells * c * plan.hidden,
     )
 
@@ -578,12 +623,11 @@
     rows = []
     for i in range(side):
         pieces = [[] for _ in range(side)]
-        for half in range(plan.channels // LANES):
-            lanes = pl.ds(half * LANES, LANES)
+        for half in range(plan.halves):
             totals = [jnp.zeros((8, LANES), f32) for _ in range(side)]
             for block in range(full // 8):
-                window = xw_ref[:, pl.ds(PAD - plan.margin + i + 8 * block, 8), lanes]
-                grad = cg_ref[:, pl.ds(PAD + 8 * block, 8), lanes]
+                window = xw_ref[half, :, pl.ds(PAD - plan.margin + i + 8 * block, 8), :]
+                grad = cg_ref[half, :, pl.ds(PAD + 8 * block, 8), :]
                 for j in range(side):
                     totals[j] = totals[j] + jnp.sum(window[j : j + width] * grad, axis=0)
             for j in range(side):
@@ -597,7 +641,7 @@
 def taps_step(plan, norm_grad, halves, gain, standard, inv, xw):
     c, full = plan.channels, plan.full
     outs = [
-        shape((plan.width, full + 2 * PAD, c), f32),
+        shape(plan.wide(plan.width), f32),
         shape((plan.cols // 2 * in_share(plan)[1] + taps_rows(plan), c), bf16),
         *edge_shapes(plan),
     ]
@@ -634,7 +678,7 @@
         "finish",
         [upstream, conv_grad, taps, *edges],
         [shape((plan.rows, plan.width, plan.height, c), bf16)],
-        [pltpu.VMEM((plan.padded, plan.full + 2 * PAD, c), f32)],
+        [pltpu.VMEM(plan.wide(plan.padded), f32)],
         2 * plan.cells * c * plan.side**2,
     )[0]
 
@@ -674,6 +718,7 @@
     def __init__(self, plan, halves, send, share_rows, extra):
         self.plan, self.share_rows, self.extra = plan, share_rows, extra
         self.keep, self.send, self.bit = halves, send, 1
+        self.total = None
         if plan.cols > 2:
             self.next_stage()
 
@@ -694,19 +739,23 @@
             1000,
         )
 
-    def terms(self):
+    def close(self, after=None):
         plan = self.plan
         while 2 * self.bit < plan.cols:
             self.next_stage()
         got = swap(self.send, "col", self.bit)
-        total = call(
+        if after is not None:
+            got, _ = lax.optimization_barrier((got, after))
+        self.total = call(
             functools.partial(close_kernel, self.share_rows, self.extra),
             "close",
             [self.keep, self.send, got],
             [shape((self.share_rows + self.extra, plan.channels), bf16)],
             [],
-            1000,
         )[0]
+
+    def terms(self):
+        plan, total = self.plan, self.total
         terms = [total]
         bit = 1
         while bit < plan.rows:
@@ -732,7 +781,9 @@
         in_ref[:, pl.ds(n * plan.part, plan.part)] = read(terms, scale, n * rows, rows)
     sums = read(terms, scale, share_rows, taps_rows(plan))
     for i in range(plan.side):
-        taps_ref[i] = sums[i * plan.side : (i + 1) * plan.side]
+        for j in range(plan.side):
+            row = i * plan.side + j
+            taps_ref[i, j] = sums[row : row + 1]
 
 
 def out_result(plan, scale, terms):
@@ -743,7 +794,7 @@
 def in_result(plan, scale, terms):
     outs = [
         shape((in_share(plan)[0], plan.hidden), f32),
-        shape((plan.side, plan.side, plan.channels), f32),
+        shape((plan.side, plan.side, 1, plan.channels), f32),
     ]
     return call(functools.partial(in_result_kernel, plan, scale), "in_result", terms, outs, [], 1000)
 
@@ -764,13 +815,17 @@
 
 
 def one_crop(plan, norm_scale, tissue, saved, out_grad, params):
-    packed, params = pack(plan, tissue, saved, out_grad, params)
-    taps, w_in, w_out, conv_bias, gain, bias, b_in, scale = params
-    pieces = exchange(plan, packed)
-    taps_above = to_segment_below(plan, taps)
-    og, xw, mask, standard, inv, gate, hidden, normed = forward(
+    packed = pack(plan, saved)
+    mains, sides = packed[: plan.rows], packed[plan.rows :]
+    sides, mains = lax.optimization_barrier((exchange_sides(plan, sides), mains))
+    pieces = exchange_mains(plan, mains) + sides
+    upstream = exchange_mains(plan, pack_upstream(plan, tissue, out_grad))
+    taps_above = to_segment_below(plan, params[0])
+    taps, w_in, w_out, conv_bias, gain, bias, b_in, scale = load(params)
+    xw, standard, inv, gate, hidden, normed = forward(
         plan, pieces, taps, conv_bias, gain, bias, w_in, b_in
     )
+    og, mask, taps_above = lax.optimization_barrier((*upstream_strip(plan, upstream), taps_above))
     step_params, kept = (scale, gain, w_in, w_out, taps), (standard, inv, gate, mask)
     received, turned = [], None
     for _ in range(plan.segments - 1):
@@ -786,8 +841,11 @@
     norm_grad, _ = lax.optimization_barrier((norm_grad, out_sum.send))
     conv_grad, send, *edges = taps_step(plan, norm_grad, halves, gain, standard, inv, xw)
     in_sum = Reduction(plan, halves, send, in_share(plan)[1], taps_rows(plan))
+    out_sum.close(in_sum.send)
     grad_out = out_result(plan, norm_scale, out_sum.terms())
+    edges, _, _ = lax.optimization_barrier((edges, in_sum.send, out_sum.total))
     strips = finish(plan, upstream, conv_grad, taps, send_edges(plan, edges, 0))
+    in_sum.close()
     grad_in, grad_taps = in_result(plan, norm_scale, in_sum.terms())
     return to_tile(plan, strips), grad_in, grad_out, grad_taps
 
@@ -817,14 +875,14 @@
         conv_taps.shape[1],
     )
     norm_scale = 1.0 / math.sqrt(crop_count * plan.full * across * plan.cols)
-    params = (conv_taps[0], w_in[0], w_out[0], conv_bias, norm_gain, norm_bias, b_in, layer_scale)
+    params = (conv_taps.transpose(1, 2, 0, 3), w_in[0], w_out[0], conv_bias, norm_gain, norm_bias, b_in, layer_scale)
     results = [
         one_crop(plan, norm_scale, tissue[crop], saved_inputs[0, crop], out_grad[crop], params)
         for crop in range(crop_count)
     ]
     grads, *weights = zip(*results)
     grad_in, grad_out, grad_taps = (sum(w[1:], w[0]) for w in weights)
-    return (jnp.stack(grads)[None], grad_in[None], grad_out[None], grad_taps[None])
+    return (jnp.stack(grads)[None], grad_in[None], grad_out[None], grad_taps.transpose(2, 0, 1, 3))
 
 
 def solution(mesh):

time: 100 us -> 93 us (0.930)
  Pallas kernels: 25 us -> 13.7 us
  waiting for transfers between devices: 25.5 us -> 29.7 us
  local copies, waits for them, and re-layouts: 6.18 us -> 3.75 us
  starting transfers between devices: 41.1 us -> 42.8 us
    pallas_call x15 -> x17, Pallas kernels: 24.2 us -> 13.4 us  [call(): pl.pallas_call(kernel, out_shape=outs, in_specs=[vmem()] * len(operands),...]
    ppermute x6, waiting for transfers between devices: 8.91 us -> 13.1 us  [swap(): return lax.ppermute(value, axis, [(i, i ^ bit) for i in range(size)])]
    unnamed x22, local copies, waits for them, and re-layouts: 6.09 us -> 3.65 us
    ppermute x3 -> x4, starting transfers between devices: 7.14 us -> 7.68 us  [the longest x2 5.59 us: exchange_sides(): received.append(lax.ppermute(pieces[rows * k + dr], LINE, pairs))]
  transfers between devices with their start and end apart: 22 -> 23, of which waited for: 11 -> 16; matrix products, arithmetic and copies ran while one was open for 0% -> 0% of each run, Pallas kernels for 5% -> 4%
where the time goes in v2:
time: 93 us; the launch traced here: 91.6 us
  starting transfers between devices  42.8 us (46%)
  waiting for transfers between devices  29.7 us (32%)
  Pallas kernels  13.7 us (15%)
  local copies, waits for them, and re-layouts  3.75 us (4%)
  between operations  1.63 us (2%)
    ppermute x8, starting transfers between devices, send_edges(): received.append(lax.ppermute(piece, LINE, pairs))  19 us
    ppermute x8, waiting for transfers between devices, send_edges(): received.append(lax.ppermute(piece, LINE, pairs))  14.1 us
    pallas_call x17, Pallas kernels, call(): pl.pallas_call(kernel, out_shape=outs, in_specs=[vmem()] * len(operands),...  13.4 us
    ppermute x6, waiting for transfers between devices, swap(): return lax.ppermute(value, axis, [(i, i ^ bit) for i in range(size)])  13.1 us
    ppermute x4, starting transfers between devices, to_segment_below(): lax.ppermute(value, 'segment', [(s, s - 1) for s in range(1, plan.segment...  9.11 us
    ppermute x2, starting transfers between devices, exchange_sides(): received.append(lax.ppermute(pieces[rows * k + dr], LINE, pairs))  5.59 us
    ppermute x6, starting transfers between devices, swap(): return lax.ppermute(value, axis, [(i, i ^ bit) for i in range(size)])  4.66 us
    unnamed x22, local copies, waits for them, and re-layouts  3.65 us
  transfers between devices with their start and end apart: 23, of which 16 were waited for; matrix products, arithmetic and copies ran while one was open for 0% of the time, Pallas kernels for 4%

profile of v2, /device:TPU:18, one launch (start us, length us, event | category | flops | bytes accessed | tf_op | source)
XLA Modules:
  0.0 91.6 jit_solution(1828279864539760294)
XLA Ops:
  0.6 0.9 copy-done.2
  1.6 1.3 %collective-permute-start.2 = (bf16[3,16,256]{2,1,0:T(8,128)(2,1)S(1)}, bf16[3,16,256]{2,1,0:T(8,128)(2,1)S(1)}, u32[]{:S(2)}, u32[]{:S(2)}) collective-permute-start(bf16[3,16,256]{2,1,0:T(8,128)(2,1)S(1)} %get-tuple-element.76), channel_id=1, source_target_pairs={{0,1},{1,2},{2,3},{5,4},{6,5},{7,6},{8,9},{9,10},{10,11},{13,12},{... | collective-permute-start | bytes 73736 | tf_op jit(solution)/shard_map/ppermute | solution.py:216
  2.9 4.3 %collective-permute-start.3 = (bf16[3,16,256]{2,1,0:T(8,128)(2,1)S(1)}, bf16[3,16,256]{2,1,0:T(8,128)(2,1)S(1)}, u32[]{:S(2)}, u32[]{:S(2)}) collective-permute-start(bf16[3,16,256]{2,1,0:T(8,128)(2,1)S(1)} %get-tuple-element.77), channel_id=1, source_target_pairs={{4,1},{5,2},{6,3},{1,4},{2,5},{3,6},{12,9},{13,10},{14,11},{9,12},... | collective-permute-start | bytes 73736 | tf_op jit(solution)/shard_map/ppermute | solution.py:216
  7.2 1.5 %collective-permute-done.3.refs_3_ = bf16[3,16,256]{2,1,0:T(8,128)(2,1)S(1)} collective-permute-done((bf16[3,16,256]{2,1,0:T(8,128)(2,1)S(1)}, bf16[3,16,256]{2,1,0:T(8,128)(2,1)S(1)}, u32[]{:S(2)}, u32[]{:S(2)}) %collective-permute-start.3) | collective-permute-done | bytes 24608 | tf_op jit(solution)/shard_map/ppermute | solution.py:216
  9.5 2.1 %collective-permute-start = (bf16[9,16,256]{2,1,0:T(8,128)(2,1)S(1)}, bf16[9,16,256]{2,1,0:T(8,128)(2,1)S(1)}, u32[]{:S(2)}, u32[]{:S(2)}) collective-permute-start(bf16[9,16,256]{2,1,0:T(8,128)(2,1)S(1)} %get-tuple-element.67), channel_id=1, source_target_pairs={{4,0},{0,4},{5,1},{1,5},{6,2},{2,6},{7,3},{3,7},{12,8},{8,12},{13,... | collective-permute-start | bytes 221192 | tf_op jit(solution)/shard_map/ppermute | solution.py:199
  11.6 2.5 %collective-permute-start.1 = (f32[7,7,1,256]{3,2,1,0:T(1,128)S(1)}, f32[7,7,1,256]{3,2,1,0:T(1,128)S(1)}, u32[]{:S(2)}, u32[]{:S(2)}) collective-permute-start(f32[7,7,1,256]{3,2,1,0:T(1,128)S(1)} %bitcast.19), channel_id=1, source_target_pairs={{8,0},{16,8},{24,16},{9,1},{17,9},{25,17},{10,2},{18,10},{26,18},{... | collective-permute-start | bytes 150536 | tf_op jit(solution)/shard_map/ppermute | solution.py:470
  14.2 0.6 copy-done.6
  14.8 1.0 %copy-done = bf16[1,256,1024]{2,1,0:T(8,128)(2,1)S(1)} copy-done((bf16[1,256,1024]{2,1,0:T(8,128)(2,1)S(1)}, bf16[1,256,1024]{2,1,0:T(8,128)(2,1)}, u32[]{:S(2)}) %copy-start) | copy-done | bytes 524312
  15.8 1.0 %copy-done.1 = bf16[1,1024,256]{2,1,0:T(8,128)(2,1)S(1)} copy-done((bf16[1,1024,256]{2,1,0:T(8,128)(2,1)S(1)}, bf16[1,1024,256]{2,1,0:T(8,128)(2,1)}, u32[]{:S(2)}) %copy-start.1) | copy-done | bytes 524312
  17.2 0.9 %collective-permute-done.1.refs_0_ = f32[7,7,1,256]{3,2,1,0:T(1,128)S(1)} collective-permute-done((f32[7,7,1,256]{3,2,1,0:T(1,128)S(1)}, f32[7,7,1,256]{3,2,1,0:T(1,128)S(1)}, u32[]{:S(2)}, u32[]{:S(2)}) %collective-permute-start.1) | collective-permute-done | bytes 50208 | tf_op jit(solution)/shard_map/ppermute | solution.py:470
  18.1 2.1 %forward.1 = (f32[2,14,48,128]{3,2,1,0:T(8,128)S(1)}, f32[256,256]{1,0:T(8,128)S(1)}, f32[256,128]{1,0:T(8,128)S(1)}, bf16[256,1024]{1,0:T(8,128)(2,1)S(1)}, bf1...) custom-call(bf16[11,16,256]{2,1,0:T(8,128)(2,1)S(1)} %get-tuple-element.80.refs_0_, ...), custom_call_target="tpu_custom_call" | custom-call | flops 2415919104 | bytes 1000 | tf_op jit(solution)/shard_map/forward/pallas_call | solution.py:92
  20.2 1.7 %backward.3 = (bf16[8,32,256]{2,1,0:T(8,128)(2,1)S(1)}, bf16[3,32,256]{2,1,0:T(8,128)(2,1)S(1)}, bf16[3,32,256]{2,1,0:T(8,128)(2,1)S(1)}) custom-call(bf16[8,32,256]{2,1,0:T(8,128)(2,1)S(1)} %get-tuple-element.70.og_ref, f32[1,256]{1,0:T(1,128)S(1)} %get-tuple-element.72.refs_0_.refs_4_, f32[1,256]{1,0:T(1,128)S(1)} %get-tuple-element.73.refs_6_.refs_1_.refs_5_.gain_ref, ...), custom_call_target="tpu_custom_call" | custom-call | flops 268435456 | bytes 1000 | tf_op jit(solution)/shard_map/backward/pallas_call | solution.py:92
  21.9 2.4 %collective-permute-start.5 = (bf16[8,32,256]{2,1,0:T(8,128)(2,1)S(1)}, bf16[8,32,256]{2,1,0:T(8,128)(2,1)S(1)}, u32[]{:S(2)}, u32[]{:S(2)}) collective-permute-start(bf16[8,32,256]{2,1,0:T(8,128)(2,1)S(1)} %get-tuple-element.92), channel_id=1, source_target_pairs={{8,0},{16,8},{24,16},{9,1},{17,9},{25,17},{10,2},{18,10},{26,18},{... | collective-permute-start | bytes 393224 | tf_op jit(solution)/shard_map/ppermute | solution.py:470
  24.3 1.9 %collective-permute-start.6 = (bf16[3,32,256]{2,1,0:T(8,128)(2,1)S(1)}, bf16[3,32,256]{2,1,0:T(8,128)(2,1)S(1)}, u32[]{:S(2)}, u32[]{:S(2)}) collective-permute-start(bf16[3,32,256]{2,1,0:T(8,128)(2,1)S(1)} %get-tuple-element.93), channel_id=1, source_target_pairs={{8,4},{12,1},{9,5},{13,2},{10,6},{14,3},{11,7},{16,12},{20,9},{17,... | collective-permute-start | bytes 147464 | tf_op jit(solution)/shard_map/ppermute | solution.py:465
  26.2 2.6 %collective-permute-start.7 = (bf16[3,32,256]{2,1,0:T(8,128)(2,1)S(1)}, bf16[3,32,256]{2,1,0:T(8,128)(2,1)S(1)}, u32[]{:S(2)}, u32[]{:S(2)}) collective-permute-start(bf16[3,32,256]{2,1,0:T(8,128)(2,1)S(1)} %get-tuple-element.94), channel_id=1, source_target_pairs={{12,0},{9,4},{13,1},{10,5},{14,2},{11,6},{15,3},{20,8},{17,12},{21... | collective-permute-start | bytes 147464 | tf_op jit(solution)/shard_map/ppermute | solution.py:465
  28.8 2.3 %collective-permute-done.6.refs_2_ = bf16[3,32,256]{2,1,0:T(8,128)(2,1)S(1)} collective-permute-done((bf16[3,32,256]{2,1,0:T(8,128)(2,1)S(1)}, bf16[3,32,256]{2,1,0:T(8,128)(2,1)S(1)}, u32[]{:S(2)}, u32[]{:S(2)}) %collective-permute-start.6) | collective-permute-done | bytes 49184 | tf_op jit(solution)/shard_map/ppermute | solution.py:465
  31.1 1.4 %collective-permute-done.7.refs_3_ = bf16[3,32,256]{2,1,0:T(8,128)(2,1)S(1)} collective-permute-done((bf16[3,32,256]{2,1,0:T(8,128)(2,1)S(1)}, bf16[3,32,256]{2,1,0:T(8,128)(2,1)S(1)}, u32[]{:S(2)}, u32[]{:S(2)}) %collective-permute-start.7) | collective-permute-done | bytes 49184 | tf_op jit(solution)/shard_map/ppermute | solution.py:465
  32.5 1.9 %backward.4 = (bf16[8,32,256]{2,1,0:T(8,128)(2,1)S(1)}, bf16[3,32,256]{2,1,0:T(8,128)(2,1)S(1)}, bf16[3,32,256]{2,1,0:T(8,128)(2,1)S(1)}) custom-call(bf16[8,32,256]{2,1,0:T(8,128)(2,1)S(1)} %get-tuple-element.70.og_ref, f32[7,7,1,256]{3,2,1,0:T(1,128)S(1)} %collective-permute-done.1.refs_0_, bf16[8,32,256]{2,1,0:T(8,128)(2,1)S(1)} %collective-permute-done.5.refs_1_, ...), custom_call_target="tpu_custom_call" | custom-call | flops 268435456 | bytes 1000 | tf_op jit(solution)/shard_map/backward/pallas_call | solution.py:92
  34.4 2.4 %collective-permute-start.8 = (bf16[8,32,256]{2,1,0:T(8,128)(2,1)S(1)}, bf16[8,32,256]{2,1,0:T(8,128)(2,1)S(1)}, u32[]{:S(2)}, u32[]{:S(2)}) collective-permute-start(bf16[8,32,256]{2,1,0:T(8,128)(2,1)S(1)} %get-tuple-element.95), channel_id=1, source_target_pairs={{8,0},{16,8},{24,16},{9,1},{17,9},{25,17},{10,2},{18,10},{26,18},{... | collective-permute-start | bytes 393224 | tf_op jit(solution)/shard_map/ppermute | solution.py:470
  36.7 2.8 %collective-permute-start.10 = (bf16[3,32,256]{2,1,0:T(8,128)(2,1)S(1)}, bf16[3,32,256]{2,1,0:T(8,128)(2,1)S(1)}, u32[]{:S(2)}, u32[]{:S(2)}) collective-permute-start(bf16[3,32,256]{2,1,0:T(8,128)(2,1)S(1)} %get-tuple-element.97), channel_id=1, source_target_pairs={{12,0},{9,4},{13,1},{10,5},{14,2},{11,6},{15,3},{20,8},{17,12},{21... | collective-permute-start | bytes 147464 | tf_op jit(solution)/shard_map/ppermute | solution.py:465
  39.6 1.9 %collective-permute-start.9 = (bf16[3,32,256]{2,1,0:T(8,128)(2,1)S(1)}, bf16[3,32,256]{2,1,0:T(8,128)(2,1)S(1)}, u32[]{:S(2)}, u32[]{:S(2)}) collective-permute-start(bf16[3,32,256]{2,1,0:T(8,128)(2,1)S(1)} %get-tuple-element.96), channel_id=1, source_target_pairs={{8,4},{12,1},{9,5},{13,2},{10,6},{14,3},{11,7},{16,12},{20,9},{17,... | collective-permute-start | bytes 147464 | tf_op jit(solution)/shard_map/ppermute | solution.py:465
  41.5 2.0 %collective-permute-done.10.refs_3_ = bf16[3,32,256]{2,1,0:T(8,128)(2,1)S(1)} collective-permute-done((bf16[3,32,256]{2,1,0:T(8,128)(2,1)S(1)}, bf16[3,32,256]{2,1,0:T(8,128)(2,1)S(1)}, u32[]{:S(2)}, u32[]{:S(2)}) %collective-permute-start.10) | collective-permute-done | bytes 49184 | tf_op jit(solution)/shard_map/ppermute | solution.py:465
  43.5 2.9 %collective-permute-done.9.refs_2_ = bf16[3,32,256]{2,1,0:T(8,128)(2,1)S(1)} collective-permute-done((bf16[3,32,256]{2,1,0:T(8,128)(2,1)S(1)}, bf16[3,32,256]{2,1,0:T(8,128)(2,1)S(1)}, u32[]{:S(2)}, u32[]{:S(2)}) %collective-permute-start.9) | collective-permute-done | bytes 49184 | tf_op jit(solution)/shard_map/ppermute | solution.py:465
  46.5 1.9 %backward.5 = (bf16[8,32,256]{2,1,0:T(8,128)(2,1)S(1)}, bf16[3,32,256]{2,1,0:T(8,128)(2,1)S(1)}, bf16[3,32,256]{2,1,0:T(8,128)(2,1)S(1)}) custom-call(bf16[8,32,256]{2,1,0:T(8,128)(2,1)S(1)} %get-tuple-element.70.og_ref, f32[7,7,1,256]{3,2,1,0:T(1,128)S(1)} %collective-permute-done.1.refs_0_, bf16[8,32,256]{2,1,0:T(8,128)(2,1)S(1)} %collective-permute-done.8.refs_1_, ...), custom_call_target="tpu_custom_call" | custom-call | flops 268435456 | bytes 1000 | tf_op jit(solution)/shard_map/backward/pallas_call | solution.py:92
  48.3 1.9 %collective-permute-start.11 = (bf16[8,32,256]{2,1,0:T(8,128)(2,1)S(1)}, bf16[8,32,256]{2,1,0:T(8,128)(2,1)S(1)}, u32[]{:S(2)}, u32[]{:S(2)}) collective-permute-start(bf16[8,32,256]{2,1,0:T(8,128)(2,1)S(1)} %get-tuple-element.98), channel_id=1, source_target_pairs={{8,0},{16,8},{24,16},{9,1},{17,9},{25,17},{10,2},{18,10},{26,18},{... | collective-permute-start | bytes 393224 | tf_op jit(solution)/shard_map/ppermute | solution.py:470
  50.3 1.9 %collective-permute-start.12 = (bf16[3,32,256]{2,1,0:T(8,128)(2,1)S(1)}, bf16[3,32,256]{2,1,0:T(8,128)(2,1)S(1)}, u32[]{:S(2)}, u32[]{:S(2)}) collective-permute-start(bf16[3,32,256]{2,1,0:T(8,128)(2,1)S(1)} %get-tuple-element.99), channel_id=1, source_target_pairs={{8,4},{12,1},{9,5},{13,2},{10,6},{14,3},{11,7},{16,12},{20,9},{17,... | collective-permute-start | bytes 147464 | tf_op jit(solution)/shard_map/ppermute | solution.py:465
  52.2 1.9 %collective-permute-start.13 = (bf16[3,32,256]{2,1,0:T(8,128)(2,1)S(1)}, bf16[3,32,256]{2,1,0:T(8,128)(2,1)S(1)}, u32[]{:S(2)}, u32[]{:S(2)}) collective-permute-start(bf16[3,32,256]{2,1,0:T(8,128)(2,1)S(1)} %get-tuple-element.100), channel_id=1, source_target_pairs={{12,0},{9,4},{13,1},{10,5},{14,2},{11,6},{15,3},{20,8},{17,12},{21... | collective-permute-start | bytes 147464 | tf_op jit(solution)/shard_map/ppermute | solution.py:465
  54.4 2.8 %collective-permute-done.12.refs_2_ = bf16[3,32,256]{2,1,0:T(8,128)(2,1)S(1)} collective-permute-done((bf16[3,32,256]{2,1,0:T(8,128)(2,1)S(1)}, bf16[3,32,256]{2,1,0:T(8,128)(2,1)S(1)}, u32[]{:S(2)}, u32[]{:S(2)}) %collective-permute-start.12) | collective-permute-done | bytes 49184 | tf_op jit(solution)/shard_map/ppermute | solution.py:465
  57.2 1.3 %collective-permute-done.13.refs_3_ = bf16[3,32,256]{2,1,0:T(8,128)(2,1)S(1)} collective-permute-done((bf16[3,32,256]{2,1,0:T(8,128)(2,1)S(1)}, bf16[3,32,256]{2,1,0:T(8,128)(2,1)S(1)}, u32[]{:S(2)}, u32[]{:S(2)}) %collective-permute-start.13) | collective-permute-done | bytes 49184 | tf_op jit(solution)/shard_map/ppermute | solution.py:465
  58.5 0.7 grad_out.1
  59.3 2.8 %collective-permute-start.14 = (bf16[512,256]{1,0:T(8,128)(2,1)S(1)}, bf16[512,256]{1,0:T(8,128)(2,1)S(1)}, u32[]{:S(2)}, u32[]{:S(2)}) collective-permute-start(bf16[512,256]{1,0:T(8,128)(2,1)S(1)} %get-tuple-element.111.sent_ref), channel_id=1, source_target_pairs={{0,1},{1,0},{2,3},{3,2},{4,5},{5,4},{6,7},{7,6},{8,9},{9,8},{10,11... | collective-permute-start | bytes 786440 | tf_op jit(solution)/shard_map/ppermute | solution.py:688
  62.1 1.1 %grad_in.1 = (f32[256,256]{1,0:T(8,128)S(1)}, f32[2,2,256,256]{3,2,1,0:T(8,128)S(1)}) custom-call(bf16[256,256]{1,0:T(8,128)(2,1)S(1)} %get-tuple-element.107.bg_ref, bf16[256,1024]{1,0:T(8,128)(2,1)S(1)} %get-tuple-element.74.refs_8_.refs_2_.refs_6_.w_in_ref, bf16[1024,256]{1,0:T(8,128)(2,1)S(1)} %get-tuple-element.75.refs_3_.refs_7_.w_out_ref, ...), custom_call_target="tpu_custom_call" | custom-call | flops 402653184 | bytes 1000 | tf_op jit(solution)/shard_map/grad_in/pallas_call | solution.py:92
  63.3 1.1 %grad_taps.1 = (f32[2,8,48,128]{3,2,1,0:T(8,128)S(1)}, bf16[576,256]{1,0:T(8,128)(2,1)S(1)}, bf16[3,32,256]{2,1,0:T(8,128)(2,1)S(1)}, bf16[3,32,256]{2,1,0:T(8,128)(2,1)S(1)}) custom-call(f32[256,256]{1,0:T(8,128)S(1)} %get-tuple-element.113.ng_ref, f32[2,2,256,256]{3,2,1,0:T(8,128)S(1)} %get-tuple-element.114.halves_ref.keep_ref, ...), custom_call_target="tpu_custom_call" | custom-call | flops 6422528 | bytes 1000 | tf_op jit(solution)/shard_map/grad_taps/pallas_call | solution.py:92
  64.4 0.4 collective-permute-start.15
  64.8 1.2 %collective-permute-done.15.got_ref = bf16[576,256]{1,0:T(8,128)(2,1)S(1)} collective-permute-done((bf16[576,256]{1,0:T(8,128)(2,1)S(1)}, bf16[576,256]{1,0:T(8,128)(2,1)S(1)}, u32[]{:S(2)}, u32[]{:S(2)}) %collective-permute-start.15) | collective-permute-done | bytes 294944 | tf_op jit(solution)/shard_map/ppermute | solution.py:688
  66.1 4.3 %collective-permute-done.16.got_ref = bf16[256,256]{1,0:T(8,128)(2,1)S(1)} collective-permute-done((bf16[256,256]{1,0:T(8,128)(2,1)S(1)}, bf16[256,256]{1,0:T(8,128)(2,1)S(1)}, u32[]{:S(2)}, u32[]{:S(2)}) %collective-permute-start.16) | collective-permute-done | bytes 131104 | tf_op jit(solution)/shard_map/ppermute | solution.py:688
  70.4 1.9 %collective-permute-start.17 = (bf16[3,32,256]{2,1,0:T(8,128)(2,1)S(1)}, bf16[3,32,256]{2,1,0:T(8,128)(2,1)S(1)}, u32[]{:S(2)}, u32[]{:S(2)}) collective-permute-start(bf16[3,32,256]{2,1,0:T(8,128)(2,1)S(1)} %get-tuple-element.123), channel_id=1, source_target_pairs={{0,4},{4,1},{1,5},{5,2},{2,6},{6,3},{3,7},{8,12},{12,9},{9,13},{13... | collective-permute-start | bytes 147464 | tf_op jit(solution)/shard_map/ppermute | solution.py:465
  72.3 3.9 %collective-permute-start.18 = (bf16[3,32,256]{2,1,0:T(8,128)(2,1)S(1)}, bf16[3,32,256]{2,1,0:T(8,128)(2,1)S(1)}, u32[]{:S(2)}, u32[]{:S(2)}) collective-permute-start(bf16[3,32,256]{2,1,0:T(8,128)(2,1)S(1)} %get-tuple-element.124), channel_id=1, source_target_pairs={{4,0},{1,4},{5,1},{2,5},{6,2},{3,6},{7,3},{12,8},{9,12},{13,9},{10... | collective-permute-start | bytes 147464 | tf_op jit(solution)/shard_map/ppermute | solution.py:465
  76.3 0.3 collective-permute-start.20
  76.6 1.4 %collective-permute-done.18.refs_1_ = bf16[3,32,256]{2,1,0:T(8,128)(2,1)S(1)} collective-permute-done((bf16[3,32,256]{2,1,0:T(8,128)(2,1)S(1)}, bf16[3,32,256]{2,1,0:T(8,128)(2,1)S(1)}, u32[]{:S(2)}, u32[]{:S(2)}) %collective-permute-start.18) | collective-permute-done | bytes 49184 | tf_op jit(solution)/shard_map/ppermute | solution.py:465
  78.0 0.9 finish.1
  78.9 2.4 %collective-permute-start.19 = (bf16[1,8,16,256]{3,2,1,0:T(8,128)(2,1)S(1)}, bf16[1,8,16,256]{3,2,1,0:T(8,128)(2,1)S(1)}, u32[]{:S(2)}, u32[]{:S(2)}) collective-permute-start(bf16[1,8,16,256]{3,2,1,0:T(8,128)(2,1)S(1)} %get-tuple-element.128), channel_id=1, source_target_pairs={{0,4},{4,0},{1,5},{5,1},{2,6},{6,2},{3,7},{7,3},{8,12},{12,8},{9,1... | collective-permute-start | bytes 196616 | tf_op jit(solution)/shard_map/ppermute | solution.py:811
  81.4 1.0 %collective-permute-done.20.got_ref = bf16[320,256]{1,0:T(8,128)(2,1)S(1)} collective-permute-done((bf16[320,256]{1,0:T(8,128)(2,1)S(1)}, bf16[320,256]{1,0:T(8,128)(2,1)S(1)}, u32[]{:S(2)}, u32[]{:S(2)}) %collective-permute-start.20) | collective-permute-done | bytes 163872 | tf_op jit(solution)/shard_map/ppermute | solution.py:688
  82.5 1.0 %collective-permute-start.21 = (bf16[320,256]{1,0:T(8,128)(2,1)S(1)}, bf16[320,256]{1,0:T(8,128)(2,1)S(1)}, u32[]{:S(2)}, u32[]{:S(2)}) collective-permute-start(bf16[320,256]{1,0:T(8,128)(2,1)S(1)} %close.3.refs_0_), channel_id=1, source_target_pairs={{0,4},{4,0},{1,5},{5,1},{2,6},{6,2},{3,7},{7,3},{8,12},{12,8},{9,1... | collective-permute-start | bytes 491528 | tf_op jit(solution)/shard_map/ppermute | solution.py:688
  83.6 4.1 %collective-permute-done.22.refs_1_ = bf16[256,256]{1,0:T(8,128)(2,1)S(1)} collective-permute-done((bf16[256,256]{1,0:T(8,128)(2,1)S(1)}, bf16[256,256]{1,0:T(8,128)(2,1)S(1)}, u32[]{:S(2)}, u32[]{:S(2)}) %collective-permute-start.22) | collective-permute-done | bytes 131104 | tf_op jit(solution)/shard_map/ppermute | solution.py:688
  87.7 0.7 out_result.1
  88.4 2.4 %collective-permute-done.21.refs_1_ = bf16[320,256]{1,0:T(8,128)(2,1)S(1)} collective-permute-done((bf16[320,256]{1,0:T(8,128)(2,1)S(1)}, bf16[320,256]{1,0:T(8,128)(2,1)S(1)}, u32[]{:S(2)}, u32[]{:S(2)}) %collective-permute-start.21) | collective-permute-done | bytes 163872 | tf_op jit(solution)/shard_map/ppermute | solution.py:688
  90.9 0.7 in_result.1
  (43 shorter events, 1.3 us)
Async XLA Ops:
  0.6 0.9 copy-start.2
  1.5 7.9 %copy-start.3 = (bf16[1,16,16,256]{3,2,1,0:T(8,128)(2,1)S(1)}, bf16[1,16,16,256]{3,2,1,0:T(8,128)(2,1)}, u32[]{:S(2)}) copy-start(bf16[1,16,16,256]{3,2,1,0:T(8,128)(2,1)} %param.12) | copy-start | bytes 393220
  1.6 5.6 %collective-permute-start.2 = (bf16[3,16,256]{2,1,0:T(8,128)(2,1)S(1)}, bf16[3,16,256]{2,1,0:T(8,128)(2,1)S(1)}, u32[]{:S(2)}, u32[]{:S(2)}) collective-permute-start(bf16[3,16,256]{2,1,0:T(8,128)(2,1)S(1)} %get-tuple-element.76), channel_id=1, source_target_pairs={{0,1},{1,2},{2,3},{5,4},{6,5},{7,6},{8,9},{9,10},{10,11},{13,12},{... | collective-permute-start | bytes 73736 | tf_op jit(solution)/shard_map/ppermute | solution.py:216
  2.9 5.8 %collective-permute-start.3 = (bf16[3,16,256]{2,1,0:T(8,128)(2,1)S(1)}, bf16[3,16,256]{2,1,0:T(8,128)(2,1)S(1)}, u32[]{:S(2)}, u32[]{:S(2)}) collective-permute-start(bf16[3,16,256]{2,1,0:T(8,128)(2,1)S(1)} %get-tuple-element.77), channel_id=1, source_target_pairs={{4,1},{5,2},{6,3},{1,4},{2,5},{3,6},{12,9},{13,10},{14,11},{9,12},... | collective-permute-start | bytes 73736 | tf_op jit(solution)/shard_map/ppermute | solution.py:216
  8.7 9.4 %collective-permute-start.4 = (bf16[11,16,256]{2,1,0:T(8,128)(2,1)S(1)}, bf16[11,16,256]{2,1,0:T(8,128)(2,1)S(1)}, u32[]{:S(2)}, u32[]{:S(2)}) collective-permute-start(bf16[11,16,256]{2,1,0:T(8,128)(2,1)S(1)} %get-tuple-element.81), channel_id=1, source_target_pairs={{4,0},{0,4},{5,1},{1,5},{6,2},{2,6},{7,3},{3,7},{12,8},{8,12},{13,... | collective-permute-start | bytes 270344 | tf_op jit(solution)/shard_map/ppermute | solution.py:199
  9.4 2.2 %copy-start.4 = (f32[1,7,7,256]{3,0,2,1:T(1,128)S(1)}, f32[1,7,7,256]{3,0,2,1:T(1,128)}, u32[]{:S(2)}) copy-start(f32[1,7,7,256]{3,0,2,1:T(1,128)} %param.14) | copy-start | bytes 150532
  9.4 4.7 %copy-start.9 = (f32[1,256]{1,0:T(1,128)S(1)}, f32[1,256]{1,0:T(1,128)}, u32[]{:S(2)}) copy-start(f32[1,256]{1,0:T(1,128)} %refs_7_.1) | copy-start | bytes 3076
  9.5 4.6 %copy-start.5 = (f32[1,1024]{1,0:T(1,128)S(1)}, f32[1,1024]{1,0:T(1,128)}, u32[]{:S(2)}) copy-start(f32[1,1024]{1,0:T(1,128)} %refs_6_.1) | copy-start | bytes 12292
  9.5 7.6 %collective-permute-start = (bf16[9,16,256]{2,1,0:T(8,128)(2,1)S(1)}, bf16[9,16,256]{2,1,0:T(8,128)(2,1)S(1)}, u32[]{:S(2)}, u32[]{:S(2)}) collective-permute-start(bf16[9,16,256]{2,1,0:T(8,128)(2,1)S(1)} %get-tuple-element.67), channel_id=1, source_target_pairs={{4,0},{0,4},{5,1},{1,5},{6,2},{2,6},{7,3},{3,7},{12,8},{8,12},{13,... | collective-permute-start | bytes 221192 | tf_op jit(solution)/shard_map/ppermute | solution.py:199
  11.6 2.5 %copy-start.7 = (f32[1,256]{1,0:T(1,128)S(1)}, f32[1,256]{1,0:T(1,128)}, u32[]{:S(2)}) copy-start(f32[1,256]{1,0:T(1,128)} %refs_4_.1) | copy-start | bytes 3076
  11.6 2.5 %copy-start.8 = (f32[1,256]{1,0:T(1,128)S(1)}, f32[1,256]{1,0:T(1,128)}, u32[]{:S(2)}) copy-start(f32[1,256]{1,0:T(1,128)} %refs_5_.1) | copy-start | bytes 3076
  11.6 6.5 %collective-permute-start.1 = (f32[7,7,1,256]{3,2,1,0:T(1,128)S(1)}, f32[7,7,1,256]{3,2,1,0:T(1,128)S(1)}, u32[]{:S(2)}, u32[]{:S(2)}) collective-permute-start(f32[7,7,1,256]{3,2,1,0:T(1,128)S(1)} %bitcast.19), channel_id=1, source_target_pairs={{8,0},{16,8},{24,16},{9,1},{17,9},{25,17},{10,2},{18,10},{26,18},{... | collective-permute-start | bytes 150536 | tf_op jit(solution)/shard_map/ppermute | solution.py:470
  14.1 0.7 copy-start.6
  14.8 1.0 %copy-start = (bf16[1,256,1024]{2,1,0:T(8,128)(2,1)S(1)}, bf16[1,256,1024]{2,1,0:T(8,128)(2,1)}, u32[]{:S(2)}) copy-start(bf16[1,256,1024]{2,1,0:T(8,128)(2,1)} %param.18) | copy-start | bytes 1572868
  15.8 1.0 %copy-start.1 = (bf16[1,1024,256]{2,1,0:T(8,128)(2,1)S(1)}, bf16[1,1024,256]{2,1,0:T(8,128)(2,1)}, u32[]{:S(2)}) copy-start(bf16[1,1024,256]{2,1,0:T(8,128)(2,1)} %param.20) | copy-start | bytes 1572868
  21.9 10.6 %collective-permute-start.5 = (bf16[8,32,256]{2,1,0:T(8,128)(2,1)S(1)}, bf16[8,32,256]{2,1,0:T(8,128)(2,1)S(1)}, u32[]{:S(2)}, u32[]{:S(2)}) collective-permute-start(bf16[8,32,256]{2,1,0:T(8,128)(2,1)S(1)} %get-tuple-element.92), channel_id=1, source_target_pairs={{8,0},{16,8},{24,16},{9,1},{17,9},{25,17},{10,2},{18,10},{26,18},{... | collective-permute-start | bytes 393224 | tf_op jit(solution)/shard_map/ppermute | solution.py:470
  24.3 6.9 %collective-permute-start.6 = (bf16[3,32,256]{2,1,0:T(8,128)(2,1)S(1)}, bf16[3,32,256]{2,1,0:T(8,128)(2,1)S(1)}, u32[]{:S(2)}, u32[]{:S(2)}) collective-permute-start(bf16[3,32,256]{2,1,0:T(8,128)(2,1)S(1)} %get-tuple-element.93), channel_id=1, source_target_pairs={{8,4},{12,1},{9,5},{13,2},{10,6},{14,3},{11,7},{16,12},{20,9},{17,... | collective-permute-start | bytes 147464 | tf_op jit(solution)/shard_map/ppermute | solution.py:465
  26.2 6.3 %collective-permute-start.7 = (bf16[3,32,256]{2,1,0:T(8,128)(2,1)S(1)}, bf16[3,32,256]{2,1,0:T(8,128)(2,1)S(1)}, u32[]{:S(2)}, u32[]{:S(2)}) collective-permute-start(bf16[3,32,256]{2,1,0:T(8,128)(2,1)S(1)} %get-tuple-element.94), channel_id=1, source_target_pairs={{12,0},{9,4},{13,1},{10,5},{14,2},{11,6},{15,3},{20,8},{17,12},{21... | collective-permute-start | bytes 147464 | tf_op jit(solution)/shard_map/ppermute | solution.py:465
  34.4 12.1 %collective-permute-start.8 = (bf16[8,32,256]{2,1,0:T(8,128)(2,1)S(1)}, bf16[8,32,256]{2,1,0:T(8,128)(2,1)S(1)}, u32[]{:S(2)}, u32[]{:S(2)}) collective-permute-start(bf16[8,32,256]{2,1,0:T(8,128)(2,1)S(1)} %get-tuple-element.95), channel_id=1, source_target_pairs={{8,0},{16,8},{24,16},{9,1},{17,9},{25,17},{10,2},{18,10},{26,18},{... | collective-permute-start | bytes 393224 | tf_op jit(solution)/shard_map/ppermute | solution.py:470
  36.7 6.8 %collective-permute-start.10 = (bf16[3,32,256]{2,1,0:T(8,128)(2,1)S(1)}, bf16[3,32,256]{2,1,0:T(8,128)(2,1)S(1)}, u32[]{:S(2)}, u32[]{:S(2)}) collective-permute-start(bf16[3,32,256]{2,1,0:T(8,128)(2,1)S(1)} %get-tuple-element.97), channel_id=1, source_target_pairs={{12,0},{9,4},{13,1},{10,5},{14,2},{11,6},{15,3},{20,8},{17,12},{21... | collective-permute-start | bytes 147464 | tf_op jit(solution)/shard_map/ppermute | solution.py:465
  39.6 6.9 %collective-permute-start.9 = (bf16[3,32,256]{2,1,0:T(8,128)(2,1)S(1)}, bf16[3,32,256]{2,1,0:T(8,128)(2,1)S(1)}, u32[]{:S(2)}, u32[]{:S(2)}) collective-permute-start(bf16[3,32,256]{2,1,0:T(8,128)(2,1)S(1)} %get-tuple-element.96), channel_id=1, source_target_pairs={{8,4},{12,1},{9,5},{13,2},{10,6},{14,3},{11,7},{16,12},{20,9},{17,... | collective-permute-start | bytes 147464 | tf_op jit(solution)/shard_map/ppermute | solution.py:465
  48.3 10.2 %collective-permute-start.11 = (bf16[8,32,256]{2,1,0:T(8,128)(2,1)S(1)}, bf16[8,32,256]{2,1,0:T(8,128)(2,1)S(1)}, u32[]{:S(2)}, u32[]{:S(2)}) collective-permute-start(bf16[8,32,256]{2,1,0:T(8,128)(2,1)S(1)} %get-tuple-element.98), channel_id=1, source_target_pairs={{8,0},{16,8},{24,16},{9,1},{17,9},{25,17},{10,2},{18,10},{26,18},{... | collective-permute-start | bytes 393224 | tf_op jit(solution)/shard_map/ppermute | solution.py:470
  50.3 6.9 %collective-permute-start.12 = (bf16[3,32,256]{2,1,0:T(8,128)(2,1)S(1)}, bf16[3,32,256]{2,1,0:T(8,128)(2,1)S(1)}, u32[]{:S(2)}, u32[]{:S(2)}) collective-permute-start(bf16[3,32,256]{2,1,0:T(8,128)(2,1)S(1)} %get-tuple-element.99), channel_id=1, source_target_pairs={{8,4},{12,1},{9,5},{13,2},{10,6},{14,3},{11,7},{16,12},{20,9},{17,... | collective-permute-start | bytes 147464 | tf_op jit(solution)/shard_map/ppermute | solution.py:465
  52.2 6.3 %collective-permute-start.13 = (bf16[3,32,256]{2,1,0:T(8,128)(2,1)S(1)}, bf16[3,32,256]{2,1,0:T(8,128)(2,1)S(1)}, u32[]{:S(2)}, u32[]{:S(2)}) collective-permute-start(bf16[3,32,256]{2,1,0:T(8,128)(2,1)S(1)} %get-tuple-element.100), channel_id=1, source_target_pairs={{12,0},{9,4},{13,1},{10,5},{14,2},{11,6},{15,3},{20,8},{17,12},{21... | collective-permute-start | bytes 147464 | tf_op jit(solution)/shard_map/ppermute | solution.py:465
  59.3 4.0 %collective-permute-start.14 = (bf16[512,256]{1,0:T(8,128)(2,1)S(1)}, bf16[512,256]{1,0:T(8,128)(2,1)S(1)}, u32[]{:S(2)}, u32[]{:S(2)}) collective-permute-start(bf16[512,256]{1,0:T(8,128)(2,1)S(1)} %get-tuple-element.111.sent_ref), channel_id=1, source_target_pairs={{0,1},{1,0},{2,3},{3,2},{4,5},{5,4},{6,7},{7,6},{8,9},{9,8},{10,11... | collective-permute-start | bytes 786440 | tf_op jit(solution)/shard_map/ppermute | solution.py:688
  64.4 1.6 %collective-permute-start.15 = (bf16[576,256]{1,0:T(8,128)(2,1)S(1)}, bf16[576,256]{1,0:T(8,128)(2,1)S(1)}, u32[]{:S(2)}, u32[]{:S(2)}) collective-permute-start(bf16[576,256]{1,0:T(8,128)(2,1)S(1)} %get-tuple-element.119.sent_ref), channel_id=1, source_target_pairs={{0,1},{1,0},{2,3},{3,2},{4,5},{5,4},{6,7},{7,6},{8,9},{9,8},{10,11... | collective-permute-start | bytes 884744 | tf_op jit(solution)/shard_map/ppermute | solution.py:688
  64.8 5.5 %collective-permute-start.16 = (bf16[256,256]{1,0:T(8,128)(2,1)S(1)}, bf16[256,256]{1,0:T(8,128)(2,1)S(1)}, u32[]{:S(2)}, u32[]{:S(2)}) collective-permute-start(bf16[256,256]{1,0:T(8,128)(2,1)S(1)} %get-tuple-element.112.sent_ref), channel_id=1, source_target_pairs={{0,2},{1,3},{2,0},{3,1},{4,6},{5,7},{6,4},{7,5},{8,10},{9,11},{10,... | collective-permute-start | bytes 393224 | tf_op jit(solution)/shard_map/ppermute | solution.py:688
  70.4 6.2 %collective-permute-start.17 = (bf16[3,32,256]{2,1,0:T(8,128)(2,1)S(1)}, bf16[3,32,256]{2,1,0:T(8,128)(2,1)S(1)}, u32[]{:S(2)}, u32[]{:S(2)}) collective-permute-start(bf16[3,32,256]{2,1,0:T(8,128)(2,1)S(1)} %get-tuple-element.123), channel_id=1, source_target_pairs={{0,4},{4,1},{1,5},{5,2},{2,6},{6,3},{3,7},{8,12},{12,9},{9,13},{13... | collective-permute-start | bytes 147464 | tf_op jit(solution)/shard_map/ppermute | solution.py:465
  72.3 5.7 %collective-permute-start.18 = (bf16[3,32,256]{2,1,0:T(8,128)(2,1)S(1)}, bf16[3,32,256]{2,1,0:T(8,128)(2,1)S(1)}, u32[]{:S(2)}, u32[]{:S(2)}) collective-permute-start(bf16[3,32,256]{2,1,0:T(8,128)(2,1)S(1)} %get-tuple-element.124), channel_id=1, source_target_pairs={{4,0},{1,4},{5,1},{2,5},{6,2},{3,6},{7,3},{12,8},{9,12},{13,9},{10... | collective-permute-start | bytes 147464 | tf_op jit(solution)/shard_map/ppermute | solution.py:465
  76.3 6.2 %collective-permute-start.20 = (bf16[320,256]{1,0:T(8,128)(2,1)S(1)}, bf16[320,256]{1,0:T(8,128)(2,1)S(1)}, u32[]{:S(2)}, u32[]{:S(2)}) collective-permute-start(bf16[320,256]{1,0:T(8,128)(2,1)S(1)} %get-tuple-element.120.sent_ref), channel_id=1, source_target_pairs={{0,2},{1,3},{2,0},{3,1},{4,6},{5,7},{6,4},{7,5},{8,10},{9,11},{10,... | collective-permute-start | bytes 491528 | tf_op jit(solution)/shard_map/ppermute | solution.py:688
  78.9 4.6 %collective-permute-start.19 = (bf16[1,8,16,256]{3,2,1,0:T(8,128)(2,1)S(1)}, bf16[1,8,16,256]{3,2,1,0:T(8,128)(2,1)S(1)}, u32[]{:S(2)}, u32[]{:S(2)}) collective-permute-start(bf16[1,8,16,256]{3,2,1,0:T(8,128)(2,1)S(1)} %get-tuple-element.128), channel_id=1, source_target_pairs={{0,4},{4,0},{1,5},{5,1},{2,6},{6,2},{3,7},{7,3},{8,12},{12,8},{9,1... | collective-permute-start | bytes 196616 | tf_op jit(solution)/shard_map/ppermute | solution.py:811
  81.3 6.4 %collective-permute-start.22 = (bf16[256,256]{1,0:T(8,128)(2,1)S(1)}, bf16[256,256]{1,0:T(8,128)(2,1)S(1)}, u32[]{:S(2)}, u32[]{:S(2)}) collective-permute-start(bf16[256,256]{1,0:T(8,128)(2,1)S(1)} %close.2.refs_0_), channel_id=1, source_target_pairs={{0,4},{4,0},{1,5},{5,1},{2,6},{6,2},{3,7},{7,3},{8,12},{12,8},{9,1... | collective-permute-start | bytes 393224 | tf_op jit(solution)/shard_map/ppermute | solution.py:688
  82.5 8.4 %collective-permute-start.21 = (bf16[320,256]{1,0:T(8,128)(2,1)S(1)}, bf16[320,256]{1,0:T(8,128)(2,1)S(1)}, u32[]{:S(2)}, u32[]{:S(2)}) collective-permute-start(bf16[320,256]{1,0:T(8,128)(2,1)S(1)} %close.3.refs_0_), channel_id=1, source_target_pairs={{0,4},{4,0},{1,5},{5,1},{2,6},{6,2},{3,7},{7,3},{8,12},{12,8},{9,1... | collective-permute-start | bytes 491528 | tf_op jit(solution)/shard_map/ppermute | solution.py:688
  83.6 4.8 %copy-start.10 = (bf16[2,8,16,256]{3,1,0,2:T(8,128)(2,1)}, bf16[2,8,16,256]{3,1,0,2:T(8,128)(2,1)S(1)}, u32[]{:S(2)}) copy-start(bf16[2,8,16,256]{3,1,0,2:T(8,128)(2,1)S(1)} %copy_dynamic-update-slice_fusion) | copy-start | bytes 393220

commit v3 on v2

--- a/solution.py
+++ b/solution.py
@@ -42,18 +42,18 @@
             sizes.append(high - low)
         return max(sizes)
 
-    def main_start(self, r):
-        return jnp.clip(r * self.width - self.margin, 0, self.across - self.main_size())
-
-    def needs_left(self, r):
-        return r * self.width < self.margin
-
-    def needs_right(self, r):
-        return (r + 1) * self.width + self.margin > self.across
+    def turned(self, place, c):
+        return place + (c % 2) * (self.rows - 1 - 2 * place)
+
+    def place(self, r):
+        return self.turned(r, lax.axis_index("col"))
+
+    def main_start(self, place):
+        return jnp.clip(place * self.width - self.margin, 0, self.across - self.main_size())
 
     def sides(self):
-        left = [r for r in range(self.rows) if self.needs_left(r)]
-        right = [r for r in range(self.rows) if self.needs_right(r)]
+        left = [u for u in range(self.rows) if u * self.width < self.margin]
+        right = [u for u in range(self.rows) if (u + 1) * self.width + self.margin > self.across]
         if set(left) & set(right):
             return [(left, []), ([], right)]
         return [(left, right)]
@@ -70,7 +70,8 @@
         return (s * self.rows + r) * self.cols + c
 
     def strip(self, s, t):
-        return self.index(s, t % self.rows, t // self.rows)
+        c = t // self.rows
+        return self.index(s, self.turned(t % self.rows, c), c)
 
     def own(self, column):
         return self.margin <= column < self.margin + self.width
@@ -102,28 +103,40 @@
 
 
 def pack_kernel(plan, x_ref, *refs):
-    rows, across = plan.rows, plan.across
     outs, xt = refs[:-1], refs[-1]
     me = lax.axis_index("row")
     xt[...] = jnp.swapaxes(x_ref[...].astype(f32), 0, 1).astype(bf16)
-    nx, m = plan.main_size(), plan.margin
-    for dr in range(rows):
-        target = lax.rem(me - dr + rows, rows)
-        outs[dr][...] = xt[pl.ds(plan.main_start(target), nx)]
-    for k, (left, right) in enumerate(plan.sides()):
-        for dr in range(rows):
-            target = lax.rem(me - dr + rows, rows)
-            is_left = functools.reduce(jnp.logical_or, [target == r for r in left], jnp.bool_(False))
-            outs[rows * (1 + k) + dr][...] = xt[pl.ds(jnp.where(is_left, across - m, 0), m)]
+    for dr in range(plan.rows):
+        target = plan.place(lax.rem(me - dr + plan.rows, plan.rows))
+        outs[dr][...] = xt[pl.ds(plan.main_start(target), plan.main_size())]
 
 
 def pack(plan, x):
-    rows, h, c = plan.rows, plan.height, plan.channels
-    outs = [shape((plan.main_size(), h, c), bf16)] * rows
-    outs += [shape((plan.margin, h, c), bf16)] * (rows * len(plan.sides()))
+    h, c = plan.height, plan.channels
+    outs = [shape((plan.main_size(), h, c), bf16)] * plan.rows
     return call(
         functools.partial(pack_kernel, plan), "pack", [x], outs, [pltpu.VMEM((plan.across, h, c), bf16)]
     )
+
+
+def among(value, numbers):
+    return functools.reduce(jnp.logical_or, [value == k for k in numbers], jnp.bool_(False))
+
+
+def pack_sides_kernel(plan, *refs):
+    pieces, outs = refs[: plan.rows], refs[plan.rows :]
+    me = lax.axis_index("row")
+    m, nx = plan.margin, plan.main_size()
+    for out, (left, right) in zip(outs, plan.sides()):
+        is_left = among(plan.place(me), left)
+        for dr, piece in enumerate(pieces):
+            top = pl.multiple_of(lax.rem(me + dr, plan.rows) * plan.height, plan.height)
+            out[:, pl.ds(top, plan.height), :] = jnp.where(is_left, piece[0:m], piece[nx - m : nx])
+
+
+def pack_sides(plan, pieces):
+    outs = [shape((plan.margin, plan.full, plan.channels), bf16)] * len(plan.sides())
+    return call(functools.partial(pack_sides_kernel, plan), "pack_sides", pieces, outs, [])
 
 
 def pack_upstream_kernel(plan, tissue_ref, g_ref, *refs):
@@ -148,7 +161,7 @@
     gt[...] = jnp.swapaxes(g_ref[...].astype(f32), 0, 1).astype(bf16)
     w = plan.width
     for dr in range(rows):
-        target = lax.rem(me - dr + rows, rows)
+        target = plan.place(lax.rem(me - dr + rows, rows))
         outs[dr][0:w] = gt[pl.ds(target * w, w)]
         outs[dr][w] = slot(target * w)
 
@@ -203,17 +216,16 @@
 def exchange_sides(plan, pieces):
     rows, cols = plan.rows, plan.cols
     received = []
-    for k, (left, right) in enumerate(plan.sides()):
-        for dr in range(rows):
-            pairs = []
-            for s in range(plan.segments):
-                for r in range(rows):
-                    for c in range(cols):
-                        step = (-1 if r in left else 0) + (1 if r in right else 0)
-                        if step != 0 and 0 <= c + step < cols:
-                            source = plan.index(s, (r + dr) % rows, c + step)
-                            pairs.append((source, plan.index(s, r, c)))
-            received.append(lax.ppermute(pieces[rows * k + dr], LINE, pairs))
+    for piece, (left, right) in zip(pieces, plan.sides()):
+        pairs = []
+        for s in range(plan.segments):
+            for c in range(cols):
+                for u in range(rows):
+                    step = (-1 if u in left else 0) + (1 if u in right else 0)
+                    if step != 0 and 0 <= c + step < cols:
+                        source = plan.index(s, plan.turned(rows - 1 - u, c + step), c + step)
+                        pairs.append((source, plan.index(s, plan.turned(u, c), c)))
+        received.append(lax.ppermute(piece, LINE, pairs))
     return received
 
 
@@ -246,28 +258,29 @@
 
 def forward_kernel(plan, *refs):
     rows, full, h = plan.rows, plan.full, plan.height
-    pieces = refs[: rows * (1 + len(plan.sides()))]
-    refs = refs[len(pieces) :]
+    mains, sides = refs[:rows], refs[rows : rows + len(plan.sides())]
+    refs = refs[rows + len(sides) :]
     (taps_ref, conv_bias_ref, gain_ref, bias_ref, w_in_ref, b_in_ref) = refs[:6]
     (xw_ref, standard_ref, inv_ref, gate_ref, hidden_ref, normed_ref) = refs[6:12]
     wide_x, conv_ref, pre_ref = refs[12:]
     me = lax.axis_index("row")
+    place = plan.place(me)
     m, w, nx = plan.margin, plan.width, plan.main_size()
 
     clear_rims(wide_x, full)
-    parts = [(m + plan.main_start(me), nx, pieces[dr], dr) for dr in range(rows)]
-    for k, (left, right) in enumerate(plan.sides()):
-        is_left = functools.reduce(jnp.logical_or, [me == r for r in left], jnp.bool_(False))
-        start = jnp.where(is_left, 0, m + plan.across)
-        parts += [(start, m, pieces[rows * (1 + k) + dr], dr) for dr in range(rows)]
-    for start, count, piece, dr in parts:
+    parts = []
+    for dr, piece in enumerate(mains):
         top = pl.multiple_of(lax.rem(me + dr, rows) * h, h)
+        parts.append((m + plan.main_start(place), nx, top, h, piece))
+    for piece, (left, right) in zip(sides, plan.sides()):
+        parts.append((jnp.where(among(place, left), 0, m + plan.across), m, 0, full, piece))
+    for start, count, top, height, piece in parts:
         for half in range(plan.halves):
-            wide_x[half, pl.ds(start, count), pl.ds(PAD + top, h), :] = piece[
+            wide_x[half, pl.ds(start, count), pl.ds(PAD + top, height), :] = piece[
                 :, :, half * LANES : (half + 1) * LANES
             ].astype(f32)
 
-    base = me * w
+    base = place * w
     xw_ref[...] = wide_x[:, pl.ds(base, plan.padded)]
 
     def load(column, rows_at, half):
@@ -804,21 +817,20 @@
     me = lax.axis_index("row")
     tile = jnp.zeros((rows, *strips.shape[1:]), strips.dtype)
     own = lax.dynamic_index_in_dim(strips, me, 0, keepdims=True)
-    tile = lax.dynamic_update_slice_in_dim(tile, own, me, 0)
+    tile = lax.dynamic_update_slice_in_dim(tile, own, plan.place(me), 0)
     for dr in range(1, rows):
         target = lax.rem(me + dr, rows)
         piece = lax.dynamic_index_in_dim(strips, target, 0, keepdims=True)
         got = lax.ppermute(piece, "row", [(r, (r + dr) % rows) for r in range(rows)])
-        tile = lax.dynamic_update_slice_in_dim(tile, got, lax.rem(me - dr + rows, rows), 0)
+        source = plan.place(lax.rem(me - dr + rows, rows))
+        tile = lax.dynamic_update_slice_in_dim(tile, got, source, 0)
     tile = tile.reshape(plan.across, plan.height, plan.channels)
     return jnp.swapaxes(tile, 0, 1)
 
 
 def one_crop(plan, norm_scale, tissue, saved, out_grad, params):
-    packed = pack(plan, saved)
-    mains, sides = packed[: plan.rows], packed[plan.rows :]
-    sides, mains = lax.optimization_barrier((exchange_sides(plan, sides), mains))
-    pieces = exchange_mains(plan, mains) + sides
+    mains = exchange_mains(plan, pack(plan, saved))
+    pieces = [*mains, *exchange_sides(plan, pack_sides(plan, mains))]
     upstream = exchange_mains(plan, pack_upstream(plan, tissue, out_grad))
     taps_above = to_segment_below(plan, params[0])
     taps, w_in, w_out, conv_bias, gain, bias, b_in, scale = load(params)
@@ -841,9 +853,9 @@
     norm_grad, _ = lax.optimization_barrier((norm_grad, out_sum.send))
     conv_grad, send, *edges = taps_step(plan, norm_grad, halves, gain, standard, inv, xw)
     in_sum = Reduction(plan, halves, send, in_share(plan)[1], taps_rows(plan))
-    out_sum.close(in_sum.send)
+    out_sum.close()
     grad_out = out_result(plan, norm_scale, out_sum.terms())
-    edges, _, _ = lax.optimization_barrier((edges, in_sum.send, out_sum.total))
+    edges, _ = lax.optimization_barrier((edges, in_sum.send))
     strips = finish(plan, upstream, conv_grad, taps, send_edges(plan, edges, 0))
     in_sum.close()
     grad_in, grad_taps = in_result(plan, norm_scale, in_sum.terms())

time: 93 us -> 78.4 us (0.84)
  waiting for transfers between devices: 29.7 us -> 17.9 us
  starting transfers between devices: 42.8 us -> 40.8 us
    ppermute x6, waiting for transfers between devices: 13.1 us -> 7.57 us  [swap(): return lax.ppermute(value, axis, [(i, i ^ bit) for i in range(size)])]
    ppermute x8, waiting for transfers between devices: 14.1 us -> 9.63 us  [send_edges(): received.append(lax.ppermute(piece, LINE, pairs))]
    ppermute x2 -> x1, starting transfers between devices: 5.59 us -> 2.05 us  [exchange_sides(): received.append(lax.ppermute(piece, LINE, pairs))]
    ppermute x1, starting transfers between devices: 2.4 us -> 0.45 us  [to_tile(): lax.ppermute(piece, 'row', [(r, (r + dr) % rows) for r in range(rows)])]
    ppermute x6, starting transfers between devices: 4.66 us -> 6.52 us  [swap(): return lax.ppermute(value, axis, [(i, i ^ bit) for i in range(size)])]
    ppermute x4, starting transfers between devices: 9.11 us -> 10.9 us  [to_segment_below(): lax.ppermute(value, 'segment', [(s, s - 1) for s in range(1, plan.segment...]
    ppermute x2 -> x1, waiting for transfers between devices: 1.49 us -> 0.01 us  [exchange_sides(): received.append(lax.ppermute(piece, LINE, pairs))]
    pallas_call x17 -> x18, Pallas kernels: 13.4 us -> 13.5 us  [call(): pl.pallas_call(kernel, out_shape=outs, in_specs=[vmem()] * len(operands),...]
  transfers between devices with their start and end apart: 23 -> 22, of which waited for: 16 -> 13; matrix products, arithmetic and copies ran while one was open for 0% -> 0% of each run, Pallas kernels for 4% -> 4%
where the time goes in v3:
time: 78.4 us; the launch traced here: 77.8 us
  starting transfers between devices  40.8 us (52%)
  waiting for transfers between devices  17.9 us (23%)
  Pallas kernels  13.7 us (17%)
  local copies, waits for them, and re-layouts  3.74 us (5%)
  between operations  1.66 us (2%)
    ppermute x8, starting transfers between devices, send_edges(): received.append(lax.ppermute(piece, LINE, pairs))  18.7 us
    pallas_call x18, Pallas kernels, call(): pl.pallas_call(kernel, out_shape=outs, in_specs=[vmem()] * len(operands),...  13.5 us
    ppermute x4, starting transfers between devices, to_segment_below(): lax.ppermute(value, 'segment', [(s, s - 1) for s in range(1, plan.segment...  10.9 us
    ppermute x8, waiting for transfers between devices, send_edges(): received.append(lax.ppermute(piece, LINE, pairs))  9.63 us
    ppermute x6, waiting for transfers between devices, swap(): return lax.ppermute(value, axis, [(i, i ^ bit) for i in range(size)])  7.57 us
    ppermute x6, starting transfers between devices, swap(): return lax.ppermute(value, axis, [(i, i ^ bit) for i in range(size)])  6.52 us
    unnamed x22, local copies, waits for them, and re-layouts  3.65 us
    ppermute x2, starting transfers between devices, exchange_mains(): received.append(lax.ppermute(pieces[dr], 'row', pairs))  2.16 us
  transfers between devices with their start and end apart: 22, of which 13 were waited for; matrix products, arithmetic and copies ran while one was open for 0% of the time, Pallas kernels for 4%

profile of v3, /device:TPU:18, one launch (start us, length us, event | category | flops | bytes accessed | tf_op | source)
XLA Modules:
  0.0 77.8 jit_solution(11088992557498247991)
XLA Ops:
  0.6 0.9 %copy-done.2 = bf16[1,1,16,16,256]{4,3,2,1,0:T(8,128)(2,1)S(1)} copy-done((bf16[1,1,16,16,256]{4,3,2,1,0:T(8,128)(2,1)S(1)}, bf16[1,1,16,16,256]{4,3,2,1,0:T(8,128)(2,1)}, u32[]{:S(2)}) %copy-start.2) | copy-done | bytes 131096
  1.6 0.6 collective-permute-start.2
  3.0 1.6 %collective-permute-start = (bf16[9,16,256]{2,1,0:T(8,128)(2,1)S(1)}, bf16[9,16,256]{2,1,0:T(8,128)(2,1)S(1)}, u32[]{:S(2)}, u32[]{:S(2)}) collective-permute-start(bf16[9,16,256]{2,1,0:T(8,128)(2,1)S(1)} %get-tuple-element.60), channel_id=1, source_target_pairs={{4,0},{0,4},{5,1},{1,5},{6,2},{2,6},{7,3},{3,7},{12,8},{8,12},{13,... | collective-permute-start | bytes 221192 | tf_op jit(solution)/shard_map/ppermute | solution.py:212
  4.5 2.3 %collective-permute-start.1 = (f32[7,7,1,256]{3,2,1,0:T(1,128)S(1)}, f32[7,7,1,256]{3,2,1,0:T(1,128)S(1)}, u32[]{:S(2)}, u32[]{:S(2)}) collective-permute-start(f32[7,7,1,256]{3,2,1,0:T(1,128)S(1)} %bitcast.19), channel_id=1, source_target_pairs={{8,0},{16,8},{24,16},{9,1},{17,9},{25,17},{10,2},{18,10},{26,18},{... | collective-permute-start | bytes 150536 | tf_op jit(solution)/shard_map/ppermute | solution.py:483
  7.0 2.1 %collective-permute-start.3 = (bf16[3,32,256]{2,1,0:T(8,128)(2,1)S(1)}, bf16[3,32,256]{2,1,0:T(8,128)(2,1)S(1)}, u32[]{:S(2)}, u32[]{:S(2)}) collective-permute-start(bf16[3,32,256]{2,1,0:T(8,128)(2,1)S(1)} %pack_sides.1), channel_id=1, source_target_pairs={{5,4},{4,5},{2,1},{1,2},{7,6},{6,7},{13,12},{12,13},{10,9},{9,10},... | collective-permute-start | bytes 147464 | tf_op jit(solution)/shard_map/ppermute | solution.py:228
  9.1 0.6 copy-done.6
  9.7 1.0 %copy-done = bf16[1,256,1024]{2,1,0:T(8,128)(2,1)S(1)} copy-done((bf16[1,256,1024]{2,1,0:T(8,128)(2,1)S(1)}, bf16[1,256,1024]{2,1,0:T(8,128)(2,1)}, u32[]{:S(2)}) %copy-start) | copy-done | bytes 524312
  10.8 1.0 %copy-done.1 = bf16[1,1024,256]{2,1,0:T(8,128)(2,1)S(1)} copy-done((bf16[1,1024,256]{2,1,0:T(8,128)(2,1)S(1)}, bf16[1,1024,256]{2,1,0:T(8,128)(2,1)}, u32[]{:S(2)}) %copy-start.1) | copy-done | bytes 524312
  12.2 2.1 %forward.1 = (f32[2,14,48,128]{3,2,1,0:T(8,128)S(1)}, f32[256,256]{1,0:T(8,128)S(1)}, f32[256,128]{1,0:T(8,128)S(1)}, bf16[256,1024]{1,0:T(8,128)(2,1)S(1)}, bf1...) custom-call(bf16[11,16,256]{2,1,0:T(8,128)(2,1)S(1)} %get-tuple-element.69.refs_0_, ...), custom_call_target="tpu_custom_call" | custom-call | flops 2415919104 | bytes 1000 | tf_op jit(solution)/shard_map/forward/pallas_call | solution.py:93
  14.3 1.7 %backward.3 = (bf16[8,32,256]{2,1,0:T(8,128)(2,1)S(1)}, bf16[3,32,256]{2,1,0:T(8,128)(2,1)S(1)}, bf16[3,32,256]{2,1,0:T(8,128)(2,1)S(1)}) custom-call(bf16[8,32,256]{2,1,0:T(8,128)(2,1)S(1)} %get-tuple-element.63.og_ref, f32[1,256]{1,0:T(1,128)S(1)} %get-tuple-element.65.refs_0_.refs_4_, f32[1,256]{1,0:T(1,128)S(1)} %get-tuple-element.66.refs_5_.refs_1_.gain_ref, ...), custom_call_target="tpu_custom_call" | custom-call | flops 268435456 | bytes 1000 | tf_op jit(solution)/shard_map/backward/pallas_call | solution.py:93
  16.0 2.4 %collective-permute-start.4 = (bf16[8,32,256]{2,1,0:T(8,128)(2,1)S(1)}, bf16[8,32,256]{2,1,0:T(8,128)(2,1)S(1)}, u32[]{:S(2)}, u32[]{:S(2)}) collective-permute-start(bf16[8,32,256]{2,1,0:T(8,128)(2,1)S(1)} %get-tuple-element.79), channel_id=1, source_target_pairs={{8,0},{16,8},{24,16},{9,1},{17,9},{25,17},{10,2},{18,10},{26,18},{... | collective-permute-start | bytes 393224 | tf_op jit(solution)/shard_map/ppermute | solution.py:483
  18.3 2.1 %collective-permute-start.5 = (bf16[3,32,256]{2,1,0:T(8,128)(2,1)S(1)}, bf16[3,32,256]{2,1,0:T(8,128)(2,1)S(1)}, u32[]{:S(2)}, u32[]{:S(2)}) collective-permute-start(bf16[3,32,256]{2,1,0:T(8,128)(2,1)S(1)} %get-tuple-element.80), channel_id=1, source_target_pairs={{8,4},{12,5},{13,1},{9,2},{10,6},{14,7},{15,3},{16,12},{20,13},{21... | collective-permute-start | bytes 147464 | tf_op jit(solution)/shard_map/ppermute | solution.py:478
  20.4 2.4 %collective-permute-start.6 = (bf16[3,32,256]{2,1,0:T(8,128)(2,1)S(1)}, bf16[3,32,256]{2,1,0:T(8,128)(2,1)S(1)}, u32[]{:S(2)}, u32[]{:S(2)}) collective-permute-start(bf16[3,32,256]{2,1,0:T(8,128)(2,1)S(1)} %get-tuple-element.81), channel_id=1, source_target_pairs={{12,0},{13,4},{9,5},{10,1},{14,2},{15,6},{11,7},{20,8},{21,12},{17... | collective-permute-start | bytes 147464 | tf_op jit(solution)/shard_map/ppermute | solution.py:478
  22.8 2.7 %collective-permute-done.5.refs_2_ = bf16[3,32,256]{2,1,0:T(8,128)(2,1)S(1)} collective-permute-done((bf16[3,32,256]{2,1,0:T(8,128)(2,1)S(1)}, bf16[3,32,256]{2,1,0:T(8,128)(2,1)S(1)}, u32[]{:S(2)}, u32[]{:S(2)}) %collective-permute-start.5) | collective-permute-done | bytes 49184 | tf_op jit(solution)/shard_map/ppermute | solution.py:478
  25.5 0.4 collective-permute-done.6.refs_3_
  25.9 1.9 %backward.4 = (bf16[8,32,256]{2,1,0:T(8,128)(2,1)S(1)}, bf16[3,32,256]{2,1,0:T(8,128)(2,1)S(1)}, bf16[3,32,256]{2,1,0:T(8,128)(2,1)S(1)}) custom-call(bf16[8,32,256]{2,1,0:T(8,128)(2,1)S(1)} %get-tuple-element.63.og_ref, f32[7,7,1,256]{3,2,1,0:T(1,128)S(1)} %collective-permute-done.1.refs_0_, bf16[8,32,256]{2,1,0:T(8,128)(2,1)S(1)} %collective-permute-done.4.refs_1_, ...), custom_call_target="tpu_custom_call" | custom-call | flops 268435456 | bytes 1000 | tf_op jit(solution)/shard_map/backward/pallas_call | solution.py:93
  27.8 3.4 %collective-permute-start.7 = (bf16[8,32,256]{2,1,0:T(8,128)(2,1)S(1)}, bf16[8,32,256]{2,1,0:T(8,128)(2,1)S(1)}, u32[]{:S(2)}, u32[]{:S(2)}) collective-permute-start(bf16[8,32,256]{2,1,0:T(8,128)(2,1)S(1)} %get-tuple-element.82), channel_id=1, source_target_pairs={{8,0},{16,8},{24,16},{9,1},{17,9},{25,17},{10,2},{18,10},{26,18},{... | collective-permute-start | bytes 393224 | tf_op jit(solution)/shard_map/ppermute | solution.py:483
  31.2 1.9 %collective-permute-start.8 = (bf16[3,32,256]{2,1,0:T(8,128)(2,1)S(1)}, bf16[3,32,256]{2,1,0:T(8,128)(2,1)S(1)}, u32[]{:S(2)}, u32[]{:S(2)}) collective-permute-start(bf16[3,32,256]{2,1,0:T(8,128)(2,1)S(1)} %get-tuple-element.83), channel_id=1, source_target_pairs={{8,4},{12,5},{13,1},{9,2},{10,6},{14,7},{15,3},{16,12},{20,13},{21... | collective-permute-start | bytes 147464 | tf_op jit(solution)/shard_map/ppermute | solution.py:478
  33.1 2.2 %collective-permute-start.9 = (bf16[3,32,256]{2,1,0:T(8,128)(2,1)S(1)}, bf16[3,32,256]{2,1,0:T(8,128)(2,1)S(1)}, u32[]{:S(2)}, u32[]{:S(2)}) collective-permute-start(bf16[3,32,256]{2,1,0:T(8,128)(2,1)S(1)} %get-tuple-element.84), channel_id=1, source_target_pairs={{12,0},{13,4},{9,5},{10,1},{14,2},{15,6},{11,7},{20,8},{21,12},{17... | collective-permute-start | bytes 147464 | tf_op jit(solution)/shard_map/ppermute | solution.py:478
  35.3 2.7 %collective-permute-done.8.refs_2_ = bf16[3,32,256]{2,1,0:T(8,128)(2,1)S(1)} collective-permute-done((bf16[3,32,256]{2,1,0:T(8,128)(2,1)S(1)}, bf16[3,32,256]{2,1,0:T(8,128)(2,1)S(1)}, u32[]{:S(2)}, u32[]{:S(2)}) %collective-permute-start.8) | collective-permute-done | bytes 49184 | tf_op jit(solution)/shard_map/ppermute | solution.py:478
  38.1 0.5 collective-permute-done.9.refs_3_
  38.5 1.9 %backward.5 = (bf16[8,32,256]{2,1,0:T(8,128)(2,1)S(1)}, bf16[3,32,256]{2,1,0:T(8,128)(2,1)S(1)}, bf16[3,32,256]{2,1,0:T(8,128)(2,1)S(1)}) custom-call(bf16[8,32,256]{2,1,0:T(8,128)(2,1)S(1)} %get-tuple-element.63.og_ref, f32[7,7,1,256]{3,2,1,0:T(1,128)S(1)} %collective-permute-done.1.refs_0_, bf16[8,32,256]{2,1,0:T(8,128)(2,1)S(1)} %collective-permute-done.7.refs_1_, ...), custom_call_target="tpu_custom_call" | custom-call | flops 268435456 | bytes 1000 | tf_op jit(solution)/shard_map/backward/pallas_call | solution.py:93
  40.4 2.9 %collective-permute-start.10 = (bf16[8,32,256]{2,1,0:T(8,128)(2,1)S(1)}, bf16[8,32,256]{2,1,0:T(8,128)(2,1)S(1)}, u32[]{:S(2)}, u32[]{:S(2)}) collective-permute-start(bf16[8,32,256]{2,1,0:T(8,128)(2,1)S(1)} %get-tuple-element.85), channel_id=1, source_target_pairs={{8,0},{16,8},{24,16},{9,1},{17,9},{25,17},{10,2},{18,10},{26,18},{... | collective-permute-start | bytes 393224 | tf_op jit(solution)/shard_map/ppermute | solution.py:483
  43.3 1.9 %collective-permute-start.11 = (bf16[3,32,256]{2,1,0:T(8,128)(2,1)S(1)}, bf16[3,32,256]{2,1,0:T(8,128)(2,1)S(1)}, u32[]{:S(2)}, u32[]{:S(2)}) collective-permute-start(bf16[3,32,256]{2,1,0:T(8,128)(2,1)S(1)} %get-tuple-element.86), channel_id=1, source_target_pairs={{8,4},{12,5},{13,1},{9,2},{10,6},{14,7},{15,3},{16,12},{20,13},{21... | collective-permute-start | bytes 147464 | tf_op jit(solution)/shard_map/ppermute | solution.py:478
  45.2 2.4 %collective-permute-start.12 = (bf16[3,32,256]{2,1,0:T(8,128)(2,1)S(1)}, bf16[3,32,256]{2,1,0:T(8,128)(2,1)S(1)}, u32[]{:S(2)}, u32[]{:S(2)}) collective-permute-start(bf16[3,32,256]{2,1,0:T(8,128)(2,1)S(1)} %get-tuple-element.87), channel_id=1, source_target_pairs={{12,0},{13,4},{9,5},{10,1},{14,2},{15,6},{11,7},{20,8},{21,12},{17... | collective-permute-start | bytes 147464 | tf_op jit(solution)/shard_map/ppermute | solution.py:478
  47.6 0.2 turn.1
  47.9 2.9 %collective-permute-done.11.refs_2_ = bf16[3,32,256]{2,1,0:T(8,128)(2,1)S(1)} collective-permute-done((bf16[3,32,256]{2,1,0:T(8,128)(2,1)S(1)}, bf16[3,32,256]{2,1,0:T(8,128)(2,1)S(1)}, u32[]{:S(2)}, u32[]{:S(2)}) %collective-permute-start.11) | collective-permute-done | bytes 49184 | tf_op jit(solution)/shard_map/ppermute | solution.py:478
  50.7 0.4 collective-permute-done.12.refs_3_
  51.1 0.7 grad_out.1
  51.9 1.3 %collective-permute-start.13 = (bf16[512,256]{1,0:T(8,128)(2,1)S(1)}, bf16[512,256]{1,0:T(8,128)(2,1)S(1)}, u32[]{:S(2)}, u32[]{:S(2)}) collective-permute-start(bf16[512,256]{1,0:T(8,128)(2,1)S(1)} %get-tuple-element.98.sent_ref), channel_id=1, source_target_pairs={{0,1},{1,0},{2,3},{3,2},{4,5},{5,4},{6,7},{7,6},{8,9},{9,8},{10,11... | collective-permute-start | bytes 786440 | tf_op jit(solution)/shard_map/ppermute | solution.py:701
  53.2 1.1 %grad_in.1 = (f32[256,256]{1,0:T(8,128)S(1)}, f32[2,2,256,256]{3,2,1,0:T(8,128)S(1)}) custom-call(bf16[256,256]{1,0:T(8,128)(2,1)S(1)} %get-tuple-element.94.bg_ref, bf16[256,1024]{1,0:T(8,128)(2,1)S(1)} %get-tuple-element.67.refs_7_.refs_2_.refs_6_.w_in_ref, bf16[1024,256]{1,0:T(8,128)(2,1)S(1)} %get-tuple-element.68.refs_3_.refs_7_.w_out_ref, ...), custom_call_target="tpu_custom_call" | custom-call | flops 402653184 | bytes 1000 | tf_op jit(solution)/shard_map/grad_in/pallas_call | solution.py:93
  54.4 1.1 %grad_taps.1 = (f32[2,8,48,128]{3,2,1,0:T(8,128)S(1)}, bf16[576,256]{1,0:T(8,128)(2,1)S(1)}, bf16[3,32,256]{2,1,0:T(8,128)(2,1)S(1)}, bf16[3,32,256]{2,1,0:T(8,128)(2,1)S(1)}) custom-call(f32[256,256]{1,0:T(8,128)S(1)} %get-tuple-element.100.ng_ref, f32[2,2,256,256]{3,2,1,0:T(8,128)S(1)} %get-tuple-element.101.halves_ref.keep_ref, ...), custom_call_target="tpu_custom_call" | custom-call | flops 6422528 | bytes 1000 | tf_op jit(solution)/shard_map/grad_taps/pallas_call | solution.py:93
  55.5 0.4 collective-permute-start.14
  56.0 0.2 collective-permute-start.20
  56.2 1.0 %collective-permute-done.14.got_ref = bf16[576,256]{1,0:T(8,128)(2,1)S(1)} collective-permute-done((bf16[576,256]{1,0:T(8,128)(2,1)S(1)}, bf16[576,256]{1,0:T(8,128)(2,1)S(1)}, u32[]{:S(2)}, u32[]{:S(2)}) %collective-permute-start.14) | collective-permute-done | bytes 294944 | tf_op jit(solution)/shard_map/ppermute | solution.py:701
  57.3 2.3 %collective-permute-start.15 = (bf16[3,32,256]{2,1,0:T(8,128)(2,1)S(1)}, bf16[3,32,256]{2,1,0:T(8,128)(2,1)S(1)}, u32[]{:S(2)}, u32[]{:S(2)}) collective-permute-start(bf16[3,32,256]{2,1,0:T(8,128)(2,1)S(1)} %get-tuple-element.108), channel_id=1, source_target_pairs={{0,4},{4,5},{5,1},{1,2},{2,6},{6,7},{7,3},{8,12},{12,13},{13,9},{9... | collective-permute-start | bytes 147464 | tf_op jit(solution)/shard_map/ppermute | solution.py:478
  59.5 3.6 %collective-permute-start.16 = (bf16[3,32,256]{2,1,0:T(8,128)(2,1)S(1)}, bf16[3,32,256]{2,1,0:T(8,128)(2,1)S(1)}, u32[]{:S(2)}, u32[]{:S(2)}) collective-permute-start(bf16[3,32,256]{2,1,0:T(8,128)(2,1)S(1)} %get-tuple-element.109), channel_id=1, source_target_pairs={{4,0},{5,4},{1,5},{2,1},{6,2},{7,6},{3,7},{12,8},{13,12},{9,13},{1... | collective-permute-start | bytes 147464 | tf_op jit(solution)/shard_map/ppermute | solution.py:478
  63.2 0.5 collective-permute-start.21
  63.7 3.1 %collective-permute-start.18 = (bf16[320,256]{1,0:T(8,128)(2,1)S(1)}, bf16[320,256]{1,0:T(8,128)(2,1)S(1)}, u32[]{:S(2)}, u32[]{:S(2)}) collective-permute-start(bf16[320,256]{1,0:T(8,128)(2,1)S(1)} %get-tuple-element.107.sent_ref), channel_id=1, source_target_pairs={{0,2},{1,3},{2,0},{3,1},{4,6},{5,7},{6,4},{7,5},{8,10},{9,11},{10,... | collective-permute-start | bytes 491528 | tf_op jit(solution)/shard_map/ppermute | solution.py:701
  66.8 0.9 %finish.1 = bf16[2,8,16,256]{3,2,1,0:T(8,128)(2,1)S(1)} custom-call(bf16[8,32,256]{2,1,0:T(8,128)(2,1)S(1)} %get-tuple-element.93.g_ref, f32[2,8,48,128]{3,2,1,0:T(8,128)S(1)} %get-tuple-element.103.cg_ref, f32[7,7,1,256]{3,2,1,0:T(1,128)S(1)} %get-tuple-element.71.refs_3_.refs_8_.refs_12_.taps_ref, bf16[3,32,256]{2,1,0:T(8,128)(2,1)S(1)} %collective-permute-done.15.refs_0_, ...), custom_call_target="tpu_custom_call" | custom-call | flops 6422528 | bytes 1000 | tf_op jit(solution)/shard_map/finish/pallas_call | solution.py:93
  67.7 0.5 collective-permute-start.17
  68.2 1.0 %collective-permute-done.21.refs_1_ = bf16[256,256]{1,0:T(8,128)(2,1)S(1)} collective-permute-done((bf16[256,256]{1,0:T(8,128)(2,1)S(1)}, bf16[256,256]{1,0:T(8,128)(2,1)S(1)}, u32[]{:S(2)}, u32[]{:S(2)}) %collective-permute-start.21) | collective-permute-done | bytes 131104 | tf_op jit(solution)/shard_map/ppermute | solution.py:701
  69.2 0.7 out_result.1
  70.0 1.0 %collective-permute-done.18.got_ref = bf16[320,256]{1,0:T(8,128)(2,1)S(1)} collective-permute-done((bf16[320,256]{1,0:T(8,128)(2,1)S(1)}, bf16[320,256]{1,0:T(8,128)(2,1)S(1)}, u32[]{:S(2)}, u32[]{:S(2)}) %collective-permute-start.18) | collective-permute-done | bytes 163872 | tf_op jit(solution)/shard_map/ppermute | solution.py:701
  71.0 0.9 %collective-permute-start.19 = (bf16[320,256]{1,0:T(8,128)(2,1)S(1)}, bf16[320,256]{1,0:T(8,128)(2,1)S(1)}, u32[]{:S(2)}, u32[]{:S(2)}) collective-permute-start(bf16[320,256]{1,0:T(8,128)(2,1)S(1)} %close.2.refs_0_), channel_id=1, source_target_pairs={{0,4},{4,0},{1,5},{5,1},{2,6},{6,2},{3,7},{7,3},{8,12},{12,8},{9,1... | collective-permute-start | bytes 491528 | tf_op jit(solution)/shard_map/ppermute | solution.py:701
  72.0 0.6 collective-permute-done.17
  72.6 4.4 %collective-permute-done.19.refs_1_ = bf16[320,256]{1,0:T(8,128)(2,1)S(1)} collective-permute-done((bf16[320,256]{1,0:T(8,128)(2,1)S(1)}, bf16[320,256]{1,0:T(8,128)(2,1)S(1)}, u32[]{:S(2)}, u32[]{:S(2)}) %collective-permute-start.19) | collective-permute-done | bytes 163872 | tf_op jit(solution)/shard_map/ppermute | solution.py:701
  77.1 0.7 in_result.1
  (42 shorter events, 1.0 us)
Async XLA Ops:
  0.6 0.9 %copy-start.2 = (bf16[1,1,16,16,256]{4,3,2,1,0:T(8,128)(2,1)S(1)}, bf16[1,1,16,16,256]{4,3,2,1,0:T(8,128)(2,1)}, u32[]{:S(2)}) copy-start(bf16[1,1,16,16,256]{4,3,2,1,0:T(8,128)(2,1)} %param.11) | copy-start | bytes 393220
  1.5 1.3 %copy-start.3 = (bf16[1,16,16,256]{3,2,1,0:T(8,128)(2,1)S(1)}, bf16[1,16,16,256]{3,2,1,0:T(8,128)(2,1)}, u32[]{:S(2)}) copy-start(bf16[1,16,16,256]{3,2,1,0:T(8,128)(2,1)} %param.12) | copy-start | bytes 393220
  1.6 5.3 %collective-permute-start.2 = (bf16[11,16,256]{2,1,0:T(8,128)(2,1)S(1)}, bf16[11,16,256]{2,1,0:T(8,128)(2,1)S(1)}, u32[]{:S(2)}, u32[]{:S(2)}) collective-permute-start(bf16[11,16,256]{2,1,0:T(8,128)(2,1)S(1)} %get-tuple-element.70), channel_id=1, source_target_pairs={{4,0},{0,4},{5,1},{1,5},{6,2},{2,6},{7,3},{3,7},{12,8},{8,12},{13,... | collective-permute-start | bytes 270344 | tf_op jit(solution)/shard_map/ppermute | solution.py:212
  2.9 1.7 %copy-start.4 = (f32[1,7,7,256]{3,0,2,1:T(1,128)S(1)}, f32[1,7,7,256]{3,0,2,1:T(1,128)}, u32[]{:S(2)}) copy-start(f32[1,7,7,256]{3,0,2,1:T(1,128)} %param.14) | copy-start | bytes 150532
  3.0 9.0 %collective-permute-start = (bf16[9,16,256]{2,1,0:T(8,128)(2,1)S(1)}, bf16[9,16,256]{2,1,0:T(8,128)(2,1)S(1)}, u32[]{:S(2)}, u32[]{:S(2)}) collective-permute-start(bf16[9,16,256]{2,1,0:T(8,128)(2,1)S(1)} %get-tuple-element.60), channel_id=1, source_target_pairs={{4,0},{0,4},{5,1},{1,5},{6,2},{2,6},{7,3},{3,7},{12,8},{8,12},{13,... | collective-permute-start | bytes 221192 | tf_op jit(solution)/shard_map/ppermute | solution.py:212
  4.5 7.6 %collective-permute-start.1 = (f32[7,7,1,256]{3,2,1,0:T(1,128)S(1)}, f32[7,7,1,256]{3,2,1,0:T(1,128)S(1)}, u32[]{:S(2)}, u32[]{:S(2)}) collective-permute-start(f32[7,7,1,256]{3,2,1,0:T(1,128)S(1)} %bitcast.19), channel_id=1, source_target_pairs={{8,0},{16,8},{24,16},{9,1},{17,9},{25,17},{10,2},{18,10},{26,18},{... | collective-permute-start | bytes 150536 | tf_op jit(solution)/shard_map/ppermute | solution.py:483
  7.0 2.1 %copy-start.5 = (f32[1,1024]{1,0:T(1,128)S(1)}, f32[1,1024]{1,0:T(1,128)}, u32[]{:S(2)}) copy-start(f32[1,1024]{1,0:T(1,128)} %refs_6_.1) | copy-start | bytes 12292
  7.0 2.1 %copy-start.7 = (f32[1,256]{1,0:T(1,128)S(1)}, f32[1,256]{1,0:T(1,128)}, u32[]{:S(2)}) copy-start(f32[1,256]{1,0:T(1,128)} %refs_4_.1) | copy-start | bytes 3076
  7.0 2.1 %copy-start.8 = (f32[1,256]{1,0:T(1,128)S(1)}, f32[1,256]{1,0:T(1,128)}, u32[]{:S(2)}) copy-start(f32[1,256]{1,0:T(1,128)} %refs_5_.1) | copy-start | bytes 3076
  7.0 2.1 %copy-start.9 = (f32[1,256]{1,0:T(1,128)S(1)}, f32[1,256]{1,0:T(1,128)}, u32[]{:S(2)}) copy-start(f32[1,256]{1,0:T(1,128)} %refs_7_.1) | copy-start | bytes 3076
  7.0 5.2 %collective-permute-start.3 = (bf16[3,32,256]{2,1,0:T(8,128)(2,1)S(1)}, bf16[3,32,256]{2,1,0:T(8,128)(2,1)S(1)}, u32[]{:S(2)}, u32[]{:S(2)}) collective-permute-start(bf16[3,32,256]{2,1,0:T(8,128)(2,1)S(1)} %pack_sides.1), channel_id=1, source_target_pairs={{5,4},{4,5},{2,1},{1,2},{7,6},{6,7},{13,12},{12,13},{10,9},{9,10},... | collective-permute-start | bytes 147464 | tf_op jit(solution)/shard_map/ppermute | solution.py:228
  9.1 0.7 copy-start.6
  9.7 1.0 %copy-start = (bf16[1,256,1024]{2,1,0:T(8,128)(2,1)S(1)}, bf16[1,256,1024]{2,1,0:T(8,128)(2,1)}, u32[]{:S(2)}) copy-start(bf16[1,256,1024]{2,1,0:T(8,128)(2,1)} %param.18) | copy-start | bytes 1572868
  10.8 1.0 %copy-start.1 = (bf16[1,1024,256]{2,1,0:T(8,128)(2,1)S(1)}, bf16[1,1024,256]{2,1,0:T(8,128)(2,1)}, u32[]{:S(2)}) copy-start(bf16[1,1024,256]{2,1,0:T(8,128)(2,1)} %param.20) | copy-start | bytes 1572868
  16.0 10.0 %collective-permute-start.4 = (bf16[8,32,256]{2,1,0:T(8,128)(2,1)S(1)}, bf16[8,32,256]{2,1,0:T(8,128)(2,1)S(1)}, u32[]{:S(2)}, u32[]{:S(2)}) collective-permute-start(bf16[8,32,256]{2,1,0:T(8,128)(2,1)S(1)} %get-tuple-element.79), channel_id=1, source_target_pairs={{8,0},{16,8},{24,16},{9,1},{17,9},{25,17},{10,2},{18,10},{26,18},{... | collective-permute-start | bytes 393224 | tf_op jit(solution)/shard_map/ppermute | solution.py:483
  18.3 7.2 %collective-permute-start.5 = (bf16[3,32,256]{2,1,0:T(8,128)(2,1)S(1)}, bf16[3,32,256]{2,1,0:T(8,128)(2,1)S(1)}, u32[]{:S(2)}, u32[]{:S(2)}) collective-permute-start(bf16[3,32,256]{2,1,0:T(8,128)(2,1)S(1)} %get-tuple-element.80), channel_id=1, source_target_pairs={{8,4},{12,5},{13,1},{9,2},{10,6},{14,7},{15,3},{16,12},{20,13},{21... | collective-permute-start | bytes 147464 | tf_op jit(solution)/shard_map/ppermute | solution.py:478
  20.4 5.5 %collective-permute-start.6 = (bf16[3,32,256]{2,1,0:T(8,128)(2,1)S(1)}, bf16[3,32,256]{2,1,0:T(8,128)(2,1)S(1)}, u32[]{:S(2)}, u32[]{:S(2)}) collective-permute-start(bf16[3,32,256]{2,1,0:T(8,128)(2,1)S(1)} %get-tuple-element.81), channel_id=1, source_target_pairs={{12,0},{13,4},{9,5},{10,1},{14,2},{15,6},{11,7},{20,8},{21,12},{17... | collective-permute-start | bytes 147464 | tf_op jit(solution)/shard_map/ppermute | solution.py:478
  27.8 10.7 %collective-permute-start.7 = (bf16[8,32,256]{2,1,0:T(8,128)(2,1)S(1)}, bf16[8,32,256]{2,1,0:T(8,128)(2,1)S(1)}, u32[]{:S(2)}, u32[]{:S(2)}) collective-permute-start(bf16[8,32,256]{2,1,0:T(8,128)(2,1)S(1)} %get-tuple-element.82), channel_id=1, source_target_pairs={{8,0},{16,8},{24,16},{9,1},{17,9},{25,17},{10,2},{18,10},{26,18},{... | collective-permute-start | bytes 393224 | tf_op jit(solution)/shard_map/ppermute | solution.py:483
  31.2 6.9 %collective-permute-start.8 = (bf16[3,32,256]{2,1,0:T(8,128)(2,1)S(1)}, bf16[3,32,256]{2,1,0:T(8,128)(2,1)S(1)}, u32[]{:S(2)}, u32[]{:S(2)}) collective-permute-start(bf16[3,32,256]{2,1,0:T(8,128)(2,1)S(1)} %get-tuple-element.83), channel_id=1, source_target_pairs={{8,4},{12,5},{13,1},{9,2},{10,6},{14,7},{15,3},{16,12},{20,13},{21... | collective-permute-start | bytes 147464 | tf_op jit(solution)/shard_map/ppermute | solution.py:478
  33.1 5.4 %collective-permute-start.9 = (bf16[3,32,256]{2,1,0:T(8,128)(2,1)S(1)}, bf16[3,32,256]{2,1,0:T(8,128)(2,1)S(1)}, u32[]{:S(2)}, u32[]{:S(2)}) collective-permute-start(bf16[3,32,256]{2,1,0:T(8,128)(2,1)S(1)} %get-tuple-element.84), channel_id=1, source_target_pairs={{12,0},{13,4},{9,5},{10,1},{14,2},{15,6},{11,7},{20,8},{21,12},{17... | collective-permute-start | bytes 147464 | tf_op jit(solution)/shard_map/ppermute | solution.py:478
  40.4 10.7 %collective-permute-start.10 = (bf16[8,32,256]{2,1,0:T(8,128)(2,1)S(1)}, bf16[8,32,256]{2,1,0:T(8,128)(2,1)S(1)}, u32[]{:S(2)}, u32[]{:S(2)}) collective-permute-start(bf16[8,32,256]{2,1,0:T(8,128)(2,1)S(1)} %get-tuple-element.85), channel_id=1, source_target_pairs={{8,0},{16,8},{24,16},{9,1},{17,9},{25,17},{10,2},{18,10},{26,18},{... | collective-permute-start | bytes 393224 | tf_op jit(solution)/shard_map/ppermute | solution.py:483
  43.3 7.4 %collective-permute-start.11 = (bf16[3,32,256]{2,1,0:T(8,128)(2,1)S(1)}, bf16[3,32,256]{2,1,0:T(8,128)(2,1)S(1)}, u32[]{:S(2)}, u32[]{:S(2)}) collective-permute-start(bf16[3,32,256]{2,1,0:T(8,128)(2,1)S(1)} %get-tuple-element.86), channel_id=1, source_target_pairs={{8,4},{12,5},{13,1},{9,2},{10,6},{14,7},{15,3},{16,12},{20,13},{21... | collective-permute-start | bytes 147464 | tf_op jit(solution)/shard_map/ppermute | solution.py:478
  45.2 5.9 %collective-permute-start.12 = (bf16[3,32,256]{2,1,0:T(8,128)(2,1)S(1)}, bf16[3,32,256]{2,1,0:T(8,128)(2,1)S(1)}, u32[]{:S(2)}, u32[]{:S(2)}) collective-permute-start(bf16[3,32,256]{2,1,0:T(8,128)(2,1)S(1)} %get-tuple-element.87), channel_id=1, source_target_pairs={{12,0},{13,4},{9,5},{10,1},{14,2},{15,6},{11,7},{20,8},{21,12},{17... | collective-permute-start | bytes 147464 | tf_op jit(solution)/shard_map/ppermute | solution.py:478
  51.9 2.5 %collective-permute-start.13 = (bf16[512,256]{1,0:T(8,128)(2,1)S(1)}, bf16[512,256]{1,0:T(8,128)(2,1)S(1)}, u32[]{:S(2)}, u32[]{:S(2)}) collective-permute-start(bf16[512,256]{1,0:T(8,128)(2,1)S(1)} %get-tuple-element.98.sent_ref), channel_id=1, source_target_pairs={{0,1},{1,0},{2,3},{3,2},{4,5},{5,4},{6,7},{7,6},{8,9},{9,8},{10,11... | collective-permute-start | bytes 786440 | tf_op jit(solution)/shard_map/ppermute | solution.py:701
  55.5 1.6 %collective-permute-start.14 = (bf16[576,256]{1,0:T(8,128)(2,1)S(1)}, bf16[576,256]{1,0:T(8,128)(2,1)S(1)}, u32[]{:S(2)}, u32[]{:S(2)}) collective-permute-start(bf16[576,256]{1,0:T(8,128)(2,1)S(1)} %get-tuple-element.106.sent_ref), channel_id=1, source_target_pairs={{0,1},{1,0},{2,3},{3,2},{4,5},{5,4},{6,7},{7,6},{8,9},{9,8},{10,11... | collective-permute-start | bytes 884744 | tf_op jit(solution)/shard_map/ppermute | solution.py:701
  56.0 7.2 %collective-permute-start.20 = (bf16[256,256]{1,0:T(8,128)(2,1)S(1)}, bf16[256,256]{1,0:T(8,128)(2,1)S(1)}, u32[]{:S(2)}, u32[]{:S(2)}) collective-permute-start(bf16[256,256]{1,0:T(8,128)(2,1)S(1)} %get-tuple-element.99.sent_ref), channel_id=1, source_target_pairs={{0,2},{1,3},{2,0},{3,1},{4,6},{5,7},{6,4},{7,5},{8,10},{9,11},{10,... | collective-permute-start | bytes 393224 | tf_op jit(solution)/shard_map/ppermute | solution.py:701
  57.3 9.5 %collective-permute-start.15 = (bf16[3,32,256]{2,1,0:T(8,128)(2,1)S(1)}, bf16[3,32,256]{2,1,0:T(8,128)(2,1)S(1)}, u32[]{:S(2)}, u32[]{:S(2)}) collective-permute-start(bf16[3,32,256]{2,1,0:T(8,128)(2,1)S(1)} %get-tuple-element.108), channel_id=1, source_target_pairs={{0,4},{4,5},{5,1},{1,2},{2,6},{6,7},{7,3},{8,12},{12,13},{13,9},{9... | collective-permute-start | bytes 147464 | tf_op jit(solution)/shard_map/ppermute | solution.py:478
  59.5 7.2 %collective-permute-start.16 = (bf16[3,32,256]{2,1,0:T(8,128)(2,1)S(1)}, bf16[3,32,256]{2,1,0:T(8,128)(2,1)S(1)}, u32[]{:S(2)}, u32[]{:S(2)}) collective-permute-start(bf16[3,32,256]{2,1,0:T(8,128)(2,1)S(1)} %get-tuple-element.109), channel_id=1, source_target_pairs={{4,0},{5,4},{1,5},{2,1},{6,2},{7,6},{3,7},{12,8},{13,12},{9,13},{1... | collective-permute-start | bytes 147464 | tf_op jit(solution)/shard_map/ppermute | solution.py:478
  63.2 6.0 %collective-permute-start.21 = (bf16[256,256]{1,0:T(8,128)(2,1)S(1)}, bf16[256,256]{1,0:T(8,128)(2,1)S(1)}, u32[]{:S(2)}, u32[]{:S(2)}) collective-permute-start(bf16[256,256]{1,0:T(8,128)(2,1)S(1)} %close.3.refs_0_), channel_id=1, source_target_pairs={{0,4},{4,0},{1,5},{5,1},{2,6},{6,2},{3,7},{7,3},{8,12},{12,8},{9,1... | collective-permute-start | bytes 393224 | tf_op jit(solution)/shard_map/ppermute | solution.py:701
  63.7 7.3 %collective-permute-start.18 = (bf16[320,256]{1,0:T(8,128)(2,1)S(1)}, bf16[320,256]{1,0:T(8,128)(2,1)S(1)}, u32[]{:S(2)}, u32[]{:S(2)}) collective-permute-start(bf16[320,256]{1,0:T(8,128)(2,1)S(1)} %get-tuple-element.107.sent_ref), channel_id=1, source_target_pairs={{0,2},{1,3},{2,0},{3,1},{4,6},{5,7},{6,4},{7,5},{8,10},{9,11},{10,... | collective-permute-start | bytes 491528 | tf_op jit(solution)/shard_map/ppermute | solution.py:701
  67.7 4.9 %collective-permute-start.17 = (bf16[1,8,16,256]{3,2,1,0:T(8,128)(2,1)S(1)}, bf16[1,8,16,256]{3,2,1,0:T(8,128)(2,1)S(1)}, u32[]{:S(2)}, u32[]{:S(2)}) collective-permute-start(bf16[1,8,16,256]{3,2,1,0:T(8,128)(2,1)S(1)} %get-tuple-element.114), channel_id=1, source_target_pairs={{0,4},{4,0},{1,5},{5,1},{2,6},{6,2},{3,7},{7,3},{8,12},{12,8},{9,1... | collective-permute-start | bytes 196616 | tf_op jit(solution)/shard_map/ppermute | solution.py:824
  71.0 6.0 %collective-permute-start.19 = (bf16[320,256]{1,0:T(8,128)(2,1)S(1)}, bf16[320,256]{1,0:T(8,128)(2,1)S(1)}, u32[]{:S(2)}, u32[]{:S(2)}) collective-permute-start(bf16[320,256]{1,0:T(8,128)(2,1)S(1)} %close.2.refs_0_), channel_id=1, source_target_pairs={{0,4},{4,0},{1,5},{5,1},{2,6},{6,2},{3,7},{7,3},{8,12},{12,8},{9,1... | collective-permute-start | bytes 491528 | tf_op jit(solution)/shard_map/ppermute | solution.py:701
  72.6 5.2 %copy-start.10 = (bf16[2,8,16,256]{3,1,0,2:T(8,128)(2,1)}, bf16[2,8,16,256]{3,1,0,2:T(8,128)(2,1)S(1)}, u32[]{:S(2)}) copy-start(bf16[2,8,16,256]{3,1,0,2:T(8,128)(2,1)S(1)} %copy_dynamic-update-slice_fusion) | copy-start | bytes 393220
